TPU v7x, 32 devices: a whole 2x2x4 slice. The times are simulated.
32 devices in a mesh: tile: 16 (over z, y, core), mem: 2 (over x).
Axes of the slice: x: 2, y: 2, z: 4, core: 2. Of those that a mesh axis runs over, the one named last changes fastest.
Arguments:
- control: bfloat16 [4, 16, 768, 1536], P('mem', None, 'tile'), may hold values from -6 to 6
- members: bfloat16 [4, 16, 768, 1536], P('mem', None, 'tile'), may hold values from -6 to 6
- gradient: bfloat16 [16, 768, 1536], P('tile'), may hold values from -6 to 6
- step_x: float32 [1536], replicated, may hold values from 0.1 to 0.4
- step_y: float32 [768], replicated, may hold values from 0.01 to 0.1
- step_z: float32 [16], replicated, may hold values from 0.1 to 1
Outputs:
- increment: bfloat16 [16, 768, 1536], P('tile')
- control_grad: bfloat16 [4, 16, 768, 1536], P('mem', None, 'tile')
All inputs are finite; a program needn't handle non-finite values.
Results may differ from a plain program's by a relative error of at most 0.0085.
Values may be sent and summed in bfloat16 or wider, within the bound.
No kernel may reach another device: no remote copies, remote signals or barrier semaphores. Data moves between devices by JAX's collectives and lax.ppermute only.
A program may use at most 128 MiB of HBM per device.

v0:
```python
import functools

import jax
import jax.numpy as jnp
from jax import lax
from jax.experimental import pallas as pl
from jax.experimental.pallas import tpu as pltpu
from jax.sharding import PartitionSpec as P

BAND = 8

along_gain = 0.35
horiz_gain = 0.15
vert_gain = 0.5

BF16 = jnp.bfloat16
F32 = jnp.float32
VMEM_LIMIT = 60 * 1024 * 1024
LANES = 128
SWAP = [(0, 1), (1, 0)]
CHUNKS = [3]


def params():
    return pltpu.CompilerParams(vmem_limit_bytes=VMEM_LIMIT)


def cost(flops, values):
    return pl.CostEstimate(flops=flops, bytes_accessed=2 * values, transcendentals=0)


def pick_block(size, *wanted):
    for block in wanted:
        if size % block == 0:
            return block
    return size


def dot(a, b):
    return jnp.dot(a, b, preferred_element_type=F32)


def prepare_x_kernel(block, step_ref, spread_ref, block_ref):
    columns = step_ref.shape[1]
    blocks = columns // block
    step = jnp.broadcast_to(step_ref[...], (block, columns))
    lane = lax.broadcasted_iota(jnp.int32, (block, columns), 1)
    row = lax.broadcasted_iota(jnp.int32, (block, columns), 0)
    edge = lax.broadcasted_iota(jnp.int32, (1, LANES), 1)
    firsts = jnp.where(edge < blocks, edge, edge - blocks) * block

    def to_row(col, first):
        eye = lax.broadcasted_iota(jnp.int32, (block, block), 0) == lax.broadcasted_iota(
            jnp.int32, (block, block), 1
        )
        return jnp.sum(jnp.where(eye, jnp.broadcast_to(col, (block, block)), 0.0), axis=0)[None]

    cols = []
    for b in range(blocks):
        cols.append(jnp.sum(jnp.where(lane <= row + b * block, step, 0.0), axis=1, keepdims=True))
    rows = [to_row(col, b * block) for b, col in enumerate(cols)]
    first = jnp.zeros((1, LANES), F32)
    last = jnp.zeros((1, LANES), F32)
    for b in range(blocks):
        first = jnp.where(edge == blocks + b, rows[b][:, :1], first)
        last = jnp.where(edge == b, rows[b][:, -1:], last)
    for b in range(blocks):
        near = dot_free_spread(cols[b], edge, blocks, b, first, last)
        spread_ref[b * block : (b + 1) * block, :] = near.astype(BF16)
        inside = along_gain * jnp.exp(-jnp.abs(cols[b] - rows[b]))
        block_ref[:block, b * block : (b + 1) * block] = inside.astype(BF16)
        which = lax.broadcasted_iota(jnp.int32, (LANES, block), 0)
        enter = jnp.zeros((LANES, block), F32)
        for a in range(blocks):
            if a < b:
                reach = rows[b] - rows[a][:, -1:]
                enter = jnp.where(which == a, jnp.exp(-reach), enter)
            if a > b:
                reach = rows[a][:, :1] - rows[b]
                enter = jnp.where(which == blocks + a, jnp.exp(-reach), enter)
        block_ref[block:, b * block : (b + 1) * block] = (along_gain * enter).astype(BF16)


def dot_free_spread(col, edge, blocks, b, first, last):
    to_last = jnp.exp(jnp.minimum(col - last, 0.0))
    to_first = jnp.exp(jnp.minimum(first - col, 0.0))
    return jnp.where(edge == b, to_last, 0.0) + jnp.where(edge == blocks + b, to_first, 0.0)


def prepare_x(step_x, block):
    columns = step_x.shape[0]
    return pl.pallas_call(
        functools.partial(prepare_x_kernel, block),
        out_shape=(
            jax.ShapeDtypeStruct((columns, LANES), BF16),
            jax.ShapeDtypeStruct((block + LANES, columns), BF16),
        ),
        compiler_params=params(),
        cost_estimate=cost(20 * columns * columns, 2 * columns * block),
        name="prepare_x",
    )(step_x[None])


def prepare_y_kernel(levels, tile_ref, step_y_ref, step_z_ref, mix_ref, halo_ref):
    size = mix_ref.shape[0]
    rows = size // levels
    base = tile_ref[0] * rows

    def split(shape, axis):
        index = lax.broadcasted_iota(jnp.int32, shape, axis)
        level = ((index.astype(F32) + 0.5) * (1.0 / rows)).astype(jnp.int32)
        return index, level, index - level * rows

    def coordinate(step_ref, upto):
        step = step_ref[...]
        shape = (upto.shape[0], step.shape[1])
        lane = lax.broadcasted_iota(jnp.int32, shape, 1)
        return jnp.sum(jnp.where(lane <= upto, jnp.broadcast_to(step, shape), 0.0), axis=1, keepdims=True)

    _, out_level, out_row = split((size, 1), 0)
    out_y = coordinate(step_y_ref, out_row + base)
    out_z = coordinate(step_z_ref, out_level)
    eye = lax.broadcasted_iota(jnp.int32, (size, size), 0) == lax.broadcasted_iota(
        jnp.int32, (size, size), 1
    )

    def to_row(col):
        return jnp.sum(jnp.where(eye, jnp.broadcast_to(col, (size, size)), 0.0), axis=0, keepdims=True)

    in_y = to_row(out_y)
    in_z = to_row(out_z)
    _, in_level, _ = split((1, size), 1)
    distance = jnp.abs(out_y - in_y) + jnp.abs(out_z - in_z)
    value = (horiz_gain * vert_gain) * jnp.exp(-distance)
    mix_ref[...] = jnp.where(jnp.abs(out_level - in_level) <= BAND, value, 0.0).astype(BF16)

    wide = 2 * levels
    column = lax.broadcasted_iota(jnp.int32, (1, wide), 1)
    halo_level = jnp.where(column < levels, column, column - levels)
    step_y = step_y_ref[...]
    lane = lax.broadcasted_iota(jnp.int32, step_y.shape, 1)
    below = jnp.sum(jnp.where(lane <= base - 1, step_y, 0.0), axis=1, keepdims=True)
    above = jnp.sum(jnp.where(lane <= base + rows, step_y, 0.0), axis=1, keepdims=True)
    step_z = step_z_ref[...]
    order = lax.broadcasted_iota(jnp.int32, (step_z.shape[1], wide), 0)
    turned = lax.broadcasted_iota(jnp.int32, (step_z.shape[1], step_z.shape[1]), 0)
    turned = turned == lax.broadcasted_iota(jnp.int32, turned.shape, 1)
    step_col = jnp.sum(jnp.where(turned, jnp.broadcast_to(step_z, turned.shape), 0.0), axis=1, keepdims=True)
    halo_z = jnp.sum(jnp.where(order <= halo_level, jnp.broadcast_to(step_col, order.shape), 0.0), axis=0, keepdims=True)
    reach = jnp.where(column < levels, out_y - below, above - out_y)
    value = (horiz_gain * vert_gain) * jnp.exp(-(jnp.abs(reach) + jnp.abs(out_z - halo_z)))
    halo_ref[...] = jnp.where(jnp.abs(out_level - halo_level) <= BAND, value, 0.0).astype(BF16)


def prepare_y(tile, step_y, step_z, levels, size):
    return pl.pallas_call(
        functools.partial(prepare_y_kernel, levels),
        grid_spec=pltpu.PrefetchScalarGridSpec(
            num_scalar_prefetch=1,
            grid=(1,),
            in_specs=[
                pl.BlockSpec((1, step_y.shape[0]), lambda i, t: (0, 0)),
                pl.BlockSpec((1, step_z.shape[0]), lambda i, t: (0, 0)),
            ],
            out_specs=[
                pl.BlockSpec((size, size), lambda i, t: (0, 0)),
                pl.BlockSpec((size, 2 * levels), lambda i, t: (0, 0)),
            ],
        ),
        out_shape=[
            jax.ShapeDtypeStruct((size, size), BF16),
            jax.ShapeDtypeStruct((size, 2 * levels), BF16),
        ],
        compiler_params=params(),
        cost_estimate=cost(20 * size * size, size * size),
        name="prepare_y",
    )(tile[None], step_y[None], step_z[None])


def edge_kernel(levels, rows, tile_ref, step_ref, field_ref, edge_ref, out_ref):
    @pl.when(jnp.logical_and(pl.program_id(0) == 0, pl.program_id(1) == 0))
    def _():
        base = tile_ref[0] * rows
        steps = step_ref.shape[1]
        size = edge_ref.shape[1]
        at = lax.broadcasted_iota(jnp.int32, (rows, steps), 1) - base
        row = lax.broadcasted_iota(jnp.int32, (rows, steps), 0)
        step = jnp.broadcast_to(step_ref[...], (rows, steps))
        own = jnp.sum(jnp.where(jnp.logical_and(at == row, row > 0), step, 0.0), axis=1, keepdims=True)
        column = lax.broadcasted_iota(jnp.int32, (1, size), 1)
        level = ((column.astype(F32) + 0.5) * (1.0 / rows)).astype(jnp.int32)
        row = lax.broadcasted_iota(jnp.int32, (rows, size), 0)
        reached = jnp.where(row <= column - level * rows, jnp.broadcast_to(own, (rows, size)), 0.0)
        from_first = jnp.sum(reached, axis=0, keepdims=True)
        to_last = jnp.sum(own, axis=0, keepdims=True) - from_first
        which = lax.broadcasted_iota(jnp.int32, (2 * levels, 1), 0)
        ending = which < levels
        reach = jnp.where(ending, to_last, from_first)
        own_level = jnp.where(ending, which, which - levels) == level
        edge_ref[...] = jnp.where(own_level, jnp.exp(-jnp.abs(reach)), 0.0).astype(BF16)

    out_ref[...] = dot(edge_ref[...], field_ref[...]).astype(BF16)


def edge_sums(tile, step_y, levels, field):
    count, size, columns = field.shape
    block = pick_block(columns, 768, 256, 128)
    return pl.pallas_call(
        functools.partial(edge_kernel, levels, size // levels),
        grid_spec=pltpu.PrefetchScalarGridSpec(
            num_scalar_prefetch=1,
            grid=(count, columns // block),
            in_specs=[
                pl.BlockSpec((1, step_y.shape[0]), lambda m, j, t: (0, 0)),
                pl.BlockSpec((None, size, block), lambda m, j, t: (m, 0, j)),
            ],
            out_specs=[
                pl.BlockSpec((2 * levels, size), lambda m, j, t: (0, 0)),
                pl.BlockSpec((None, 2 * levels, block), lambda m, j, t: (m, 0, j)),
            ],
        ),
        out_shape=[
            jax.ShapeDtypeStruct((2 * levels, size), BF16),
            jax.ShapeDtypeStruct((count, 2 * levels, columns), BF16),
        ],
        compiler_params=params(),
        cost_estimate=cost(4 * levels * field.size, field.size),
        name="edge_sums",
    )(tile[None], step_y[None], field)


def weigh_kernel(edge_ref, memb_ref, grad_ref, after_ref, out_ref):
    out_ref[...] = dot(edge_ref[...], memb_ref[...] * grad_ref[...]).astype(BF16)


def weighted_edge_sums(edge, memb, grad, after):
    count, rows, columns = memb.shape
    block = pick_block(columns, 768, 256, 128)
    pick = lambda j, m: (m, 0, j)
    return pl.pallas_call(
        weigh_kernel,
        grid=(columns // block, count),
        in_specs=[
            pl.BlockSpec(edge.shape, lambda j, m: (0, 0)),
            pl.BlockSpec((None, rows, block), pick),
            pl.BlockSpec((rows, block), lambda j, m: (0, j)),
            pl.BlockSpec(memory_space=pl.ANY),
        ],
        out_specs=pl.BlockSpec((None, edge.shape[0], block), pick),
        out_shape=jax.ShapeDtypeStruct((count, edge.shape[0], columns), BF16),
        compiler_params=params(),
        cost_estimate=cost(2 * edge.shape[0] * memb.size, 2 * memb.size),
        name="weighted_edge_sums",
    )(edge, memb, grad, after)


def filter_x_kernel(block, field_ref, *refs):
    *weight, spread_ref, block_ref, after_ref, out_ref = refs
    field = field_ref[...]
    if weight:
        field = field * weight[0][...]
    edges = dot(field, spread_ref[...]).astype(BF16)
    for start in range(0, field.shape[1], block):
        part = slice(start, start + block)
        both = jnp.concatenate([field[:, part], edges], axis=1)
        out_ref[:, part] = dot(both, block_ref[:, part]).astype(BF16)


def filter_x(field, weight, spread_x, block_x, after):
    count, rows, columns = field.shape
    height = pick_block(rows, 384, 256, 128)
    block = block_x.shape[0] - LANES
    pick = lambda i, m: (m, i, 0)
    weights = () if weight is None else (weight,)
    return pl.pallas_call(
        functools.partial(filter_x_kernel, block),
        grid=(rows // height, count),
        in_specs=[
            pl.BlockSpec((None, height, columns), pick),
            *[pl.BlockSpec((height, columns), lambda i, m: (i, 0)) for _ in weights],
            pl.BlockSpec(spread_x.shape, lambda i, m: (0, 0)),
            pl.BlockSpec(block_x.shape, lambda i, m: (0, 0)),
            pl.BlockSpec(memory_space=pl.ANY),
        ],
        out_specs=pl.BlockSpec((None, height, columns), pick),
        out_shape=jax.ShapeDtypeStruct(field.shape, BF16),
        compiler_params=params(),
        cost_estimate=cost(2 * field.size * (block + 2 * LANES), 2 * field.size),
        name="filter_x",
    )(field, *weights, spread_x, block_x, after)


def halo_along_x(at, halo, sums, block_ref, block):
    part = halo[:, pl.ds(pl.multiple_of(at * block, block), block)]
    return dot(jnp.concatenate([part, sums], axis=1), block_ref[...]).astype(BF16)


def increment_kernel(
    block, side_ref, mix_ref, mix_halo_ref, field_ref, memb_ref, halo_ref, spread_ref, block_ref,
    out_ref, sums_ref,
):
    count = field_ref.shape[0]
    step = pl.program_id(0)

    @pl.when(step == 0)
    def _():
        for m in range(count):
            sums_ref[m] = dot(halo_ref[m], spread_ref[...]).astype(BF16)

    at = side_ref[0] + step
    total = None
    for m in range(count):
        halo = halo_along_x(at, halo_ref.at[m], sums_ref[m], block_ref, block)
        shaped = dot(mix_ref[...], field_ref[m]) + dot(mix_halo_ref[...], halo)
        term = shaped * memb_ref[m].astype(F32)
        total = term if total is None else total + term
    out_ref[...] = total.astype(out_ref.dtype)


def partial_increment(first, blocks, kind, mix, mix_halo, field, memb, halo, spread_x, block_x):
    count, rows, columns = field.shape
    block = block_x.shape[0] - LANES
    pick = lambda j, side: (0, 0, side[0] + j)
    whole2 = lambda j, side: (0, 0)
    return pl.pallas_call(
        functools.partial(increment_kernel, block),
        grid_spec=pltpu.PrefetchScalarGridSpec(
            num_scalar_prefetch=1,
            grid=(blocks,),
            in_specs=[
                pl.BlockSpec(mix.shape, whole2),
                pl.BlockSpec(mix_halo.shape, whole2),
                pl.BlockSpec((count, rows, block), pick),
                pl.BlockSpec((count, rows, block), pick),
                pl.BlockSpec(halo.shape, lambda j, side: (0, 0, 0)),
                pl.BlockSpec(spread_x.shape, whole2),
                pl.BlockSpec((block_x.shape[0], block), lambda j, side: (0, side[0] + j)),
            ],
            out_specs=pl.BlockSpec((rows, block), lambda j, side: (0, j)),
            scratch_shapes=[pltpu.VMEM((count, halo.shape[1], LANES), BF16)],
        ),
        out_shape=jax.ShapeDtypeStruct((rows, blocks * block), kind),
        compiler_params=params(),
        cost_estimate=cost(
            2 * count * rows * (rows + halo.shape[1]) * blocks * block,
            2 * count * rows * blocks * block + rows * rows,
        ),
        name="partial_increment",
    )(first[None], mix, mix_halo, field, memb, halo, spread_x, block_x)


def adjoint_kernel(
    block, mix_ref, mix_halo_ref, field_ref, halo_ref, spread_ref, block_ref, out_ref, sums_ref
):
    step = pl.program_id(1)
    wide = field_ref.shape[1] // block

    @pl.when(step == 0)
    def _():
        sums_ref[...] = dot(halo_ref[...], spread_ref[...]).astype(BF16)

    for k in range(wide):
        part = slice(k * block, (k + 1) * block)
        halo = halo_along_x(
            step * wide + k, halo_ref, sums_ref[...], block_ref.at[:, part], block
        )
        total = dot(mix_ref[...], field_ref[:, part]) + dot(mix_halo_ref[...], halo)
        out_ref[:, part] = total.astype(BF16)


def adjoint_mix(mix, mix_halo, field, halo, spread_x, block_x):
    count, rows, columns = field.shape
    block = block_x.shape[0] - LANES
    wide = pick_block(columns, 3 * block, 2 * block, block)
    pick = lambda m, j: (m, 0, j)
    whole2 = lambda m, j: (0, 0)
    return pl.pallas_call(
        functools.partial(adjoint_kernel, block),
        grid=(count, columns // wide),
        in_specs=[
            pl.BlockSpec(mix.shape, whole2),
            pl.BlockSpec(mix_halo.shape, whole2),
            pl.BlockSpec((None, rows, wide), pick),
            pl.BlockSpec((None,) + halo.shape[1:], lambda m, j: (m, 0, 0)),
            pl.BlockSpec(spread_x.shape, whole2),
            pl.BlockSpec((block_x.shape[0], wide), lambda m, j: (0, j)),
        ],
        out_specs=pl.BlockSpec((None, rows, wide), pick),
        out_shape=jax.ShapeDtypeStruct(field.shape, BF16),
        scratch_shapes=[pltpu.VMEM(halo.shape[1:2] + (LANES,), BF16)],
        compiler_params=params(),
        cost_estimate=cost(
            2 * rows * (rows + halo.shape[1]) * count * columns, 2 * field.size + rows * rows
        ),
        name="adjoint_mix",
    )(mix, mix_halo, field, halo, spread_x, block_x)


def exchange_factors(tile, tiles, rows, step_y):
    pairs = tiles // 2
    mine = tile - lax.rem(tile, 2)
    lasts = jnp.arange(1, pairs + 1, dtype=jnp.int32) * (2 * rows) - 1
    firsts = jnp.arange(pairs, dtype=jnp.int32) * (2 * rows)
    middle = (mine + 1) * rows
    start = mine * rows
    end = (mine + 2) * rows
    frm = jnp.concatenate(
        [jnp.stack([middle - 1, start, start - 1, (tile + 1) * rows]), lasts, jnp.full((pairs,), end)]
    )
    to = jnp.concatenate(
        [jnp.stack([end - 1, middle, tile * rows - 1, end]), jnp.full((pairs,), start - 1), firsts]
    )
    index = jnp.arange(step_y.shape[0], dtype=jnp.int32)[None]
    between = jnp.logical_and(index > frm[:, None], index <= to[:, None])
    return jnp.exp(-jnp.sum(jnp.where(between, step_y[None], 0.0), axis=1))


def outside(sums, tile, tiles, levels, factor, meanwhile):
    count, _, columns = sums.shape
    sums = sums.reshape(count, 2, levels, columns)
    part = count // 2
    pairs = tiles // 2
    odd = lax.rem(tile, 2)
    pair = lax.div(tile, 2)

    def swap(x):
        return lax.ppermute(x, "tile", [(s, s ^ 1) for s in range(tiles)])

    def by_way(up, down):
        return jnp.stack([up, down]).reshape(1, 2, 1, 1)

    other = swap(sums)
    one = jnp.float32(1.0)
    keep = by_way(jnp.where(odd == 1, one, factor[0]), jnp.where(odd == 1, factor[1], one))
    take = by_way(jnp.where(odd == 1, factor[0], one), jnp.where(odd == 1, one, factor[1]))
    mine = lax.dynamic_slice_in_dim(sums, odd * part, part, 0)
    theirs = lax.dynamic_slice_in_dim(other, odd * part, part, 0)
    group = (keep * mine.astype(F32) + take * theirs.astype(F32)).astype(BF16)
    index = jnp.arange(pairs, dtype=jnp.int32).reshape(pairs, 1, 1, 1)
    sent = jnp.where(index > pair, group[None, :, 0], group[None, :, 1])
    came = lax.all_to_all(
        sent, "tile", 0, 0, tiled=True,
        axis_index_groups=[list(range(c, tiles, 2)) for c in range(2)],
    )
    result = meanwhile(other)
    came, result = lax.optimization_barrier((came, result))
    came = came.astype(F32)
    weight = factor[4:].reshape(2, pairs, 1, 1, 1)
    below = jnp.sum(jnp.where(index < pair, weight[0] * came, 0.0), axis=0)
    above = jnp.sum(jnp.where(index > pair, weight[1] * came, 0.0), axis=0)
    far = jnp.stack([below, above], axis=1).astype(BF16)
    there = swap(far)
    far = jnp.where(
        odd == 0,
        jnp.concatenate([far, there], axis=0),
        jnp.concatenate([there, far], axis=0),
    )
    way = by_way(factor[2], factor[3])
    near = by_way(jnp.where(odd == 1, 1.0, 0.0), jnp.where(odd == 1, 0.0, 1.0))
    halo = (far.astype(F32) * way + other.astype(F32) * near).astype(BF16)
    return halo.reshape(count, 2 * levels, columns), result


def body(tiles, control, members, gradient, step_x, step_y, step_z):
    count, levels, rows, columns = control.shape
    flat = (count, levels * rows, columns)
    tile = lax.axis_index("tile")
    side = lax.axis_index("mem")
    half = columns // 2
    block = pick_block(half, 256, 128)
    owned = gradient.shape[0]

    mix, mix_halo = prepare_y(tile, step_y, step_z, levels, levels * rows)
    factor = exchange_factors(tile, tiles, rows, step_y)
    field = control.reshape(flat)
    memb = members.reshape(flat)
    edge, control_sums = edge_sums(tile, step_y, levels, field)

    level_gradient = gradient.reshape(owned, tiles, rows, columns).swapaxes(0, 1)
    row_gradient = lax.all_to_all(
        level_gradient.reshape(levels, rows, columns), "tile", 0, 0, tiled=True
    )

    spread_x, block_x = prepare_x(step_x, block)
    halo, along = outside(
        control_sums, tile, tiles, levels, factor,
        lambda after: filter_x(field, None, spread_x, block_x, after),
    )
    blocks = half // block
    share = functools.partial(
        partial_increment,
        mix=mix, mix_halo=mix_halo, field=along, memb=memb, halo=halo, spread_x=spread_x,
        block_x=block_x,
    )
    starts = [sum(CHUNKS[:k]) for k in range(len(CHUNKS))] if sum(CHUNKS) == blocks else [0]
    sizes = CHUNKS if sum(CHUNKS) == blocks else [blocks]
    sent = [share((1 - side) * blocks + at, size, BF16) for at, size in zip(starts, sizes)]
    others = [lax.ppermute(part, "mem", SWAP) for part in sent]
    kept = [share(side * blocks + at, size, F32) for at, size in zip(starts, sizes)]
    mine, rest = [], []
    for own, other in zip(kept, others):
        part = (own + other.astype(F32)).astype(BF16)
        part = lax.all_to_all(part.reshape(levels, rows, -1), "tile", 0, 0, tiled=True)
        part = part.reshape(tiles, owned, rows, -1).swapaxes(0, 1)
        mine.append(part.reshape(owned, tiles * rows, -1))
        rest.append(lax.ppermute(mine[-1], "mem", SWAP))
    increment = jnp.where(
        side == 0,
        jnp.concatenate(mine + rest, axis=2),
        jnp.concatenate(rest + mine, axis=2),
    )

    grad = row_gradient.reshape(flat[1:])
    weighted_sums = weighted_edge_sums(edge, memb, grad, sent[-1])
    weighted_halo, adj_x = outside(
        weighted_sums, tile, tiles, levels, factor,
        lambda after: filter_x(memb, grad, spread_x, block_x, after),
    )
    control_grad = adjoint_mix(mix, mix_halo, adj_x, weighted_halo, spread_x, block_x)
    return increment, control_grad.reshape(control.shape)


def solution(mesh):
    placed = (
        P("mem", None, "tile", None),
        P("mem", None, "tile", None),
        P("tile", None, None),
        P(),
        P(),
        P(),
    )
    return jax.shard_map(
        functools.partial(body, mesh.shape["tile"]),
        mesh=mesh,
        in_specs=placed,
        out_specs=(P("tile", None, None), P("mem", None, "tile", None)),
        check_vma=False,
    )
```

profile of v0, /device:TPU:0, one launch (start us, length us, event | category | flops | bytes accessed | tf_op | source)
XLA Modules:
  0.0 162.1 jit_solution(10980567543346886918)
XLA Ops:
  0.6 1.3 broadcast_in_dim.113.step_y_ref.step_ref
  1.9 4.7 %edge_sums.1 = (bf16[32,768]{1,0:T(8,128)(2,1)}, bf16[2,32,1536]{2,1,0:T(8,128)(2,1)}) custom-call(s32[1]{0:T(128)} %bitcast.1.tile_ref, f32[1,768]{1,0:T(1,128)} %broadcast_in_dim.113.step_y_ref.step_ref, bf16[2,768,1536]{2,1,0:T(8,128)(2,1)} %bitcast.57), custom_call_target="tpu_custom_call" | custom-call | flops 150994944 | bytes 4718592 | tf_op jit(solution)/shard_map/edge_sums/pallas_call | solution.py:208
  6.6 0.5 collective-permute-start
  7.0 0.1 concatenate.60
  7.1 0.1 concatenate.61
  7.2 0.2 select_reduce_fusion
  7.4 0.6 fusion.10
  10.5 0.1 pad_maximum_fusion.2
  10.6 0.0 collective-permute-done.refs_2_
  10.6 1.1 add_convert_fusion.4
  11.7 0.1 broadcast_select_fusion.1
  11.8 19.4 %all_to_all.20 = bf16[8,1,16,1536]{3,2,1,0:T(8,128)(2,1)S(1)} all-to-all(bf16[8,1,16,1536]{3,2,1,0:T(8,128)(2,1)S(1)} %broadcast_select_fusion.1), channel_id=1, replica_groups={{0,4,8,12,16,20,24,28},{2,6,10,14,18,22,26,30},{1,5,9,13,17,21,25,29},{..., dimensions={0} | all-to-all | bytes 786432 | tf_op jit(solution)/shard_map/all_to_all | solution.py:441
  31.2 3.9 %all-to-all-start.2 = ((bf16[16,48,1536]{2,1,0:T(8,128)(2,1)}), bf16[16,48,1536]{2,1,0:T(8,128)(2,1)S(1)}, u32[]{:S(2)}, u32[]{:S(2)}) async-start(bf16[16,48,1536]{2,1,0:T(8,128)(2,1)} %bitcast.62), calls=%async_computation.2 | async-start | bytes 4718592 | tf_op jit(solution)/shard_map/all_to_all | solution.py:480
  35.1 0.1 stack.99
  35.1 0.6 broadcast_in_dim.124.step_ref
  35.7 4.2 %prepare_y.1 = (bf16[768,768]{1,0:T(8,128)(2,1)}, bf16[768,32]{1,0:T(8,128)(2,1)}) custom-call(s32[1]{0:T(128)} %bitcast.1.tile_ref, f32[1,768]{1,0:T(1,128)} %broadcast_in_dim.113.step_y_ref.step_ref, f32[1,16]{1,0:T(1,128)} %bitcast.78), custom_call_target="tpu_custom_call" | custom-call | flops 11796480 | bytes 1179648 | tf_op jit(solution)/shard_map/prepare_y/pallas_call | solution.py:156
  39.9 2.9 %prepare_x.1 = (bf16[1536,128]{1,0:T(8,128)(2,1)}, bf16[384,1536]{1,0:T(8,128)(2,1)}) custom-call(f32[1,1536]{1,0:T(1,128)} %broadcast_in_dim.124.step_ref), custom_call_target="tpu_custom_call" | custom-call | flops 47185920 | bytes 1572864 | tf_op jit(solution)/shard_map/prepare_x/pallas_call | solution.py:92
  42.8 0.1 fusion.9
  42.9 8.8 %filter_x.2.field_ref = bf16[2,768,1536]{2,1,0:T(8,128)(2,1)} custom-call(bf16[2,768,1536]{2,1,0:T(8,128)(2,1)} %bitcast.58, bf16[1536,128]{1,0:T(8,128)(2,1)} %get-tuple-element.15.refs_0_.spread_ref.refs_1_, bf16[384,1536]{1,0:T(8,128)(2,1)} %get-tuple-element.16.refs_1_.block_ref.refs_2_, bf16[2,2,16,1536]{3,2,1,0:T(8,128)(2,1)} %copy-done.1), custom_call_target="tpu_custom_call" | custom-call | flops 2415919104 | bytes 9437184 | tf_op jit(solution)/shard_map/filter_x/pallas_call | solution.py:275
  51.7 0.3 fusion.1
  52.0 0.3 collective-permute-start.1
  52.3 0.1 pad_maximum_fusion.4
  52.4 0.9 collective-permute-done.1
  53.3 0.8 add_convert_fusion.2
  54.1 7.2 %partial_increment.3.after_ref = bf16[768,768]{1,0:T(8,128)(2,1)} custom-call(s32[1]{0:T(128)} %bitcast.27.side_ref, bf16[768,768]{1,0:T(8,128)(2,1)} %get-tuple-element.12.mix_ref, bf16[768,32]{1,0:T(8,128)(2,1)} %get-tuple-element.13.mix_halo_ref, bf16[2,768,1536]{2,1,0:T(8,128)(2,1)} %filter_x.2.field_ref, bf16[2,768,1536]{2,1,0:T(8,128)(2,1)} %bitcast.51, ...), custom_call_target="tpu_custom_call" | custom-call | flops 1887436800 | bytes 5898240 | tf_op jit(solution)/shard_map/partial_increment/pallas_call | solution.py:325
  61.4 1.5 collective-permute-start.2
  62.8 7.4 %partial_increment.2 = f32[768,768]{1,0:T(8,128)} custom-call(s32[1]{0:T(128)} %bitcast.side_ref, bf16[768,768]{1,0:T(8,128)(2,1)} %get-tuple-element.12.mix_ref, bf16[768,32]{1,0:T(8,128)(2,1)} %get-tuple-element.13.mix_halo_ref, bf16[2,768,1536]{2,1,0:T(8,128)(2,1)} %filter_x.2.field_ref, bf16[2,768,1536]{2,1,0:T(8,128)(2,1)} %bitcast.52, ...), custom_call_target="tpu_custom_call" | custom-call | flops 1887436800 | bytes 5898240 | tf_op jit(solution)/shard_map/partial_increment/pallas_call | solution.py:325
  70.3 19.4 %collective-permute-done.2 = bf16[768,768]{1,0:T(8,128)(2,1)S(1)} collective-permute-done((bf16[768,768]{1,0:T(8,128)(2,1)}, bf16[768,768]{1,0:T(8,128)(2,1)S(1)}, u32[]{:S(2)}, u32[]{:S(2)}) %collective-permute-start.2) | collective-permute-done | bytes 1179680 | tf_op jit(solution)/shard_map/ppermute | solution.py:498
  89.7 2.9 %add_convert_fusion = bf16[768,768]{1,0:T(8,128)(2,1)} fusion(f32[768,768]{1,0:T(8,128)} %partial_increment.2, bf16[768,768]{1,0:T(8,128)(2,1)S(1)} %collective-permute-done.2), kind=kLoop, calls=%fused_computation.1 | loop fusion | flops 1769472 | bytes 4718592 | tf_op jit(solution)/shard_map/convert_element_type | solution.py:502
  92.6 0.0 all-to-all-done.2
  92.6 5.8 %all-to-all-start.1 = ((bf16[16,48,768]{2,1,0:T(8,128)(2,1)}), bf16[16,48,768]{2,1,0:T(8,128)(2,1)S(1)}, u32[]{:S(2)}, u32[]{:S(2)}) async-start(bf16[16,48,768]{2,1,0:T(8,128)(2,1)} %bitcast.61), calls=%async_computation.1 | async-start | bytes 2359296 | tf_op jit(solution)/shard_map/all_to_all | solution.py:503
  98.5 5.1 %weighted_edge_sums.1 = bf16[2,32,1536]{2,1,0:T(8,128)(2,1)} custom-call(bf16[32,768]{1,0:T(8,128)(2,1)} %get-tuple-element.19.edge_ref, bf16[2,768,1536]{2,1,0:T(8,128)(2,1)} %bitcast.53, bf16[768,1536]{1,0:T(8,128)(2,1)} %bitcast.55, bf16[768,768]{1,0:T(8,128)(2,1)} %partial_increment.3.after_ref), custom_call_target="tpu_custom_call" | custom-call | flops 150994944 | bytes 9437184 | tf_op jit(solution)/shard_map/weighted_edge_sums/pallas_call | solution.py:240
  103.6 0.4 collective-permute-start.4
  104.0 1.3 collective-permute-done.4.refs_3_
  105.3 1.1 add_convert_fusion.3
  106.4 0.8 broadcast_select_fusion
  107.2 16.4 %all-to-all-done.1 = bf16[16,48,768]{2,1,0:T(8,128)(2,1)S(1)} async-done(((bf16[16,48,768]{2,1,0:T(8,128)(2,1)}), bf16[16,48,768]{2,1,0:T(8,128)(2,1)S(1)}, u32[]{:S(2)}, u32[]{:S(2)}) %all-to-all-start.1) | async-done | bytes 1179680 | tf_op jit(solution)/shard_map/all_to_all | solution.py:503
  123.6 7.4 %all-to-all-start.3 = ((bf16[8,1,16,1536]{3,2,1,0:T(8,128)(2,1)}), bf16[8,1,16,1536]{3,2,1,0:T(8,128)(2,1)S(1)}, u32[]{:S(2)}, u32[]{:S(2)}) async-start(bf16[8,1,16,1536]{3,2,1,0:T(8,128)(2,1)} %broadcast_select_fusion), calls=%async_computation.3 | async-start | bytes 786432 | tf_op jit(solution)/shard_map/all_to_all | solution.py:441
  131.0 1.6 collective-permute-start.3
  132.6 9.4 %filter_x.3.field_ref = bf16[2,768,1536]{2,1,0:T(8,128)(2,1)} custom-call(bf16[2,768,1536]{2,1,0:T(8,128)(2,1)} %bitcast.54, bf16[768,1536]{1,0:T(8,128)(2,1)} %bitcast.56, bf16[1536,128]{1,0:T(8,128)(2,1)} %get-tuple-element.15.refs_0_.spread_ref.refs_1_, bf16[384,1536]{1,0:T(8,128)(2,1)} %get-tuple-element.16.refs_1_.block_ref.refs_2_, ...), custom_call_target="tpu_custom_call" | custom-call | flops 2415919104 | bytes 9437184 | tf_op jit(solution)/shard_map/filter_x/pallas_call | solution.py:275
  142.0 1.1 all-to-all-done.3
  143.1 0.3 fusion.5
  143.4 0.1 collective-permute-start.5
  143.5 1.3 collective-permute-done.5
  144.8 1.7 %add_convert_fusion.1 = bf16[2,2,16,1536]{3,2,1,0:T(8,128)(2,1)} fusion(bf16[2,2,16,1536]{3,2,1,0:T(8,128)(2,1)} %copy-done.3, bf16[1,2,16,1536]{3,2,1,0:T(8,128)(2,1)S(1)} %collective-permute-done.5, bf16[1,1,16,1536]{3,2,1,0:T(8,128)(2,1)S(1)} %bitcast.70, bf16[1,1,16,1536]{3,2,1,0:T(8,128)(2,1)S(1)} %bitcast.68, f32[2]{0:T(128)S(1)} %copy-done.11, ...), kind=kLoop, calls=%fused_computation.14 | loop fusion | flops 1081344 | bytes 589841 | tf_op jit(solution)/shard_map/convert_element_type | solution.py:460
  146.5 13.8 %adjoint_mix.1 = bf16[2,768,1536]{2,1,0:T(8,128)(2,1)} custom-call(bf16[768,768]{1,0:T(8,128)(2,1)} %get-tuple-element.12.mix_ref, bf16[768,32]{1,0:T(8,128)(2,1)} %get-tuple-element.13.mix_halo_ref, bf16[2,768,1536]{2,1,0:T(8,128)(2,1)} %filter_x.3.field_ref, bf16[2,32,1536]{2,1,0:T(8,128)(2,1)} %bitcast.75, ...), custom_call_target="tpu_custom_call" | custom-call | flops 3774873600 | bytes 10616832 | tf_op jit(solution)/shard_map/adjoint_mix/pallas_call | solution.py:377
  160.4 0.0 collective-permute-done.3
  160.4 1.7 %maximum_select_fusion = bf16[1,768,1536]{2,1,0:T(8,128)(2,1)} fusion(bf16[1,768,768]{2,1,0:T(8,128)(2,1)S(1)} %collective-permute-done.3, bf16[1,768,768]{2,1,0:T(8,128)(2,1)S(1)} %bitcast.60, pred[]{:T(512)S(6)} %eq.6), kind=kLoop, calls=%fused_computation | loop fusion | flops 10616832 | bytes 4718593 | tf_op jit(solution)/shard_map/jit(_where)/select_n | solution.py:507
  (39 shorter events, 0.1 us)
Async XLA Ops:
  1.9 5.3 %copy-start.4 = (f32[768]{0:T(1024)S(1)}, f32[768]{0:T(1024)}, u32[]{:S(2)}) copy-start(f32[768]{0:T(1024)} %param.10) | copy-start | bytes 9220
  6.6 4.1 %collective-permute-start = (bf16[2,2,16,1536]{3,2,1,0:T(8,128)(2,1)}, bf16[2,2,16,1536]{3,2,1,0:T(8,128)(2,1)S(1)}, u32[]{:S(2)}, u32[]{:S(2)}) collective-permute-start(bf16[2,2,16,1536]{3,2,1,0:T(8,128)(2,1)} %bitcast.76), channel_id=1, source_target_pairs={{0,2},{2,0},{4,6},{6,4},{8,10},{10,8},{12,14},{14,12},{16,18},{18,... | collective-permute-start | bytes 589832 | tf_op jit(solution)/shard_map/ppermute | solution.py:427
  10.6 20.6 %copy-start.1 = (bf16[2,2,16,1536]{3,2,1,0:T(8,128)(2,1)}, bf16[2,2,16,1536]{3,2,1,0:T(8,128)(2,1)S(1)}, u32[]{:S(2)}) copy-start(bf16[2,2,16,1536]{3,2,1,0:T(8,128)(2,1)S(1)} %collective-permute-done.refs_2_) | copy-start | bytes 589828
  31.2 4.0 %copy-start.5 = (f32[1536]{0:T(1024)S(1)}, f32[1536]{0:T(1024)}, u32[]{:S(2)}) copy-start(f32[1536]{0:T(1024)} %param.9) | copy-start | bytes 18436
  31.2 61.5 %all-to-all-start.2 = ((bf16[16,48,1536]{2,1,0:T(8,128)(2,1)}), bf16[16,48,1536]{2,1,0:T(8,128)(2,1)S(1)}, u32[]{:S(2)}, u32[]{:S(2)}) async-start(bf16[16,48,1536]{2,1,0:T(8,128)(2,1)} %bitcast.62), calls=%async_computation.2 | async-start | bytes 4718592 | tf_op jit(solution)/shard_map/all_to_all | solution.py:480
  35.1 18.2 %copy-start.8 = (f32[2]{0:T(128)}, f32[2]{0:T(128)S(1)}, u32[]{:S(2)}) copy-start(f32[2]{0:T(128)S(1)} %stack.99) | copy-start | bytes 28
  42.8 8.9 %copy-start.12 = (pred[8]{0:T(512)(128)(4,1)}, pred[8]{0:T(512)(128)(4,1)S(1)}, u32[]{:S(2)}) copy-start(pred[8]{0:T(512)(128)(4,1)S(1)} %iota_compare_fusion.2) | copy-start | bytes 28
  42.9 8.8 %copy-start.6 = (f32[8]{0:T(128)}, f32[8]{0:T(128)S(1)}, u32[]{:S(2)}) copy-start(f32[8]{0:T(128)S(1)} %get-tuple-element.31) | copy-start | bytes 100
  42.9 10.5 %copy-start.2 = (bf16[2,2,16,1536]{3,2,1,0:T(8,128)(2,1)S(1)}, bf16[2,2,16,1536]{3,2,1,0:T(8,128)(2,1)}, u32[]{:S(2)}) copy-start(bf16[2,2,16,1536]{3,2,1,0:T(8,128)(2,1)} %copy-done.1) | copy-start | bytes 589828
  52.0 1.4 collective-permute-start.1
  52.4 9.0 %copy-start.10 = (f32[2]{0:T(128)}, f32[2]{0:T(128)S(1)}, u32[]{:S(2)}) copy-start(f32[2]{0:T(128)S(1)} %pad_maximum_fusion.4) | copy-start | bytes 28
  61.4 28.4 %collective-permute-start.2 = (bf16[768,768]{1,0:T(8,128)(2,1)}, bf16[768,768]{1,0:T(8,128)(2,1)S(1)}, u32[]{:S(2)}, u32[]{:S(2)}) collective-permute-start(bf16[768,768]{1,0:T(8,128)(2,1)} %partial_increment.3.after_ref), channel_id=1, source_target_pairs={{0,1},{1,0},{2,3},{3,2},{4,5},{5,4},{6,7},{7,6},{8,9},{9,8},{10,11... | collective-permute-start | bytes 3538952 | tf_op jit(solution)/shard_map/ppermute | solution.py:498
  92.6 5.8 %copy-start = (bf16[16,48,1536]{2,1,0:T(8,128)(2,1)}, bf16[16,48,1536]{2,1,0:T(8,128)(2,1)S(1)}, u32[]{:S(2)}) copy-start(bf16[16,48,1536]{2,1,0:T(8,128)(2,1)S(1)} %all-to-all-done.2) | copy-start | bytes 7077892
  92.6 31.0 %all-to-all-start.1 = ((bf16[16,48,768]{2,1,0:T(8,128)(2,1)}), bf16[16,48,768]{2,1,0:T(8,128)(2,1)S(1)}, u32[]{:S(2)}, u32[]{:S(2)}) async-start(bf16[16,48,768]{2,1,0:T(8,128)(2,1)} %bitcast.61), calls=%async_computation.1 | async-start | bytes 2359296 | tf_op jit(solution)/shard_map/all_to_all | solution.py:503
  103.6 1.7 %collective-permute-start.4 = (bf16[2,2,16,1536]{3,2,1,0:T(8,128)(2,1)}, bf16[2,2,16,1536]{3,2,1,0:T(8,128)(2,1)S(1)}, u32[]{:S(2)}, u32[]{:S(2)}) collective-permute-start(bf16[2,2,16,1536]{3,2,1,0:T(8,128)(2,1)} %bitcast.65), channel_id=1, source_target_pairs={{0,2},{2,0},{4,6},{6,4},{8,10},{10,8},{12,14},{14,12},{16,18},{18,... | collective-permute-start | bytes 589832 | tf_op jit(solution)/shard_map/ppermute | solution.py:427
  105.3 27.3 %copy-start.3 = (bf16[2,2,16,1536]{3,2,1,0:T(8,128)(2,1)}, bf16[2,2,16,1536]{3,2,1,0:T(8,128)(2,1)S(1)}, u32[]{:S(2)}) copy-start(bf16[2,2,16,1536]{3,2,1,0:T(8,128)(2,1)S(1)} %collective-permute-done.4.refs_3_) | copy-start | bytes 589828
  123.6 19.5 %all-to-all-start.3 = ((bf16[8,1,16,1536]{3,2,1,0:T(8,128)(2,1)}), bf16[8,1,16,1536]{3,2,1,0:T(8,128)(2,1)S(1)}, u32[]{:S(2)}, u32[]{:S(2)}) async-start(bf16[8,1,16,1536]{3,2,1,0:T(8,128)(2,1)} %broadcast_select_fusion), calls=%async_computation.3 | async-start | bytes 786432 | tf_op jit(solution)/shard_map/all_to_all | solution.py:441
  131.0 12.1 %copy-start.7 = (f32[8]{0:T(128)S(1)}, f32[8]{0:T(128)}, u32[]{:S(2)}) copy-start(f32[8]{0:T(128)} %copy-done.6) | copy-start | bytes 100
  131.0 12.1 %copy-start.13 = (pred[8]{0:T(512)(128)(4,1)S(1)}, pred[8]{0:T(512)(128)(4,1)}, u32[]{:S(2)}) copy-start(pred[8]{0:T(512)(128)(4,1)} %copy-done.12) | copy-start | bytes 28
  131.0 13.8 %copy-start.9 = (f32[2]{0:T(128)S(1)}, f32[2]{0:T(128)}, u32[]{:S(2)}) copy-start(f32[2]{0:T(128)} %copy-done.8) | copy-start | bytes 28
  131.0 13.8 %copy-start.11 = (f32[2]{0:T(128)S(1)}, f32[2]{0:T(128)}, u32[]{:S(2)}) copy-start(f32[2]{0:T(128)} %copy-done.10) | copy-start | bytes 28
  131.0 29.3 %collective-permute-start.3 = (bf16[1,768,768]{2,1,0:T(8,128)(2,1)S(1)}, bf16[1,768,768]{2,1,0:T(8,128)(2,1)S(1)}, u32[]{:S(2)}, u32[]{:S(2)}) collective-permute-start(bf16[1,768,768]{2,1,0:T(8,128)(2,1)S(1)} %bitcast.59), channel_id=1, source_target_pairs={{0,1},{1,0},{2,3},{3,2},{4,5},{5,4},{6,7},{7,6},{8,9},{9,8},{10,11... | collective-permute-start | bytes 3538952 | tf_op jit(solution)/shard_map/ppermute | solution.py:506
  143.4 1.4 collective-permute-start.5
where the time goes:
time: 163 us; the launch traced here: 162 us
  Pallas kernels  63.5 us (39%)
  waiting for transfers between devices  40.5 us (25%)
  starting transfers between devices  21.4 us (13%)
  blocking collectives  19.4 us (12%)
  other arithmetic  11.1 us (7%)
  between operations  3.33 us (2%)
  local copies, waits for them, and re-layouts  2.86 us (2%)
    ppermute x1, waiting for transfers between devices, body(): others = [lax.ppermute(part, 'mem', SWAP) for part in sent]  19.4 us
    all_to_all x1, blocking collectives, outside(): lax.all_to_all(sent, 'tile', 0, 0, tiled=True, axis_index_groups=[list(ra...  19.4 us
    pallas_call x2, Pallas kernels, filter_x(): pl.pallas_call(functools.partial(filter_x_kernel, block), grid=(rows // h...  18.2 us
    all_to_all x1, waiting for transfers between devices, body(): lax.all_to_all(part.reshape(levels, rows, -1), 'tile', 0, 0, tiled=True)  16.4 us
    pallas_call x2, Pallas kernels, partial_increment(): pl.pallas_call(functools.partial(increment_kernel, block), grid_spec=pltp...  14.7 us
    pallas_call x1, Pallas kernels, adjoint_mix(): pl.pallas_call(functools.partial(adjoint_kernel, block), grid=(count, col...  13.8 us
    all_to_all x1, starting transfers between devices, outside(): lax.all_to_all(sent, 'tile', 0, 0, tiled=True, axis_index_groups=[list(ra...  7.38 us
    all_to_all x1, starting transfers between devices, body(): lax.all_to_all(part.reshape(levels, rows, -1), 'tile', 0, 0, tiled=True)  5.84 us
  transfers between devices with their start and end apart: 9, of which 6 were waited for; matrix products, arithmetic and copies ran while one was open for 6% of the time, Pallas kernels for 36%

commit v1 on v0

v1 whole, which is shorter than its diff:
```python
import functools

import jax
import jax.numpy as jnp
import numpy as np
from jax import lax
from jax.experimental import pallas as pl
from jax.experimental.pallas import tpu as pltpu
from jax.sharding import PartitionSpec as P

BAND = 8

along_gain = 0.35
horiz_gain = 0.15
vert_gain = 0.5

BF16 = jnp.bfloat16
F32 = jnp.float32
VMEM_LIMIT = 60 * 1024 * 1024
LANES = 128
SWAP = [(0, 1), (1, 0)]
CHUNKS = [2, 1]


def params():
    return pltpu.CompilerParams(vmem_limit_bytes=VMEM_LIMIT)


def cost(flops, values):
    return pl.CostEstimate(flops=flops, bytes_accessed=2 * values, transcendentals=0)


def pick_block(size, *wanted):
    for block in wanted:
        if size % block == 0:
            return block
    return size


def dot(a, b):
    return jnp.dot(a, b, preferred_element_type=F32)


def prepare_x_kernel(block, step_ref, spread_ref, block_ref):
    columns = step_ref.shape[1]
    blocks = columns // block
    step = jnp.broadcast_to(step_ref[...], (block, columns))
    lane = lax.broadcasted_iota(jnp.int32, (block, columns), 1)
    row = lax.broadcasted_iota(jnp.int32, (block, columns), 0)
    edge = lax.broadcasted_iota(jnp.int32, (1, LANES), 1)
    firsts = jnp.where(edge < blocks, edge, edge - blocks) * block

    def to_row(col, first):
        eye = lax.broadcasted_iota(jnp.int32, (block, block), 0) == lax.broadcasted_iota(
            jnp.int32, (block, block), 1
        )
        return jnp.sum(jnp.where(eye, jnp.broadcast_to(col, (block, block)), 0.0), axis=0)[None]

    cols = []
    for b in range(blocks):
        cols.append(jnp.sum(jnp.where(lane <= row + b * block, step, 0.0), axis=1, keepdims=True))
    rows = [to_row(col, b * block) for b, col in enumerate(cols)]
    first = jnp.zeros((1, LANES), F32)
    last = jnp.zeros((1, LANES), F32)
    for b in range(blocks):
        first = jnp.where(edge == blocks + b, rows[b][:, :1], first)
        last = jnp.where(edge == b, rows[b][:, -1:], last)
    for b in range(blocks):
        near = dot_free_spread(cols[b], edge, blocks, b, first, last)
        spread_ref[b * block : (b + 1) * block, :] = near.astype(BF16)
        inside = along_gain * jnp.exp(-jnp.abs(cols[b] - rows[b]))
        block_ref[:block, b * block : (b + 1) * block] = inside.astype(BF16)
        which = lax.broadcasted_iota(jnp.int32, (LANES, block), 0)
        enter = jnp.zeros((LANES, block), F32)
        for a in range(blocks):
            if a < b:
                reach = rows[b] - rows[a][:, -1:]
                enter = jnp.where(which == a, jnp.exp(-reach), enter)
            if a > b:
                reach = rows[a][:, :1] - rows[b]
                enter = jnp.where(which == blocks + a, jnp.exp(-reach), enter)
        block_ref[block:, b * block : (b + 1) * block] = (along_gain * enter).astype(BF16)


def dot_free_spread(col, edge, blocks, b, first, last):
    to_last = jnp.exp(jnp.minimum(col - last, 0.0))
    to_first = jnp.exp(jnp.minimum(first - col, 0.0))
    return jnp.where(edge == b, to_last, 0.0) + jnp.where(edge == blocks + b, to_first, 0.0)


def prepare_x(step_x, block):
    columns = step_x.shape[0]
    return pl.pallas_call(
        functools.partial(prepare_x_kernel, block),
        out_shape=(
            jax.ShapeDtypeStruct((columns, LANES), BF16),
            jax.ShapeDtypeStruct((block + LANES, columns), BF16),
        ),
        compiler_params=params(),
        cost_estimate=cost(20 * columns * columns, 2 * columns * block),
        name="prepare_x",
    )(step_x[None])


def prepare_y_kernel(levels, tile_ref, step_y_ref, step_z_ref, after_ref, mix_ref, halo_ref, token_ref):
    size = mix_ref.shape[0]
    rows = size // levels
    base = tile_ref[0] * rows

    def split(shape, axis):
        index = lax.broadcasted_iota(jnp.int32, shape, axis)
        level = ((index.astype(F32) + 0.5) * (1.0 / rows)).astype(jnp.int32)
        return index, level, index - level * rows

    def coordinate(step_ref, upto):
        step = step_ref[...]
        shape = (upto.shape[0], step.shape[1])
        lane = lax.broadcasted_iota(jnp.int32, shape, 1)
        return jnp.sum(jnp.where(lane <= upto, jnp.broadcast_to(step, shape), 0.0), axis=1, keepdims=True)

    _, out_level, out_row = split((size, 1), 0)
    out_y = coordinate(step_y_ref, out_row + base)
    out_z = coordinate(step_z_ref, out_level)
    eye = lax.broadcasted_iota(jnp.int32, (size, size), 0) == lax.broadcasted_iota(
        jnp.int32, (size, size), 1
    )

    def to_row(col):
        return jnp.sum(jnp.where(eye, jnp.broadcast_to(col, (size, size)), 0.0), axis=0, keepdims=True)

    in_y = to_row(out_y)
    in_z = to_row(out_z)
    _, in_level, _ = split((1, size), 1)
    distance = jnp.abs(out_y - in_y) + jnp.abs(out_z - in_z)
    value = (horiz_gain * vert_gain) * jnp.exp(-distance)
    mix_ref[...] = jnp.where(jnp.abs(out_level - in_level) <= BAND, value, 0.0).astype(BF16)

    wide = 2 * levels
    column = lax.broadcasted_iota(jnp.int32, (1, wide), 1)
    halo_level = jnp.where(column < levels, column, column - levels)
    step_y = step_y_ref[...]
    lane = lax.broadcasted_iota(jnp.int32, step_y.shape, 1)
    below = jnp.sum(jnp.where(lane <= base - 1, step_y, 0.0), axis=1, keepdims=True)
    above = jnp.sum(jnp.where(lane <= base + rows, step_y, 0.0), axis=1, keepdims=True)
    step_z = step_z_ref[...]
    order = lax.broadcasted_iota(jnp.int32, (step_z.shape[1], wide), 0)
    turned = lax.broadcasted_iota(jnp.int32, (step_z.shape[1], step_z.shape[1]), 0)
    turned = turned == lax.broadcasted_iota(jnp.int32, turned.shape, 1)
    step_col = jnp.sum(jnp.where(turned, jnp.broadcast_to(step_z, turned.shape), 0.0), axis=1, keepdims=True)
    halo_z = jnp.sum(jnp.where(order <= halo_level, jnp.broadcast_to(step_col, order.shape), 0.0), axis=0, keepdims=True)
    reach = jnp.where(column < levels, out_y - below, above - out_y)
    value = (horiz_gain * vert_gain) * jnp.exp(-(jnp.abs(reach) + jnp.abs(out_z - halo_z)))
    halo_ref[...] = jnp.where(jnp.abs(out_level - halo_level) <= BAND, value, 0.0).astype(BF16)
    token_ref[...] = jnp.zeros_like(token_ref)


def prepare_y(tile, step_y, step_z, levels, size, after):
    return pl.pallas_call(
        functools.partial(prepare_y_kernel, levels),
        grid_spec=pltpu.PrefetchScalarGridSpec(
            num_scalar_prefetch=1,
            grid=(1,),
            in_specs=[
                pl.BlockSpec((1, step_y.shape[0]), lambda i, t: (0, 0)),
                pl.BlockSpec((1, step_z.shape[0]), lambda i, t: (0, 0)),
                pl.BlockSpec(memory_space=pl.ANY),
            ],
            out_specs=[
                pl.BlockSpec((size, size), lambda i, t: (0, 0)),
                pl.BlockSpec((size, 2 * levels), lambda i, t: (0, 0)),
                pl.BlockSpec((1, 2), lambda i, t: (0, 0)),
            ],
        ),
        out_shape=[
            jax.ShapeDtypeStruct((size, size), BF16),
            jax.ShapeDtypeStruct((size, 2 * levels), BF16),
            jax.ShapeDtypeStruct((1, 2), F32),
        ],
        compiler_params=params(),
        cost_estimate=cost(20 * size * size, size * size),
        name="prepare_y",
    )(tile[None], step_y[None], step_z[None], after)


def edge_kernel(levels, rows, tile_ref, step_ref, field_ref, edge_ref, out_ref):
    @pl.when(jnp.logical_and(pl.program_id(0) == 0, pl.program_id(1) == 0))
    def _():
        base = tile_ref[0] * rows
        steps = step_ref.shape[1]
        size = edge_ref.shape[1]
        at = lax.broadcasted_iota(jnp.int32, (rows, steps), 1) - base
        row = lax.broadcasted_iota(jnp.int32, (rows, steps), 0)
        step = jnp.broadcast_to(step_ref[...], (rows, steps))
        own = jnp.sum(jnp.where(jnp.logical_and(at == row, row > 0), step, 0.0), axis=1, keepdims=True)
        column = lax.broadcasted_iota(jnp.int32, (1, size), 1)
        level = ((column.astype(F32) + 0.5) * (1.0 / rows)).astype(jnp.int32)
        row = lax.broadcasted_iota(jnp.int32, (rows, size), 0)
        reached = jnp.where(row <= column - level * rows, jnp.broadcast_to(own, (rows, size)), 0.0)
        from_first = jnp.sum(reached, axis=0, keepdims=True)
        to_last = jnp.sum(own, axis=0, keepdims=True) - from_first
        which = lax.broadcasted_iota(jnp.int32, (2 * levels, 1), 0)
        ending = which < levels
        reach = jnp.where(ending, to_last, from_first)
        own_level = jnp.where(ending, which, which - levels) == level
        edge_ref[...] = jnp.where(own_level, jnp.exp(-jnp.abs(reach)), 0.0).astype(BF16)

    out_ref[...] = dot(edge_ref[...], field_ref[...]).astype(BF16)


def edge_sums(tile, step_y, levels, field):
    count, size, columns = field.shape
    block = pick_block(columns, 768, 256, 128)
    return pl.pallas_call(
        functools.partial(edge_kernel, levels, size // levels),
        grid_spec=pltpu.PrefetchScalarGridSpec(
            num_scalar_prefetch=1,
            grid=(count, columns // block),
            in_specs=[
                pl.BlockSpec((1, step_y.shape[0]), lambda m, j, t: (0, 0)),
                pl.BlockSpec((None, size, block), lambda m, j, t: (m, 0, j)),
            ],
            out_specs=[
                pl.BlockSpec((2 * levels, size), lambda m, j, t: (0, 0)),
                pl.BlockSpec((None, 2 * levels, block), lambda m, j, t: (m, 0, j)),
            ],
        ),
        out_shape=[
            jax.ShapeDtypeStruct((2 * levels, size), BF16),
            jax.ShapeDtypeStruct((count, 2 * levels, columns), BF16),
        ],
        compiler_params=params(),
        cost_estimate=cost(4 * levels * field.size, field.size),
        name="edge_sums",
    )(tile[None], step_y[None], field)


def weigh_kernel(edge_ref, memb_ref, grad_ref, after_ref, out_ref):
    out_ref[...] = dot(edge_ref[...], memb_ref[...] * grad_ref[...]).astype(BF16)


def weighted_edge_sums(which, edge, memb, grad, after):
    count, rows, columns = memb.shape
    half = columns // 2
    block = pick_block(half, 384, 256, 128)
    steps = half // block
    return pl.pallas_call(
        weigh_kernel,
        grid=(steps, count),
        in_specs=[
            pl.BlockSpec(edge.shape, lambda j, m: (0, 0)),
            pl.BlockSpec((None, rows, block), lambda j, m: (m, 0, which * steps + j)),
            pl.BlockSpec((rows, block), lambda j, m: (0, j)),
            pl.BlockSpec(memory_space=pl.ANY),
        ],
        out_specs=pl.BlockSpec((None, edge.shape[0], block), lambda j, m: (m, 0, j)),
        out_shape=jax.ShapeDtypeStruct((count, edge.shape[0], half), BF16),
        compiler_params=params(),
        cost_estimate=cost(edge.shape[0] * memb.size, memb.size),
        name="weighted_edge_sums",
    )(edge, memb, grad, after)


def filter_x_kernel(block, count, field_ref, *refs):
    weights, (spread_ref, block_ref), (out_ref, token_ref) = refs[:count], refs[count : count + 2], refs[-2:]
    field = field_ref[...]
    if weights:
        field = field * jnp.concatenate([ref[...] for ref in weights], axis=1)
    edges = dot(field, spread_ref[...]).astype(BF16)
    for start in range(0, field.shape[1], block):
        part = slice(start, start + block)
        both = jnp.concatenate([field[:, part], edges], axis=1)
        out_ref[:, part] = dot(both, block_ref[:, part]).astype(BF16)
    token_ref[...] = jnp.zeros_like(token_ref)


def filter_x(members, field, weights, spread_x, block_x, after):
    count, rows, columns = field.shape
    height = pick_block(rows, 384, 256, 128)
    block = block_x.shape[0] - LANES
    whole = lambda i, m: (0, 0)
    return pl.pallas_call(
        functools.partial(filter_x_kernel, block, len(weights)),
        grid=(rows // height, len(members)),
        in_specs=[
            pl.BlockSpec((None, height, columns), lambda i, m: (members[0] + m, i, 0)),
            *[pl.BlockSpec((height, columns // 2), lambda i, m: (i, 0)) for _ in weights],
            pl.BlockSpec(spread_x.shape, whole),
            pl.BlockSpec(block_x.shape, whole),
            *[pl.BlockSpec(memory_space=pl.ANY) for _ in after],
        ],
        out_specs=[
            pl.BlockSpec((None, height, columns), lambda i, m: (m, i, 0)),
            pl.BlockSpec((1, 2), whole),
        ],
        out_shape=[
            jax.ShapeDtypeStruct((len(members), rows, columns), BF16),
            jax.ShapeDtypeStruct((1, 2), F32),
        ],
        compiler_params=params(),
        cost_estimate=cost(
            2 * len(members) * rows * columns * (block + 2 * LANES), 2 * len(members) * rows * columns
        ),
        name="filter_x",
    )(field, *weights, spread_x, block_x, *after)


def halo_along_x(at, halo, sums, block_ref, block):
    part = halo[:, pl.ds(pl.multiple_of(at * block, block), block)]
    return dot(jnp.concatenate([part, sums], axis=1), block_ref[...]).astype(BF16)


def increment_kernel(
    block, slow, fast, where_ref, mix_ref, mix_halo_ref, memb_ref, halo_ref, spread_ref, block_ref,
    *refs
):
    count, size, _ = memb_ref.shape
    fields, outs, (sums_ref, mix_here, halo_here) = refs[:count], refs[-3 - fast : -3], refs[-3:]
    height = size // (slow * fast)
    step = pl.program_id(0)

    def owner(d, z):
        at = z * fast + lax.rem(where_ref[1] + d, fast)
        return pl.ds(pl.multiple_of(at * height, height), height)

    def place(d, z):
        return slice((d * slow + z) * height, (d * slow + z + 1) * height)

    @pl.when(step == 0)
    def _():
        for m in range(count):
            sums_ref[m] = dot(halo_ref[m], spread_ref[...]).astype(BF16)
        for d in range(fast):
            for z in range(slow):
                mix_here[place(d, z), :] = mix_ref[owner(d, z), :]
                halo_here[place(d, z), :] = mix_halo_ref[owner(d, z), :]

    at = where_ref[0] + step
    shaped = []
    for m in range(count):
        halo = halo_along_x(at, halo_ref.at[m], sums_ref[m], block_ref, block)
        shaped.append(dot(mix_here[...], fields[m][...]) + dot(halo_here[...], halo))
    for d in range(fast):
        for z in range(slow):
            total = None
            for m in range(count):
                term = shaped[m][place(d, z)] * memb_ref[m, owner(d, z), :].astype(F32)
                total = term if total is None else total + term
            outs[d][z * height : (z + 1) * height, :] = total.astype(BF16)


def partial_increment(
    first, after, blocks, place, slow, fast, mix, mix_halo, fields, memb, halo, spread_x, block_x
):
    count, rows, columns = memb.shape
    block = block_x.shape[0] - LANES
    pick = lambda j, w: (0, 0, w[0] + j)
    whole2 = lambda j, w: (0, 0)
    return pl.pallas_call(
        functools.partial(increment_kernel, block, slow, fast),
        grid_spec=pltpu.PrefetchScalarGridSpec(
            num_scalar_prefetch=1,
            grid=(blocks,),
            in_specs=[
                pl.BlockSpec(mix.shape, whole2),
                pl.BlockSpec(mix_halo.shape, whole2),
                pl.BlockSpec((count, rows, block), pick),
                pl.BlockSpec(halo.shape, lambda j, w: (0, 0, 0)),
                pl.BlockSpec(spread_x.shape, whole2),
                pl.BlockSpec((block_x.shape[0], block), lambda j, w: (0, w[0] + j)),
                *[pl.BlockSpec((None, rows, block), pick) for _ in fields],
                *[pl.BlockSpec(memory_space=pl.ANY) for _ in after],
            ],
            out_specs=[pl.BlockSpec((rows // fast, block), lambda j, w: (0, j))] * fast,
            scratch_shapes=[
                pltpu.VMEM((count, halo.shape[1], LANES), BF16),
                pltpu.VMEM(mix.shape, BF16),
                pltpu.VMEM(mix_halo.shape, BF16),
            ],
        ),
        out_shape=[jax.ShapeDtypeStruct((rows // fast, blocks * block), BF16)] * fast,
        compiler_params=params(),
        cost_estimate=cost(
            2 * count * rows * (rows + halo.shape[1]) * blocks * block,
            2 * count * rows * blocks * block + rows * rows,
        ),
        name="partial_increment",
    )(jnp.stack([first, place]), mix, mix_halo, memb, halo, spread_x, block_x, *fields, *after)


def join_kernel(slow, fast, layer_ref, *refs):
    own, other, outs = refs[:fast], refs[fast : 2 * fast], refs[-slow:]
    height = own[0].shape[0] // slow
    for d in range(slow):
        z = lax.rem(layer_ref[0] + d, slow)
        rows = pl.ds(pl.multiple_of(z * height, height), height)
        for k in range(fast):
            total = own[k][rows, :].astype(F32) + other[k][rows, :].astype(F32)
            outs[d][k * height : (k + 1) * height, :] = total.astype(BF16)


def join(layer, slow, fast, own, other, after):
    rows, columns = own[0].shape
    block = pick_block(columns, 384, 256, 128)
    pick = lambda j, layer: (0, j)
    height = rows // slow
    return pl.pallas_call(
        functools.partial(join_kernel, slow, fast),
        grid_spec=pltpu.PrefetchScalarGridSpec(
            num_scalar_prefetch=1,
            grid=(columns // block,),
            in_specs=[pl.BlockSpec((rows, block), pick)] * (2 * fast)
            + [pl.BlockSpec(memory_space=pl.ANY)],
            out_specs=[pl.BlockSpec((fast * height, block), pick)] * slow,
        ),
        out_shape=[jax.ShapeDtypeStruct((fast * height, columns), BF16)] * slow,
        compiler_params=params(),
        cost_estimate=cost(fast * rows * columns, 3 * fast * rows * columns),
        name="join",
    )(layer[None], *own, *other, after)


def hold_kernel(*refs):
    del refs


def hold(array, *after):
    return pl.pallas_call(
        hold_kernel,
        in_specs=[pl.BlockSpec(memory_space=pl.ANY)] * (1 + len(after)),
        out_specs=pl.BlockSpec(memory_space=pl.ANY),
        out_shape=jax.ShapeDtypeStruct(array.shape, array.dtype),
        input_output_aliases={0: 0},
        name="hold",
    )(array, *after)


def adjoint_inside_kernel(mix_ref, memb_ref, grad_ref, after_ref, out_ref, token_ref):
    token_ref[...] = jnp.zeros_like(token_ref)
    out_ref[...] = dot(mix_ref[...], memb_ref[...] * grad_ref[...]).astype(BF16)


def adjoint_inside(which, mix, memb, grad, after):
    count, rows, columns = memb.shape
    half = columns // 2
    block = pick_block(half, 384, 256, 128)
    steps = half // block
    return pl.pallas_call(
        adjoint_inside_kernel,
        grid=(steps, count),
        in_specs=[
            pl.BlockSpec(mix.shape, lambda j, m: (0, 0)),
            pl.BlockSpec((None, rows, block), lambda j, m: (m, 0, which * steps + j)),
            pl.BlockSpec((rows, block), lambda j, m: (0, j)),
            pl.BlockSpec(memory_space=pl.ANY),
        ],
        out_specs=[
            pl.BlockSpec((None, rows, block), lambda j, m: (m, 0, j)),
            pl.BlockSpec((1, 2), lambda j, m: (0, 0)),
        ],
        out_shape=[
            jax.ShapeDtypeStruct((count, rows, half), BF16),
            jax.ShapeDtypeStruct((1, 2), F32),
        ],
        compiler_params=params(),
        cost_estimate=cost(rows * memb.size, memb.size + rows * rows),
        name="adjoint_inside",
    )(mix, memb, grad, after)


def adjoint_kernel(
    block, left_ref, right_ref, mix_halo_ref, halo_ref, spread_ref, block_ref, out_ref
):
    inside = jnp.concatenate([left_ref[...], right_ref[...]], axis=1)
    field = (dot(mix_halo_ref[...], halo_ref[...]) + inside.astype(F32)).astype(BF16)
    edges = dot(field, spread_ref[...]).astype(BF16)
    for start in range(0, field.shape[1], block):
        part = slice(start, start + block)
        both = jnp.concatenate([field[:, part], edges], axis=1)
        out_ref[:, part] = dot(both, block_ref[:, part]).astype(BF16)


def adjoint_outside(left, right, mix_halo, halo, spread_x, block_x):
    count, rows, half = left.shape
    height = pick_block(rows, 384, 256, 128)
    block = block_x.shape[0] - LANES
    pick = lambda m, i: (m, i, 0)
    whole = lambda m, i: (0, 0)
    return pl.pallas_call(
        functools.partial(adjoint_kernel, block),
        grid=(count, rows // height),
        in_specs=[
            pl.BlockSpec((None, height, half), pick),
            pl.BlockSpec((None, height, half), pick),
            pl.BlockSpec((height, mix_halo.shape[1]), lambda m, i: (i, 0)),
            pl.BlockSpec((None,) + halo.shape[1:], lambda m, i: (m, 0, 0)),
            pl.BlockSpec(spread_x.shape, whole),
            pl.BlockSpec(block_x.shape, whole),
        ],
        out_specs=pl.BlockSpec((None, height, 2 * half), pick),
        out_shape=jax.ShapeDtypeStruct((count, rows, 2 * half), BF16),
        compiler_params=params(),
        cost_estimate=cost(4 * left.size * (block + 2 * LANES), 4 * left.size),
        name="adjoint_outside",
    )(left, right, mix_halo, halo, spread_x, block_x)


def hop_factors(tile, tiles, rows, step_y):
    hops = np.array([1 << k for k in range(tiles.bit_length() - 1)], np.int32)
    pair = tile - lax.rem(tile, 2)
    group = tile - lax.rem(jnp.broadcast_to(tile, hops.shape), hops)
    upper = lax.rem(lax.div(group, hops), np.int32(2)) == 1
    first = jnp.where(upper, group - hops, group)
    middle = first + hops
    base = jnp.where(hops == 1, tile, pair)
    after = jnp.where(hops == 1, tile + 1, pair + 2)
    frm = [middle * rows - 1, first * rows, middle * rows - 1, after * rows]
    to = [(middle + hops) * rows - 1, middle * rows, base * rows - 1, middle * rows]
    frm = jnp.concatenate(frm + [jnp.stack([pair * rows - 1, (tile + 1) * rows])])
    to = jnp.concatenate(to + [jnp.stack([tile * rows - 1, (pair + 2) * rows])])
    index = jnp.arange(step_y.shape[0], dtype=jnp.int32)[None]
    between = jnp.logical_and(index > frm[:, None], index <= to[:, None])
    factor = jnp.exp(-jnp.sum(jnp.where(between, step_y[None], 0.0), axis=1))
    end, start, below, above = [factor[k * len(hops) : (k + 1) * len(hops)] for k in range(4)]
    upper = upper.astype(F32)
    lower = 1.0 - upper
    ways = [
        upper + lower * end, upper * start + lower,
        upper * end + lower, upper + lower * start,
        upper * below, lower * above,
    ]
    return jnp.stack(ways, axis=1).reshape(len(hops), 3, 2), factor[4 * len(hops) :]


def outside(sums, tile, tiles, levels, factors, meanwhile):
    count, _, columns = sums.shape
    sums = sums.reshape(count, 2, levels, columns)
    part = count // 2
    odd = lax.rem(tile, 2)
    factor, way = factors

    def pair(x, hop):
        return lax.ppermute(x, "tile", [(s, s ^ hop) for s in range(tiles)])

    def by_way(pair_of):
        return pair_of.reshape(1, 2, 1, 1)

    other = pair(sums, 1)
    mine = lax.dynamic_slice_in_dim(sums, odd * part, part, 0).astype(F32)
    theirs = lax.dynamic_slice_in_dim(other, odd * part, part, 0).astype(F32)
    group = (by_way(factor[0, 0]) * mine + by_way(factor[0, 1]) * theirs).astype(BF16)
    token = meanwhile(0, other)
    far = jnp.zeros(group.shape, F32)
    hop, at = 2, 1
    while hop < tiles:
        enter = factor[at, 2]
        if 2 * hop < tiles:
            theirs = pair(group, hop)
            came = theirs
            keep = factor[at, 0]
            if token is not None:
                keep = keep + token[0]
            group = by_way(keep) * group.astype(F32) + by_way(factor[at, 1]) * theirs.astype(F32)
            group = group.astype(BF16)
        else:
            upper = lax.rem(lax.div(tile, hop), 2) == 1
            theirs = pair(jnp.where(upper, group[:, 1], group[:, 0]), hop)
            came = theirs[:, None]
            if token is not None:
                enter = enter + token[0]
        far += by_way(enter) * came.astype(F32)
        token = meanwhile(at, theirs)
        hop *= 2
        at += 1
    far = far.astype(BF16)
    there = pair(far, 1)
    far = jnp.where(
        odd == 0,
        jnp.concatenate([far, there], axis=0),
        jnp.concatenate([there, far], axis=0),
    )
    halo = far.astype(F32) * by_way(way) + other.astype(F32) * by_way(factor[0, 2])
    return halo.astype(BF16).reshape(count, 2 * levels, columns), theirs


def body(tiles, control, members, gradient, step_x, step_y, step_z):
    count, levels, rows, columns = control.shape
    flat = (count, levels * rows, columns)
    tile = lax.axis_index("tile")
    side = lax.axis_index("mem")
    half = columns // 2
    block = pick_block(half, 256, 128)
    owned = gradient.shape[0]
    def in_order(own, other, axis):
        return jnp.where(
            side == 0,
            jnp.concatenate([own, other], axis=axis),
            jnp.concatenate([other, own], axis=axis),
        )

    def to_rows(part):
        part = part.reshape(owned, tiles, rows, -1).swapaxes(0, 1).reshape(levels, rows, -1)
        return lax.all_to_all(part, "tile", 0, 0, tiled=True).reshape(levels * rows, -1)

    def to_levels(part):
        part = lax.all_to_all(part.reshape(levels, rows, -1), "tile", 0, 0, tiled=True)
        part = part.reshape(tiles, owned, rows, -1).swapaxes(0, 1)
        return part.reshape(owned, tiles * rows, -1)

    left = to_rows(gradient[:, :, :half])

    factors = hop_factors(tile, tiles, rows, step_y)
    field = control.reshape(flat)
    memb = members.reshape(flat)
    edge, control_sums = edge_sums(tile, step_y, levels, field)
    spread_x, block_x = prepare_x(step_x, block)
    along, mixes = [], []

    def prepare(k, came):
        if k < count:
            result, token = filter_x([k], field, (), spread_x, block_x, (came,))
            along.append(result)
            return token
        if k == count:
            *result, token = prepare_y(tile, step_y, step_z, levels, levels * rows, came)
            mixes.extend(result)
            return token
        return None

    halo, last = outside(control_sums, tile, tiles, levels, factors, prepare)
    for k in range(len(along) + len(mixes) // 2, count + 1):
        prepare(k, last)
    mix, mix_halo = mixes

    right = to_rows(hold(gradient[:, :, half:], last, mix))

    blocks = half // block
    sizes = CHUNKS if sum(CHUNKS) == blocks else [blocks]
    starts = [sum(sizes[:k]) for k in range(len(sizes))]
    share = functools.partial(
        partial_increment,
        place=jnp.int32(0), slow=1, fast=1, mix=mix, mix_halo=mix_halo, fields=along, memb=memb,
        halo=halo, spread_x=spread_x, block_x=block_x,
    )
    sent, kept = [], []
    for at, size in zip(starts, sizes):
        sent += share((1 - side) * blocks + at, sent[-1:], blocks=size)
    others = [lax.ppermute(x, "mem", SWAP) for x in sent]
    left_sums = weighted_edge_sums(0, edge, memb, left, sent[-1])
    now, mine, rest = left_sums, [], []
    for k, (at, size) in enumerate(zip(starts, sizes)):
        (own,) = share(side * blocks + at, [now], blocks=size)
        now = own
        if k == 0:
            now = right_sums = weighted_edge_sums(1, edge, memb, right, now)
        if k == len(sizes) - 1:
            left_inside, _ = adjoint_inside(0, mix, memb, left, now)
            now = left_inside
        (now,) = join(jnp.int32(0), 1, 1, [own], [others[k]], now)
        mine.append(to_levels(now))
        rest.append(lax.ppermute(mine[-1], "mem", SWAP))
    increment = in_order(jnp.concatenate(mine, axis=2), jnp.concatenate(rest, axis=2), 2)

    hops = tiles.bit_length() - 1
    right_inside = []

    def work(k, came):
        if k != hops - 2:
            return None
        result, token = adjoint_inside(1, mix, memb, right, now)
        right_inside.append(result)
        return token

    weighted_sums = jnp.concatenate([left_sums, right_sums], axis=2)
    weighted_halo, _ = outside(weighted_sums, tile, tiles, levels, factors, work)
    control_grad = adjoint_outside(
        left_inside, right_inside[0], mix_halo, weighted_halo, spread_x, block_x
    )
    return increment, control_grad.reshape(control.shape)


def solution(mesh):
    placed = (
        P("mem", None, "tile", None),
        P("mem", None, "tile", None),
        P("tile", None, None),
        P(),
        P(),
        P(),
    )
    return jax.shard_map(
        functools.partial(body, mesh.shape["tile"]),
        mesh=mesh,
        in_specs=placed,
        out_specs=(P("tile", None, None), P("mem", None, "tile", None)),
        check_vma=False,
    )
```

time: 163 us -> 158 us (0.969)
  waiting for transfers between devices: 40.5 us -> 18.4 us
  blocking collectives: 19.4 us -> 0 us
  starting transfers between devices: 21.4 us -> 39.9 us
  Pallas kernels: 63.5 us -> 80.1 us
  local copies, waits for them, and re-layouts: 2.86 us -> 7.51 us
  between operations: 3.33 us -> 1.02 us
    ppermute x5 -> x12, waiting for transfers between devices: 22.9 us -> 2.2 us  [the longest x10 2.19 us: pair(): return lax.ppermute(x, 'tile', [(s, s ^ hop) for s in range(tiles)])]
    all_to_all x1 -> x0, blocking collectives: 19.4 us -> none  [outside(): lax.all_to_all(sent, 'tile', 0, 0, tiled=True, axis_index_groups=[list(ra...]
    pallas_call x6 -> x14, Pallas kernels: 51.8 us -> 68.2 us  [the longest x4 22.2 us: partial_increment(): pl.pallas_call(functools.partial(increment_kernel, block, slow, fast), gr...]
    ppermute x5 -> x12, starting transfers between devices: 2.76 us -> 17 us  [the longest x10 14.8 us: pair(): return lax.ppermute(x, 'tile', [(s, s ^ hop) for s in range(tiles)])]
    all_to_all x3 -> x4, waiting for transfers between devices: 17.5 us -> 11.3 us  [the longest x2 11.3 us: to_levels(): lax.all_to_all(part.reshape(levels, rows, -1), 'tile', 0, 0, tiled=True)]
    convert_element_type x5 -> x12, other arithmetic: 7.59 us -> 2.52 us  [the longest x2 1.63 us: outside(): return (halo.astype(BF16).reshape(count, 2 * levels, columns), theirs)]
    ppermute x1 -> x2, waiting for transfers between devices: 0.01 us -> 4.88 us  [body(): rest.append(lax.ppermute(mine[-1], 'mem', SWAP))]
    all_to_all x3 -> x4, starting transfers between devices: 17.1 us -> 21.8 us  [the longest x2 11.2 us: to_rows(): lax.all_to_all(part, 'tile', 0, 0, tiled=True).reshape(levels * rows, -1)]
  transfers between devices with their start and end apart: 9 -> 18, of which waited for: 6 -> 5; matrix products, arithmetic and copies ran while one was open for 6% -> 7% of each run, Pallas kernels for 36% -> 48%
where the time goes in v1:
time: 158 us; the launch traced here: 157 us
  Pallas kernels  80.1 us (51%)
  starting transfers between devices  39.9 us (25%)
  waiting for transfers between devices  18.4 us (12%)
  other arithmetic  10.2 us (6%)
  local copies, waits for them, and re-layouts  7.51 us (5%)
    pallas_call x4, Pallas kernels, partial_increment(): pl.pallas_call(functools.partial(increment_kernel, block, slow, fast), gr...  22.2 us
    ppermute x10, starting transfers between devices, pair(): return lax.ppermute(x, 'tile', [(s, s ^ hop) for s in range(tiles)])  14.8 us
    pallas_call x2, Pallas kernels, adjoint_inside(): pl.pallas_call(adjoint_inside_kernel, grid=(steps, count), in_specs=[pl.B...  12.7 us
    all_to_all x2, waiting for transfers between devices, to_levels(): lax.all_to_all(part.reshape(levels, rows, -1), 'tile', 0, 0, tiled=True)  11.3 us
    all_to_all x2, starting transfers between devices, to_rows(): lax.all_to_all(part, 'tile', 0, 0, tiled=True).reshape(levels * rows, -1)  11.2 us
    pallas_call x2, Pallas kernels, filter_x(): pl.pallas_call(functools.partial(filter_x_kernel, block, len(weights)), g...  11.1 us
    all_to_all x2, starting transfers between devices, to_levels(): lax.all_to_all(part.reshape(levels, rows, -1), 'tile', 0, 0, tiled=True)  10.6 us
    pallas_call x1, Pallas kernels, adjoint_outside(): pl.pallas_call(functools.partial(adjoint_kernel, block), grid=(count, row...  9.87 us
  transfers between devices with their start and end apart: 18, of which 5 were waited for; matrix products, arithmetic and copies ran while one was open for 7% of the time, Pallas kernels for 48%

profile of v1, /device:TPU:0, one launch (start us, length us, event | category | flops | bytes accessed | tf_op | source)
XLA Modules:
  0.0 157.2 jit_solution(13267572614539550041)
XLA Ops:
  0.6 1.3 broadcast_in_dim.46.step_ref.step_y_ref
  1.9 4.8 %edge_sums.1 = (bf16[32,768]{1,0:T(8,128)(2,1)}, bf16[2,32,1536]{2,1,0:T(8,128)(2,1)}) custom-call(s32[1]{0:T(128)} %bitcast.1.tile_ref, f32[1,768]{1,0:T(1,128)} %broadcast_in_dim.46.step_ref.step_y_ref, bf16[2,768,1536]{2,1,0:T(8,128)(2,1)} %bitcast.65), custom_call_target="tpu_custom_call" | custom-call | flops 150994944 | bytes 4718592 | tf_op jit(solution)/shard_map/edge_sums/pallas_call | solution.py:213
  7.2 1.6 %fusion.21 = (bf16[1,768,768]{2,1,0:T(8,128)(2,1)}, bf16[1,768,768]{2,1,0:T(8,128)(2,1)}) fusion(bf16[1,768,1536]{2,1,0:T(8,128)(2,1)S(1)} %copy-done.2), kind=kLoop, calls=%fused_computation.79 | loop fusion | bytes 4718592 | tf_op jit(solution)/shard_map/slice | solution.py:634
  8.8 7.2 %all-to-all-start = ((bf16[16,48,768]{2,1,0:T(8,128)(2,1)}), bf16[16,48,768]{2,1,0:T(8,128)(2,1)S(1)}, u32[]{:S(2)}, u32[]{:S(2)}) async-start(bf16[16,48,768]{2,1,0:T(8,128)(2,1)} %bitcast.22), calls=%async_computation | async-start | bytes 2359296 | tf_op jit(solution)/shard_map/all_to_all | solution.py:602
  17.5 2.9 %prepare_x.1 = (bf16[1536,128]{1,0:T(8,128)(2,1)}, bf16[384,1536]{1,0:T(8,128)(2,1)}) custom-call(f32[1,1536]{1,0:T(1,128)} %broadcast_in_dim.53.step_ref), custom_call_target="tpu_custom_call" | custom-call | flops 47185920 | bytes 1572864 | tf_op jit(solution)/shard_map/prepare_x/pallas_call | solution.py:93
  20.8 2.0 %collective-permute-start.1 = (bf16[1,2,16,1536]{3,2,1,0:T(8,128)(2,1)S(1)}, bf16[1,2,16,1536]{3,2,1,0:T(8,128)(2,1)S(1)}, u32[]{:S(2)}, u32[]{:S(2)}) collective-permute-start(bf16[1,2,16,1536]{3,2,1,0:T(8,128)(2,1)S(1)} %add_convert_fusion.3), channel_id=1, source_target_pairs={{0,4},{2,6},{4,0},{6,2},{8,12},{10,14},{12,8},{14,10},{16,20},{18,... | collective-permute-start | bytes 294920 | tf_op jit(solution)/shard_map/ppermute | solution.py:542
  22.8 5.5 %filter_x.2 = (bf16[1,768,1536]{2,1,0:T(8,128)(2,1)}, f32[1,2]{1,0:T(1,128)}) custom-call(bf16[2,768,1536]{2,1,0:T(8,128)(2,1)} %bitcast.66, bf16[1536,128]{1,0:T(8,128)(2,1)} %get-tuple-element.16.refs_0_.spread_ref, bf16[384,1536]{1,0:T(8,128)(2,1)} %get-tuple-element.17.refs_1_.block_ref, bf16[2,2,16,1536]{3,2,1,0:T(8,128)(2,1)} %copy-done.4), custom_call_target="tpu_custom_call" | custom-call | flops 1207959552 | bytes 4718592 | tf_op jit(solution)/shard_map/filter_x/pallas_call | solution.py:281
  28.3 0.7 bitcast_add_fusion.3
  29.1 1.5 collective-permute-start.2
  30.6 5.6 %filter_x.3 = (bf16[1,768,1536]{2,1,0:T(8,128)(2,1)}, f32[1,2]{1,0:T(1,128)}) custom-call(bf16[2,768,1536]{2,1,0:T(8,128)(2,1)} %bitcast.67, bf16[1536,128]{1,0:T(8,128)(2,1)} %get-tuple-element.16.refs_0_.spread_ref, bf16[384,1536]{1,0:T(8,128)(2,1)} %get-tuple-element.17.refs_1_.block_ref, bf16[1,2,16,1536]{3,2,1,0:T(8,128)(2,1)} %copy-done.9), custom_call_target="tpu_custom_call" | custom-call | flops 1207959552 | bytes 4718592 | tf_op jit(solution)/shard_map/filter_x/pallas_call | solution.py:281
  36.2 0.7 bitcast_add_fusion.1
  36.9 1.5 collective-permute-done.2.after_ref
  38.5 4.5 %collective-permute-start.3 = (bf16[1,16,1536]{2,1,0:T(8,128)(2,1)S(1)}, bf16[1,16,1536]{2,1,0:T(8,128)(2,1)S(1)}, u32[]{:S(2)}, u32[]{:S(2)}) collective-permute-start(bf16[1,16,1536]{2,1,0:T(8,128)(2,1)S(1)} %fusion.16), channel_id=1, source_target_pairs={{0,16},{2,18},{4,20},{6,22},{8,24},{10,26},{12,28},{14,30},{16,0},... | collective-permute-start | bytes 147464 | tf_op jit(solution)/shard_map/ppermute | solution.py:542
  43.0 4.2 %prepare_y.1 = (bf16[768,768]{1,0:T(8,128)(2,1)}, bf16[768,32]{1,0:T(8,128)(2,1)}, f32[1,2]{1,0:T(1,128)}) custom-call(s32[1]{0:T(128)} %bitcast.1.tile_ref, f32[1,768]{1,0:T(1,128)} %broadcast_in_dim.46.step_ref.step_y_ref, f32[1,16]{1,0:T(1,128)} %bitcast.88, bf16[1,2,16,1536]{3,2,1,0:T(8,128)(2,1)} %copy-done.7), custom_call_target="tpu_custom_call" | custom-call | flops 11796480 | bytes 1179648 | tf_op jit(solution)/shard_map/prepare_y/pallas_call | solution.py:158
  47.5 0.6 copy-done.13
  48.2 4.0 %all-to-all-start.1 = ((bf16[16,48,768]{2,1,0:T(8,128)(2,1)}), bf16[16,48,768]{2,1,0:T(8,128)(2,1)S(1)}, u32[]{:S(2)}, u32[]{:S(2)}) async-start(bf16[16,48,768]{2,1,0:T(8,128)(2,1)} %bitcast.70), calls=%async_computation.1 | async-start | bytes 2359296 | tf_op jit(solution)/shard_map/all_to_all | solution.py:602
  52.8 0.6 pad_add_fusion.1.where_ref
  53.8 0.8 add_convert_fusion.1
  54.6 6.3 %partial_increment.4.refs_2_ = bf16[768,512]{1,0:T(8,128)(2,1)} custom-call(s32[2]{0:T(128)} %pad_add_fusion.1.where_ref, bf16[768,768]{1,0:T(8,128)(2,1)} %get-tuple-element.20.mix_ref.refs_2_, bf16[768,32]{1,0:T(8,128)(2,1)} %get-tuple-element.21.mix_halo_ref, bf16[2,768,1536]{2,1,0:T(8,128)(2,1)} %bitcast.57, bf16[2,32,1536]{2,1,0:T(8,128)(2,1)} %bitcast.74, ...), custom_call_target="tpu_custom_call" | custom-call | flops 1258291200 | bytes 4325376 | tf_op jit(solution)/shard_map/partial_increment/pallas_call | solution.py:358
  60.9 1.6 collective-permute-start.5
  62.4 0.7 pad_add_fusion.3.where_ref
  63.1 0.6 pad_add_fusion.2.where_ref
  63.7 4.8 %partial_increment.5.after_ref = bf16[768,256]{1,0:T(8,128)(2,1)} custom-call(s32[2]{0:T(128)} %pad_add_fusion.2.where_ref, bf16[768,768]{1,0:T(8,128)(2,1)} %get-tuple-element.20.mix_ref.refs_2_, bf16[768,32]{1,0:T(8,128)(2,1)} %get-tuple-element.21.mix_halo_ref, bf16[2,768,1536]{2,1,0:T(8,128)(2,1)} %bitcast.58, bf16[2,32,1536]{2,1,0:T(8,128)(2,1)} %bitcast.75, ...), custom_call_target="tpu_custom_call" | custom-call | flops 629145600 | bytes 2752512 | tf_op jit(solution)/shard_map/partial_increment/pallas_call | solution.py:358
  68.5 4.0 %weighted_edge_sums.2.refs_2_ = bf16[2,32,768]{2,1,0:T(8,128)(2,1)} custom-call(bf16[32,768]{1,0:T(8,128)(2,1)} %get-tuple-element.26.edge_ref, bf16[2,768,1536]{2,1,0:T(8,128)(2,1)} %bitcast.59, bf16[768,768]{1,0:T(8,128)(2,1)} %bitcast.68, bf16[768,256]{1,0:T(8,128)(2,1)} %partial_increment.5.after_ref), custom_call_target="tpu_custom_call" | custom-call | flops 75497472 | bytes 4718592 | tf_op jit(solution)/shard_map/weighted_edge_sums/pallas_call | solution.py:246
  72.6 6.3 %partial_increment.6.after_ref.refs_0_ = bf16[768,512]{1,0:T(8,128)(2,1)} custom-call(s32[2]{0:T(128)} %pad_add_fusion.3.where_ref, bf16[768,768]{1,0:T(8,128)(2,1)} %get-tuple-element.20.mix_ref.refs_2_, bf16[768,32]{1,0:T(8,128)(2,1)} %get-tuple-element.21.mix_halo_ref, bf16[2,768,1536]{2,1,0:T(8,128)(2,1)} %bitcast.60, bf16[2,32,1536]{2,1,0:T(8,128)(2,1)} %bitcast.76, ...), custom_call_target="tpu_custom_call" | custom-call | flops 1258291200 | bytes 4325376 | tf_op jit(solution)/shard_map/partial_increment/pallas_call | solution.py:358
  78.9 1.0 copy-done.1
  79.9 4.1 %weighted_edge_sums.3.refs_2_ = bf16[2,32,768]{2,1,0:T(8,128)(2,1)} custom-call(bf16[32,768]{1,0:T(8,128)(2,1)} %get-tuple-element.26.edge_ref, bf16[2,768,1536]{2,1,0:T(8,128)(2,1)} %bitcast.61, bf16[768,768]{1,0:T(8,128)(2,1)} %bitcast.71, bf16[768,512]{1,0:T(8,128)(2,1)} %partial_increment.6.after_ref.refs_0_), custom_call_target="tpu_custom_call" | custom-call | flops 75497472 | bytes 4718592 | tf_op jit(solution)/shard_map/weighted_edge_sums/pallas_call | solution.py:246
  84.0 0.9 pad_maximum_fusion
  85.0 0.6 pad_add_fusion.where_ref
  85.6 0.6 collective-permute-start.6
  86.2 1.0 copy-done.11
  87.2 2.2 %join.2.refs_2_ = bf16[768,512]{1,0:T(8,128)(2,1)} custom-call(s32[1]{0:T(128)} %constant.40.clone.1.layer_ref, bf16[768,512]{1,0:T(8,128)(2,1)} %partial_increment.6.after_ref.refs_0_, bf16[768,512]{1,0:T(8,128)(2,1)} %copy-done.11, bf16[2,32,768]{2,1,0:T(8,128)(2,1)} %weighted_edge_sums.3.refs_2_), custom_call_target="tpu_custom_call" | custom-call | flops 393216 | bytes 2359296 | tf_op jit(solution)/shard_map/join/pallas_call | solution.py:406
  89.4 7.0 %all-to-all-start.2 = ((bf16[16,48,512]{2,1,0:T(8,128)(2,1)}), bf16[16,48,512]{2,1,0:T(8,128)(2,1)S(1)}, u32[]{:S(2)}, u32[]{:S(2)}) async-start(bf16[16,48,512]{2,1,0:T(8,128)(2,1)} %bitcast.73), calls=%async_computation.2 | async-start | bytes 1572864 | tf_op jit(solution)/shard_map/all_to_all | solution.py:605
  96.4 4.8 %partial_increment.7.after_ref.refs_0_ = bf16[768,256]{1,0:T(8,128)(2,1)} custom-call(s32[2]{0:T(128)} %pad_add_fusion.where_ref, bf16[768,768]{1,0:T(8,128)(2,1)} %get-tuple-element.20.mix_ref.refs_2_, bf16[768,32]{1,0:T(8,128)(2,1)} %get-tuple-element.21.mix_halo_ref, bf16[2,768,1536]{2,1,0:T(8,128)(2,1)} %bitcast.62, bf16[2,32,1536]{2,1,0:T(8,128)(2,1)} %bitcast.77, ...), custom_call_target="tpu_custom_call" | custom-call | flops 629145600 | bytes 2752512 | tf_op jit(solution)/shard_map/partial_increment/pallas_call | solution.py:358
  101.4 2.0 %collective-permute-start.10 = (bf16[1,2,16,1536]{3,2,1,0:T(8,128)(2,1)S(1)}, bf16[1,2,16,1536]{3,2,1,0:T(8,128)(2,1)S(1)}, u32[]{:S(2)}, u32[]{:S(2)}) collective-permute-start(bf16[1,2,16,1536]{3,2,1,0:T(8,128)(2,1)S(1)} %add_convert_fusion.2), channel_id=1, source_target_pairs={{0,4},{2,6},{4,0},{6,2},{8,12},{10,14},{12,8},{14,10},{16,20},{18,... | collective-permute-start | bytes 294920 | tf_op jit(solution)/shard_map/ppermute | solution.py:542
  103.4 6.3 %adjoint_inside.2 = (bf16[2,768,768]{2,1,0:T(8,128)(2,1)}, f32[1,2]{1,0:T(1,128)}) custom-call(bf16[768,768]{1,0:T(8,128)(2,1)} %get-tuple-element.20.mix_ref.refs_2_, bf16[2,768,1536]{2,1,0:T(8,128)(2,1)} %bitcast.63, bf16[768,768]{1,0:T(8,128)(2,1)} %bitcast.69, bf16[768,256]{1,0:T(8,128)(2,1)} %partial_increment.7.after_ref.refs_0_), custom_call_target="tpu_custom_call" | custom-call | flops 1811939328 | bytes 5898240 | tf_op jit(solution)/shard_map/adjoint_inside/pallas_call | solution.py:447
  109.7 0.7 copy-done.12
  110.4 2.0 %join.3.after_ref = bf16[768,256]{1,0:T(8,128)(2,1)} custom-call(s32[1]{0:T(128)} %constant.40.clone.1.layer_ref, bf16[768,256]{1,0:T(8,128)(2,1)} %partial_increment.7.after_ref.refs_0_, bf16[768,256]{1,0:T(8,128)(2,1)} %copy-done.12, bf16[2,768,768]{2,1,0:T(8,128)(2,1)} %get-tuple-element.27.refs_2_.left_ref), custom_call_target="tpu_custom_call" | custom-call | flops 196608 | bytes 1179648 | tf_op jit(solution)/shard_map/join/pallas_call | solution.py:406
  112.5 1.5 collective-permute-start.11
  114.0 6.4 %adjoint_inside.3 = (bf16[2,768,768]{2,1,0:T(8,128)(2,1)}, f32[1,2]{1,0:T(1,128)}) custom-call(bf16[768,768]{1,0:T(8,128)(2,1)} %get-tuple-element.20.mix_ref.refs_2_, bf16[2,768,1536]{2,1,0:T(8,128)(2,1)} %bitcast.64, bf16[768,768]{1,0:T(8,128)(2,1)} %bitcast.72, bf16[768,256]{1,0:T(8,128)(2,1)} %join.3.after_ref), custom_call_target="tpu_custom_call" | custom-call | flops 1811939328 | bytes 5898240 | tf_op jit(solution)/shard_map/adjoint_inside/pallas_call | solution.py:447
  120.6 2.4 %collective-permute-start.12 = (bf16[1,16,1536]{2,1,0:T(8,128)(2,1)S(1)}, bf16[1,16,1536]{2,1,0:T(8,128)(2,1)S(1)}, u32[]{:S(2)}, u32[]{:S(2)}) collective-permute-start(bf16[1,16,1536]{2,1,0:T(8,128)(2,1)S(1)} %fusion.15), channel_id=1, source_target_pairs={{0,16},{2,18},{4,20},{6,22},{8,24},{10,26},{12,28},{14,30},{16,0},... | collective-permute-start | bytes 147464 | tf_op jit(solution)/shard_map/ppermute | solution.py:542
  123.0 0.7 bitcast_add_fusion
  123.7 3.6 %all-to-all-start.3 = ((bf16[16,48,256]{2,1,0:T(8,128)(2,1)}), bf16[16,48,256]{2,1,0:T(8,128)(2,1)S(1)}, u32[]{:S(2)}, u32[]{:S(2)}) async-start(bf16[16,48,256]{2,1,0:T(8,128)(2,1)} %bitcast.31), calls=%async_computation.3 | async-start | bytes 786432 | tf_op jit(solution)/shard_map/all_to_all | solution.py:605
  128.1 11.3 %all-to-all-done.3 = bf16[16,48,256]{2,1,0:T(8,128)(2,1)S(1)} async-done(((bf16[16,48,256]{2,1,0:T(8,128)(2,1)}), bf16[16,48,256]{2,1,0:T(8,128)(2,1)S(1)}, u32[]{:S(2)}, u32[]{:S(2)}) %all-to-all-start.3) | async-done | bytes 393248 | tf_op jit(solution)/shard_map/all_to_all | solution.py:605
  139.9 0.8 add_convert_fusion
  140.8 9.9 %adjoint_outside.1 = bf16[2,768,1536]{2,1,0:T(8,128)(2,1)} custom-call(bf16[2,768,768]{2,1,0:T(8,128)(2,1)} %get-tuple-element.27.refs_2_.left_ref, bf16[2,768,768]{2,1,0:T(8,128)(2,1)} %get-tuple-element.28.right_ref, bf16[768,32]{1,0:T(8,128)(2,1)} %get-tuple-element.21.mix_halo_ref, bf16[2,32,1536]{2,1,0:T(8,128)(2,1)} %bitcast.83, ...), custom_call_target="tpu_custom_call" | custom-call | flops 2415919104 | bytes 9437184 | tf_op jit(solution)/shard_map/adjoint_outside/pallas_call | solution.py:488
  150.6 4.9 %collective-permute-done.8 = bf16[1,768,256]{2,1,0:T(8,128)(2,1)S(1)} collective-permute-done((bf16[1,768,256]{2,1,0:T(8,128)(2,1)S(1)}, bf16[1,768,256]{2,1,0:T(8,128)(2,1)S(1)}, u32[]{:S(2)}, u32[]{:S(2)}) %collective-permute-start.8) | collective-permute-done | bytes 393248 | tf_op jit(solution)/shard_map/ppermute | solution.py:660
  155.5 1.7 %maximum_select_fusion = bf16[1,768,1536]{2,1,0:T(8,128)(2,1)} fusion(bf16[1,768,256]{2,1,0:T(8,128)(2,1)S(1)} %collective-permute-done.8, bf16[1,768,512]{2,1,0:T(8,128)(2,1)S(1)} %collective-permute-done.7, bf16[1,768,256]{2,1,0:T(8,128)(2,1)S(1)} %bitcast.82, bf16[1,768,512]{2,1,0:T(8,128)(2,1)S(1)} %bitcast.80, pred[]{:T(512)S(6)} %eq.14), kind=kLoop, calls=%fused_computation | loop fusion | flops 20054016 | bytes 4718593 | tf_op jit(solution)/shard_map/jit(_where)/select_n | solution.py:594
  (89 shorter events, 5.5 us)
Async XLA Ops:
  1.9 5.3 %copy-start.2 = (bf16[1,768,1536]{2,1,0:T(8,128)(2,1)S(1)}, bf16[1,768,1536]{2,1,0:T(8,128)(2,1)}, u32[]{:S(2)}) copy-start(bf16[1,768,1536]{2,1,0:T(8,128)(2,1)} %param.11) | copy-start | bytes 7077892
  6.7 13.9 %collective-permute-start = (bf16[2,2,16,1536]{3,2,1,0:T(8,128)(2,1)}, bf16[2,2,16,1536]{3,2,1,0:T(8,128)(2,1)S(1)}, u32[]{:S(2)}, u32[]{:S(2)}) collective-permute-start(bf16[2,2,16,1536]{3,2,1,0:T(8,128)(2,1)} %bitcast.86), channel_id=1, source_target_pairs={{0,2},{2,0},{4,6},{6,4},{8,10},{10,8},{12,14},{14,12},{16,18},{18,... | collective-permute-start | bytes 589832 | tf_op jit(solution)/shard_map/ppermute | solution.py:542
  8.8 7.3 %copy-start.18 = (s32[4]{0:T(128)S(1)}, s32[4]{0:T(128)}, u32[]{:S(2)}) copy-start(s32[4]{0:T(128)} %constant.49.clone) | copy-start | bytes 52
  8.8 7.3 %copy-start.19 = (s32[4]{0:T(128)S(1)}, s32[4]{0:T(128)}, u32[]{:S(2)}) copy-start(s32[4]{0:T(128)} %constant.52) | copy-start | bytes 52
  8.8 7.3 %copy-start.20 = (pred[4]{0:T(512)(128)(4,1)S(1)}, pred[4]{0:T(512)(128)(4,1)}, u32[]{:S(2)}) copy-start(pred[4]{0:T(512)(128)(4,1)} %constant.50.clone) | copy-start | bytes 16
  8.8 7.5 %copy-start.21 = (s32[4]{0:T(128)S(1)}, s32[4]{0:T(128)}, u32[]{:S(2)}) copy-start(s32[4]{0:T(128)} %constant.53) | copy-start | bytes 52
  8.8 7.7 %copy-start.16 = (f32[768]{0:T(1024)S(1)}, f32[768]{0:T(1024)}, u32[]{:S(2)}) copy-start(f32[768]{0:T(1024)} %param.13) | copy-start | bytes 9220
  8.8 8.0 %copy-start.17 = (f32[1536]{0:T(1024)S(1)}, f32[1536]{0:T(1024)}, u32[]{:S(2)}) copy-start(f32[1536]{0:T(1024)} %param.12) | copy-start | bytes 18436
  8.8 11.9 %copy-start.15 = (bf16[2,32,1536]{2,1,0:T(8,128)(2,1)S(1)}, bf16[2,32,1536]{2,1,0:T(8,128)(2,1)}, u32[]{:S(2)}) copy-start(bf16[2,32,1536]{2,1,0:T(8,128)(2,1)} %get-tuple-element.18) | copy-start | bytes 589828
  8.8 39.4 %all-to-all-start = ((bf16[16,48,768]{2,1,0:T(8,128)(2,1)}), bf16[16,48,768]{2,1,0:T(8,128)(2,1)S(1)}, u32[]{:S(2)}, u32[]{:S(2)}) async-start(bf16[16,48,768]{2,1,0:T(8,128)(2,1)} %bitcast.22), calls=%async_computation | async-start | bytes 2359296 | tf_op jit(solution)/shard_map/all_to_all | solution.py:602
  20.7 2.1 %copy-start.4 = (bf16[2,2,16,1536]{3,2,1,0:T(8,128)(2,1)}, bf16[2,2,16,1536]{3,2,1,0:T(8,128)(2,1)S(1)}, u32[]{:S(2)}) copy-start(bf16[2,2,16,1536]{3,2,1,0:T(8,128)(2,1)S(1)} %collective-permute-done.refs_2_) | copy-start | bytes 589828
  20.8 8.2 %collective-permute-start.1 = (bf16[1,2,16,1536]{3,2,1,0:T(8,128)(2,1)S(1)}, bf16[1,2,16,1536]{3,2,1,0:T(8,128)(2,1)S(1)}, u32[]{:S(2)}, u32[]{:S(2)}) collective-permute-start(bf16[1,2,16,1536]{3,2,1,0:T(8,128)(2,1)S(1)} %add_convert_fusion.3), channel_id=1, source_target_pairs={{0,4},{2,6},{4,0},{6,2},{8,12},{10,14},{12,8},{14,10},{16,20},{18,... | collective-permute-start | bytes 294920 | tf_op jit(solution)/shard_map/ppermute | solution.py:542
  29.0 1.6 %copy-start.9 = (bf16[1,2,16,1536]{3,2,1,0:T(8,128)(2,1)}, bf16[1,2,16,1536]{3,2,1,0:T(8,128)(2,1)S(1)}, u32[]{:S(2)}) copy-start(bf16[1,2,16,1536]{3,2,1,0:T(8,128)(2,1)S(1)} %collective-permute-done.1.refs_2_) | copy-start | bytes 294916
  29.1 9.2 %collective-permute-start.2 = (bf16[1,2,16,1536]{3,2,1,0:T(8,128)(2,1)S(1)}, bf16[1,2,16,1536]{3,2,1,0:T(8,128)(2,1)S(1)}, u32[]{:S(2)}, u32[]{:S(2)}) collective-permute-start(bf16[1,2,16,1536]{3,2,1,0:T(8,128)(2,1)S(1)} %fusion.1), channel_id=1, source_target_pairs={{0,8},{2,10},{4,12},{6,14},{8,0},{10,2},{12,4},{14,6},{16,24},{18,... | collective-permute-start | bytes 294920 | tf_op jit(solution)/shard_map/ppermute | solution.py:542
  38.3 4.7 %copy-start.7 = (bf16[1,2,16,1536]{3,2,1,0:T(8,128)(2,1)}, bf16[1,2,16,1536]{3,2,1,0:T(8,128)(2,1)S(1)}, u32[]{:S(2)}) copy-start(bf16[1,2,16,1536]{3,2,1,0:T(8,128)(2,1)S(1)} %collective-permute-done.2.after_ref) | copy-start | bytes 294916
  38.5 9.1 %collective-permute-start.3 = (bf16[1,16,1536]{2,1,0:T(8,128)(2,1)S(1)}, bf16[1,16,1536]{2,1,0:T(8,128)(2,1)S(1)}, u32[]{:S(2)}, u32[]{:S(2)}) collective-permute-start(bf16[1,16,1536]{2,1,0:T(8,128)(2,1)S(1)} %fusion.16), channel_id=1, source_target_pairs={{0,16},{2,18},{4,20},{6,22},{8,24},{10,26},{12,28},{14,30},{16,0},... | collective-permute-start | bytes 147464 | tf_op jit(solution)/shard_map/ppermute | solution.py:542
  47.5 0.6 copy-start.13
  48.2 4.1 %copy-start.22 = (f32[1,2]{1,0:T(1,128)S(1)}, f32[1,2]{1,0:T(1,128)}, u32[]{:S(2)}) copy-start(f32[1,2]{1,0:T(1,128)} %get-tuple-element.22) | copy-start | bytes 28
  48.2 4.1 %copy-start.8 = (bf16[1,2,16,1536]{3,2,1,0:T(8,128)(2,1)S(1)}, bf16[1,2,16,1536]{3,2,1,0:T(8,128)(2,1)}, u32[]{:S(2)}) copy-start(bf16[1,2,16,1536]{3,2,1,0:T(8,128)(2,1)} %copy-done.7) | copy-start | bytes 294916
  48.2 4.2 %copy-start.10 = (bf16[1,2,16,1536]{3,2,1,0:T(8,128)(2,1)S(1)}, bf16[1,2,16,1536]{3,2,1,0:T(8,128)(2,1)}, u32[]{:S(2)}) copy-start(bf16[1,2,16,1536]{3,2,1,0:T(8,128)(2,1)} %copy-done.9) | copy-start | bytes 294916
  48.2 5.7 %copy-start.5 = (bf16[2,2,16,1536]{3,2,1,0:T(8,128)(2,1)S(1)}, bf16[2,2,16,1536]{3,2,1,0:T(8,128)(2,1)}, u32[]{:S(2)}) copy-start(bf16[2,2,16,1536]{3,2,1,0:T(8,128)(2,1)} %copy-done.4) | copy-start | bytes 589828
  48.2 4.1 %copy-start.14 = (bf16[1,16,1536]{2,1,0:T(8,128)(2,1)S(1)}, bf16[1,16,1536]{2,1,0:T(8,128)(2,1)}, u32[]{:S(2)}) copy-start(bf16[1,16,1536]{2,1,0:T(8,128)(2,1)} %copy-done.13) | copy-start | bytes 147460
  48.2 12.7 %copy-start = (bf16[16,48,768]{2,1,0:T(8,128)(2,1)}, bf16[16,48,768]{2,1,0:T(8,128)(2,1)S(1)}, u32[]{:S(2)}) copy-start(bf16[16,48,768]{2,1,0:T(8,128)(2,1)S(1)} %all-to-all-done) | copy-start | bytes 3538948
  48.2 30.6 %all-to-all-start.1 = ((bf16[16,48,768]{2,1,0:T(8,128)(2,1)}), bf16[16,48,768]{2,1,0:T(8,128)(2,1)S(1)}, u32[]{:S(2)}, u32[]{:S(2)}) async-start(bf16[16,48,768]{2,1,0:T(8,128)(2,1)} %bitcast.70), calls=%async_computation.1 | async-start | bytes 2359296 | tf_op jit(solution)/shard_map/all_to_all | solution.py:602
  52.5 1.4 collective-permute-start.4
  60.9 25.3 %collective-permute-start.5 = (bf16[768,512]{1,0:T(8,128)(2,1)}, bf16[768,512]{1,0:T(8,128)(2,1)S(1)}, u32[]{:S(2)}, u32[]{:S(2)}) collective-permute-start(bf16[768,512]{1,0:T(8,128)(2,1)} %partial_increment.4.refs_2_), channel_id=1, source_target_pairs={{0,1},{1,0},{2,3},{3,2},{4,5},{5,4},{6,7},{7,6},{8,9},{9,8},{10,11... | collective-permute-start | bytes 2359304 | tf_op jit(solution)/shard_map/ppermute | solution.py:647
  78.9 1.0 copy-start.1
  79.9 4.1 %copy-start.6 = (bf16[2,32,768]{2,1,0:T(8,128)(2,1)S(1)}, bf16[2,32,768]{2,1,0:T(8,128)(2,1)}, u32[]{:S(2)}) copy-start(bf16[2,32,768]{2,1,0:T(8,128)(2,1)} %weighted_edge_sums.2.refs_2_) | copy-start | bytes 294916
  79.9 5.7 %copy-start.3 = (bf16[768,256]{1,0:T(8,128)(2,1)S(1)}, bf16[768,256]{1,0:T(8,128)(2,1)}, u32[]{:S(2)}) copy-start(bf16[768,256]{1,0:T(8,128)(2,1)} %partial_increment.5.after_ref) | copy-start | bytes 1179652
  84.9 16.4 %collective-permute-start.9 = (bf16[2,2,16,1536]{3,2,1,0:T(8,128)(2,1)S(1)}, bf16[2,2,16,1536]{3,2,1,0:T(8,128)(2,1)S(1)}, u32[]{:S(2)}, u32[]{:S(2)}) collective-permute-start(bf16[2,2,16,1536]{3,2,1,0:T(8,128)(2,1)S(1)} %bitcast.84), channel_id=1, source_target_pairs={{0,2},{2,0},{4,6},{6,4},{8,10},{10,8},{12,14},{14,12},{16,18},{18,... | collective-permute-start | bytes 589832 | tf_op jit(solution)/shard_map/ppermute | solution.py:542
  85.6 24.1 %collective-permute-start.6 = (bf16[768,256]{1,0:T(8,128)(2,1)S(1)}, bf16[768,256]{1,0:T(8,128)(2,1)S(1)}, u32[]{:S(2)}, u32[]{:S(2)}) collective-permute-start(bf16[768,256]{1,0:T(8,128)(2,1)S(1)} %copy-done.3), channel_id=1, source_target_pairs={{0,1},{1,0},{2,3},{3,2},{4,5},{5,4},{6,7},{7,6},{8,9},{9,8},{10,11... | collective-permute-start | bytes 1179656 | tf_op jit(solution)/shard_map/ppermute | solution.py:647
  86.2 1.0 copy-start.11
  89.4 34.3 %all-to-all-start.2 = ((bf16[16,48,512]{2,1,0:T(8,128)(2,1)}), bf16[16,48,512]{2,1,0:T(8,128)(2,1)S(1)}, u32[]{:S(2)}, u32[]{:S(2)}) async-start(bf16[16,48,512]{2,1,0:T(8,128)(2,1)} %bitcast.73), calls=%async_computation.2 | async-start | bytes 1572864 | tf_op jit(solution)/shard_map/all_to_all | solution.py:605
  101.4 11.0 %collective-permute-start.10 = (bf16[1,2,16,1536]{3,2,1,0:T(8,128)(2,1)S(1)}, bf16[1,2,16,1536]{3,2,1,0:T(8,128)(2,1)S(1)}, u32[]{:S(2)}, u32[]{:S(2)}) collective-permute-start(bf16[1,2,16,1536]{3,2,1,0:T(8,128)(2,1)S(1)} %add_convert_fusion.2), channel_id=1, source_target_pairs={{0,4},{2,6},{4,0},{6,2},{8,12},{10,14},{12,8},{14,10},{16,20},{18,... | collective-permute-start | bytes 294920 | tf_op jit(solution)/shard_map/ppermute | solution.py:542
  109.7 0.7 copy-start.12
  112.5 8.0 %collective-permute-start.11 = (bf16[1,2,16,1536]{3,2,1,0:T(8,128)(2,1)S(1)}, bf16[1,2,16,1536]{3,2,1,0:T(8,128)(2,1)S(1)}, u32[]{:S(2)}, u32[]{:S(2)}) collective-permute-start(bf16[1,2,16,1536]{3,2,1,0:T(8,128)(2,1)S(1)} %fusion.11), channel_id=1, source_target_pairs={{0,8},{2,10},{4,12},{6,14},{8,0},{10,2},{12,4},{14,6},{16,24},{18,... | collective-permute-start | bytes 294920 | tf_op jit(solution)/shard_map/ppermute | solution.py:542
  120.6 6.7 %collective-permute-start.12 = (bf16[1,16,1536]{2,1,0:T(8,128)(2,1)S(1)}, bf16[1,16,1536]{2,1,0:T(8,128)(2,1)S(1)}, u32[]{:S(2)}, u32[]{:S(2)}) collective-permute-start(bf16[1,16,1536]{2,1,0:T(8,128)(2,1)S(1)} %fusion.15), channel_id=1, source_target_pairs={{0,16},{2,18},{4,20},{6,22},{8,24},{10,26},{12,28},{14,30},{16,0},... | collective-permute-start | bytes 147464 | tf_op jit(solution)/shard_map/ppermute | solution.py:542
  123.7 15.7 %all-to-all-start.3 = ((bf16[16,48,256]{2,1,0:T(8,128)(2,1)}), bf16[16,48,256]{2,1,0:T(8,128)(2,1)S(1)}, u32[]{:S(2)}, u32[]{:S(2)}) async-start(bf16[16,48,256]{2,1,0:T(8,128)(2,1)} %bitcast.31), calls=%async_computation.3 | async-start | bytes 786432 | tf_op jit(solution)/shard_map/all_to_all | solution.py:605
  127.3 28.2 %collective-permute-start.7 = (bf16[1,768,512]{2,1,0:T(8,128)(2,1)S(1)}, bf16[1,768,512]{2,1,0:T(8,128)(2,1)S(1)}, u32[]{:S(2)}, u32[]{:S(2)}) collective-permute-start(bf16[1,768,512]{2,1,0:T(8,128)(2,1)S(1)} %bitcast.79), channel_id=1, source_target_pairs={{0,1},{1,0},{2,3},{3,2},{4,5},{5,4},{6,7},{7,6},{8,9},{9,8},{10,11... | collective-permute-start | bytes 2359304 | tf_op jit(solution)/shard_map/ppermute | solution.py:660
  128.0 11.9 %collective-permute-start.13 = (bf16[1,2,16,1536]{3,2,1,0:T(8,128)(2,1)S(1)}, bf16[1,2,16,1536]{3,2,1,0:T(8,128)(2,1)S(1)}, u32[]{:S(2)}, u32[]{:S(2)}) collective-permute-start(bf16[1,2,16,1536]{3,2,1,0:T(8,128)(2,1)S(1)} %fusion.9), channel_id=1, source_target_pairs={{0,2},{2,0},{4,6},{6,4},{8,10},{10,8},{12,14},{14,12},{16,18},{18,... | collective-permute-start | bytes 294920 | tf_op jit(solution)/shard_map/ppermute | solution.py:542
  139.4 16.1 %collective-permute-start.8 = (bf16[1,768,256]{2,1,0:T(8,128)(2,1)S(1)}, bf16[1,768,256]{2,1,0:T(8,128)(2,1)S(1)}, u32[]{:S(2)}, u32[]{:S(2)}) collective-permute-start(bf16[1,768,256]{2,1,0:T(8,128)(2,1)S(1)} %bitcast.81), channel_id=1, source_target_pairs={{0,1},{1,0},{2,3},{3,2},{4,5},{5,4},{6,7},{7,6},{8,9},{9,8},{10,11... | collective-permute-start | bytes 1179656 | tf_op jit(solution)/shard_map/ppermute | solution.py:660

commit v2 on v1

--- a/solution.py
+++ b/solution.py
@@ -41,7 +41,7 @@
     return jnp.dot(a, b, preferred_element_type=F32)
 
 
-def prepare_x_kernel(block, step_ref, spread_ref, block_ref):
+def prepare_x_kernel(block, step_ref, after_ref, spread_ref, block_ref):
     columns = step_ref.shape[1]
     blocks = columns // block
     step = jnp.broadcast_to(step_ref[...], (block, columns))
@@ -88,10 +88,11 @@
     return jnp.where(edge == b, to_last, 0.0) + jnp.where(edge == blocks + b, to_first, 0.0)
 
 
-def prepare_x(step_x, block):
+def prepare_x(step_x, block, after):
     columns = step_x.shape[0]
     return pl.pallas_call(
         functools.partial(prepare_x_kernel, block),
+        in_specs=[pl.BlockSpec(memory_space=pltpu.VMEM), pl.BlockSpec(memory_space=pl.ANY)],
         out_shape=(
             jax.ShapeDtypeStruct((columns, LANES), BF16),
             jax.ShapeDtypeStruct((block + LANES, columns), BF16),
@@ -99,7 +100,7 @@
         compiler_params=params(),
         cost_estimate=cost(20 * columns * columns, 2 * columns * block),
         name="prepare_x",
-    )(step_x[None])
+    )(step_x[None], after)
 
 
 def prepare_y_kernel(levels, tile_ref, step_y_ref, step_z_ref, after_ref, mix_ref, halo_ref, token_ref):
@@ -310,53 +311,33 @@
 
 
 def increment_kernel(
-    block, slow, fast, where_ref, mix_ref, mix_halo_ref, memb_ref, halo_ref, spread_ref, block_ref,
-    *refs
+    block, first_ref, mix_ref, mix_halo_ref, memb_ref, halo_ref, spread_ref, block_ref, *refs
 ):
-    count, size, _ = memb_ref.shape
-    fields, outs, (sums_ref, mix_here, halo_here) = refs[:count], refs[-3 - fast : -3], refs[-3:]
-    height = size // (slow * fast)
+    count = memb_ref.shape[0]
+    fields, out_ref, sums_ref = refs[:count], refs[-2], refs[-1]
     step = pl.program_id(0)
-
-    def owner(d, z):
-        at = z * fast + lax.rem(where_ref[1] + d, fast)
-        return pl.ds(pl.multiple_of(at * height, height), height)
-
-    def place(d, z):
-        return slice((d * slow + z) * height, (d * slow + z + 1) * height)
 
     @pl.when(step == 0)
     def _():
         for m in range(count):
             sums_ref[m] = dot(halo_ref[m], spread_ref[...]).astype(BF16)
-        for d in range(fast):
-            for z in range(slow):
-                mix_here[place(d, z), :] = mix_ref[owner(d, z), :]
-                halo_here[place(d, z), :] = mix_halo_ref[owner(d, z), :]
-
-    at = where_ref[0] + step
-    shaped = []
+
+    total = None
     for m in range(count):
-        halo = halo_along_x(at, halo_ref.at[m], sums_ref[m], block_ref, block)
-        shaped.append(dot(mix_here[...], fields[m][...]) + dot(halo_here[...], halo))
-    for d in range(fast):
-        for z in range(slow):
-            total = None
-            for m in range(count):
-                term = shaped[m][place(d, z)] * memb_ref[m, owner(d, z), :].astype(F32)
-                total = term if total is None else total + term
-            outs[d][z * height : (z + 1) * height, :] = total.astype(BF16)
-
-
-def partial_increment(
-    first, after, blocks, place, slow, fast, mix, mix_halo, fields, memb, halo, spread_x, block_x
-):
+        halo = halo_along_x(first_ref[0] + step, halo_ref.at[m], sums_ref[m], block_ref, block)
+        shaped = dot(mix_ref[...], fields[m][...]) + dot(mix_halo_ref[...], halo)
+        term = shaped * memb_ref[m].astype(F32)
+        total = term if total is None else total + term
+    out_ref[...] = total.astype(BF16)
+
+
+def partial_increment(first, after, blocks, mix, mix_halo, fields, memb, halo, spread_x, block_x):
     count, rows, columns = memb.shape
     block = block_x.shape[0] - LANES
-    pick = lambda j, w: (0, 0, w[0] + j)
-    whole2 = lambda j, w: (0, 0)
-    return pl.pallas_call(
-        functools.partial(increment_kernel, block, slow, fast),
+    pick = lambda j, first: (0, 0, first[0] + j)
+    whole2 = lambda j, first: (0, 0)
+    return pl.pallas_call(
+        functools.partial(increment_kernel, block),
         grid_spec=pltpu.PrefetchScalarGridSpec(
             num_scalar_prefetch=1,
             grid=(blocks,),
@@ -364,59 +345,56 @@
                 pl.BlockSpec(mix.shape, whole2),
                 pl.BlockSpec(mix_halo.shape, whole2),
                 pl.BlockSpec((count, rows, block), pick),
-                pl.BlockSpec(halo.shape, lambda j, w: (0, 0, 0)),
+                pl.BlockSpec(halo.shape, lambda j, first: (0, 0, 0)),
                 pl.BlockSpec(spread_x.shape, whole2),
-                pl.BlockSpec((block_x.shape[0], block), lambda j, w: (0, w[0] + j)),
+                pl.BlockSpec((block_x.shape[0], block), lambda j, first: (0, first[0] + j)),
                 *[pl.BlockSpec((None, rows, block), pick) for _ in fields],
-                *[pl.BlockSpec(memory_space=pl.ANY) for _ in after],
+                pl.BlockSpec(memory_space=pl.ANY),
             ],
-            out_specs=[pl.BlockSpec((rows // fast, block), lambda j, w: (0, j))] * fast,
-            scratch_shapes=[
-                pltpu.VMEM((count, halo.shape[1], LANES), BF16),
-                pltpu.VMEM(mix.shape, BF16),
-                pltpu.VMEM(mix_halo.shape, BF16),
-            ],
+            out_specs=pl.BlockSpec((rows, block), lambda j, first: (0, j)),
+            scratch_shapes=[pltpu.VMEM((count, halo.shape[1], LANES), BF16)],
         ),
-        out_shape=[jax.ShapeDtypeStruct((rows // fast, blocks * block), BF16)] * fast,
+        out_shape=jax.ShapeDtypeStruct((rows, blocks * block), BF16),
         compiler_params=params(),
         cost_estimate=cost(
             2 * count * rows * (rows + halo.shape[1]) * blocks * block,
             2 * count * rows * blocks * block + rows * rows,
         ),
         name="partial_increment",
-    )(jnp.stack([first, place]), mix, mix_halo, memb, halo, spread_x, block_x, *fields, *after)
-
-
-def join_kernel(slow, fast, layer_ref, *refs):
-    own, other, outs = refs[:fast], refs[fast : 2 * fast], refs[-slow:]
-    height = own[0].shape[0] // slow
-    for d in range(slow):
-        z = lax.rem(layer_ref[0] + d, slow)
-        rows = pl.ds(pl.multiple_of(z * height, height), height)
-        for k in range(fast):
-            total = own[k][rows, :].astype(F32) + other[k][rows, :].astype(F32)
-            outs[d][k * height : (k + 1) * height, :] = total.astype(BF16)
-
-
-def join(layer, slow, fast, own, other, after):
-    rows, columns = own[0].shape
-    block = pick_block(columns, 384, 256, 128)
-    pick = lambda j, layer: (0, j)
-    height = rows // slow
-    return pl.pallas_call(
-        functools.partial(join_kernel, slow, fast),
-        grid_spec=pltpu.PrefetchScalarGridSpec(
-            num_scalar_prefetch=1,
-            grid=(columns // block,),
-            in_specs=[pl.BlockSpec((rows, block), pick)] * (2 * fast)
-            + [pl.BlockSpec(memory_space=pl.ANY)],
-            out_specs=[pl.BlockSpec((fast * height, block), pick)] * slow,
-        ),
-        out_shape=[jax.ShapeDtypeStruct((fast * height, columns), BF16)] * slow,
-        compiler_params=params(),
-        cost_estimate=cost(fast * rows * columns, 3 * fast * rows * columns),
+    )(first[None], mix, mix_halo, memb, halo, spread_x, block_x, *fields, after)
+
+
+def join_kernel(own_ref, other_ref, after_ref, out_ref):
+    out_ref[...] = (own_ref[...].astype(F32) + other_ref[...].astype(F32)).astype(BF16)
+
+
+def join(own, other, after):
+    rows, columns = own.shape
+    height = pick_block(rows, 384, 256, 128)
+    block = pl.BlockSpec((height, columns), lambda i: (i, 0))
+    return pl.pallas_call(
+        join_kernel,
+        grid=(rows // height,),
+        in_specs=[block, block, pl.BlockSpec(memory_space=pl.ANY)],
+        out_specs=block,
+        out_shape=jax.ShapeDtypeStruct(own.shape, BF16),
+        compiler_params=params(),
+        cost_estimate=cost(own.size, 3 * own.size),
         name="join",
-    )(layer[None], *own, *other, after)
+    )(own, other, after)
+
+
+def zero_kernel(*refs):
+    refs[-1][...] = jnp.zeros_like(refs[-1])
+
+
+def zero_after(*after):
+    return pl.pallas_call(
+        zero_kernel,
+        in_specs=[pl.BlockSpec(memory_space=pl.ANY)] * len(after),
+        out_shape=jax.ShapeDtypeStruct((1, 2), F32),
+        name="zero_after",
+    )(*after)
 
 
 def hold_kernel(*refs):
@@ -434,8 +412,7 @@
     )(array, *after)
 
 
-def adjoint_inside_kernel(mix_ref, memb_ref, grad_ref, after_ref, out_ref, token_ref):
-    token_ref[...] = jnp.zeros_like(token_ref)
+def adjoint_inside_kernel(mix_ref, memb_ref, grad_ref, after_ref, out_ref):
     out_ref[...] = dot(mix_ref[...], memb_ref[...] * grad_ref[...]).astype(BF16)
 
 
@@ -453,14 +430,8 @@
             pl.BlockSpec((rows, block), lambda j, m: (0, j)),
             pl.BlockSpec(memory_space=pl.ANY),
         ],
-        out_specs=[
-            pl.BlockSpec((None, rows, block), lambda j, m: (m, 0, j)),
-            pl.BlockSpec((1, 2), lambda j, m: (0, 0)),
-        ],
-        out_shape=[
-            jax.ShapeDtypeStruct((count, rows, half), BF16),
-            jax.ShapeDtypeStruct((1, 2), F32),
-        ],
+        out_specs=pl.BlockSpec((None, rows, block), lambda j, m: (m, 0, j)),
+        out_shape=jax.ShapeDtypeStruct((count, rows, half), BF16),
         compiler_params=params(),
         cost_estimate=cost(rows * memb.size, memb.size + rows * rows),
         name="adjoint_inside",
@@ -612,12 +583,13 @@
     field = control.reshape(flat)
     memb = members.reshape(flat)
     edge, control_sums = edge_sums(tile, step_y, levels, field)
-    spread_x, block_x = prepare_x(step_x, block)
-    along, mixes = [], []
+    along, mixes, factors_x = [], [], []
 
     def prepare(k, came):
+        if k == 0:
+            factors_x.extend(prepare_x(step_x, block, came))
         if k < count:
-            result, token = filter_x([k], field, (), spread_x, block_x, (came,))
+            result, token = filter_x([k], field, (), *factors_x, (came,))
             along.append(result)
             return token
         if k == count:
@@ -630,6 +602,7 @@
     for k in range(len(along) + len(mixes) // 2, count + 1):
         prepare(k, last)
     mix, mix_halo = mixes
+    spread_x, block_x = factors_x
 
     right = to_rows(hold(gradient[:, :, half:], last, mix))
 
@@ -638,42 +611,37 @@
     starts = [sum(sizes[:k]) for k in range(len(sizes))]
     share = functools.partial(
         partial_increment,
-        place=jnp.int32(0), slow=1, fast=1, mix=mix, mix_halo=mix_halo, fields=along, memb=memb,
-        halo=halo, spread_x=spread_x, block_x=block_x,
+        mix=mix, mix_halo=mix_halo, fields=along, memb=memb, halo=halo, spread_x=spread_x,
+        block_x=block_x,
     )
-    sent, kept = [], []
+    sent, now = [], halo
     for at, size in zip(starts, sizes):
-        sent += share((1 - side) * blocks + at, sent[-1:], blocks=size)
+        now = share((1 - side) * blocks + at, now, blocks=size)
+        sent.append(now)
     others = [lax.ppermute(x, "mem", SWAP) for x in sent]
-    left_sums = weighted_edge_sums(0, edge, memb, left, sent[-1])
-    now, mine, rest = left_sums, [], []
+    now = left_sums = weighted_edge_sums(0, edge, memb, left, now)
+    mine, rest = [], []
     for k, (at, size) in enumerate(zip(starts, sizes)):
-        (own,) = share(side * blocks + at, [now], blocks=size)
-        now = own
+        now = own = share(side * blocks + at, now, blocks=size)
         if k == 0:
             now = right_sums = weighted_edge_sums(1, edge, memb, right, now)
         if k == len(sizes) - 1:
-            left_inside, _ = adjoint_inside(0, mix, memb, left, now)
-            now = left_inside
-        (now,) = join(jnp.int32(0), 1, 1, [own], [others[k]], now)
+            now = left_inside = adjoint_inside(0, mix, memb, left, now)
+        now = join(own, others[k], now)
         mine.append(to_levels(now))
         rest.append(lax.ppermute(mine[-1], "mem", SWAP))
     increment = in_order(jnp.concatenate(mine, axis=2), jnp.concatenate(rest, axis=2), 2)
 
+    right_inside = adjoint_inside(1, mix, memb, right, now)
     hops = tiles.bit_length() - 1
-    right_inside = []
-
-    def work(k, came):
-        if k != hops - 2:
-            return None
-        result, token = adjoint_inside(1, mix, memb, right, now)
-        right_inside.append(result)
-        return token
+
+    def wait(k, came):
+        return zero_after(came, mine[0], right_inside) if k == hops - 3 else None
 
     weighted_sums = jnp.concatenate([left_sums, right_sums], axis=2)
-    weighted_halo, _ = outside(weighted_sums, tile, tiles, levels, factors, work)
+    weighted_halo, _ = outside(weighted_sums, tile, tiles, levels, factors, wait)
     control_grad = adjoint_outside(
-        left_inside, right_inside[0], mix_halo, weighted_halo, spread_x, block_x
+        left_inside, right_inside, mix_halo, weighted_halo, spread_x, block_x
     )
     return increment, control_grad.reshape(control.shape)
 

time: 158 us -> 156 us (0.987)
  starting transfers between devices: 39.9 us -> 42.2 us
  Pallas kernels: 80.1 us -> 78 us
  other arithmetic: 10.2 us -> 8.39 us
    another operation x4 -> x0, other arithmetic: 2.54 us -> none  [partial_increment(): jnp.stack([first, place])]
    pallas_call x7 -> x8, Pallas kernels: 29.2 us -> 27.2 us  [the longest x4 19.6 us: partial_increment(): pl.pallas_call(functools.partial(increment_kernel, block), grid_spec=pltp...]
    ppermute x2, starting transfers between devices: 1.12 us -> 3.05 us  [body(): rest.append(lax.ppermute(mine[-1], 'mem', SWAP))]
    all_to_all x2, waiting for transfers between devices: 11.3 us -> 9.49 us  [to_levels(): lax.all_to_all(part.reshape(levels, rows, -1), 'tile', 0, 0, tiled=True)]
    unnamed x46 -> x48, local copies, waits for them, and re-layouts: 3.43 us -> 3.51 us
  transfers between devices with their start and end apart: 18 -> 18, of which waited for: 5 -> 6; matrix products, arithmetic and copies ran while one was open for 7% -> 6% of each run, Pallas kernels for 48% -> 47%
where the time goes in v2:
time: 156 us; the launch traced here: 155 us
  Pallas kernels  78 us (50%)
  starting transfers between devices  42.2 us (27%)
  waiting for transfers between devices  18.3 us (12%)
  other arithmetic  8.39 us (5%)
  local copies, waits for them, and re-layouts  7.52 us (5%)
    pallas_call x4, Pallas kernels, partial_increment(): pl.pallas_call(functools.partial(increment_kernel, block), grid_spec=pltp...  19.6 us
    ppermute x10, starting transfers between devices, pair(): return lax.ppermute(x, 'tile', [(s, s ^ hop) for s in range(tiles)])  15 us
    pallas_call x2, Pallas kernels, adjoint_inside(): pl.pallas_call(adjoint_inside_kernel, grid=(steps, count), in_specs=[pl.B...  12.6 us
    pallas_call x2, Pallas kernels, filter_x(): pl.pallas_call(functools.partial(filter_x_kernel, block, len(weights)), g...  11.1 us
    all_to_all x2, starting transfers between devices, to_rows(): lax.all_to_all(part, 'tile', 0, 0, tiled=True).reshape(levels * rows, -1)  11 us
    all_to_all x2, starting transfers between devices, to_levels(): lax.all_to_all(part.reshape(levels, rows, -1), 'tile', 0, 0, tiled=True)  11 us
    pallas_call x1, Pallas kernels, adjoint_outside(): pl.pallas_call(functools.partial(adjoint_kernel, block), grid=(count, row...  9.94 us
    all_to_all x2, waiting for transfers between devices, to_levels(): lax.all_to_all(part.reshape(levels, rows, -1), 'tile', 0, 0, tiled=True)  9.49 us
  transfers between devices with their start and end apart: 18, of which 6 were waited for; matrix products, arithmetic and copies ran while one was open for 6% of the time, Pallas kernels for 47%

profile of v2, /device:TPU:0, one launch (start us, length us, event | category | flops | bytes accessed | tf_op | source)
XLA Modules:
  0.0 155.3 jit_solution(5744143617479970712)
XLA Ops:
  0.6 1.3 broadcast_in_dim.59.step_ref.step_y_ref
  1.9 4.8 %edge_sums.1 = (bf16[32,768]{1,0:T(8,128)(2,1)}, bf16[2,32,1536]{2,1,0:T(8,128)(2,1)}) custom-call(s32[1]{0:T(128)} %bitcast.1.tile_ref, f32[1,768]{1,0:T(1,128)} %broadcast_in_dim.59.step_ref.step_y_ref, bf16[2,768,1536]{2,1,0:T(8,128)(2,1)} %bitcast.65), custom_call_target="tpu_custom_call" | custom-call | flops 150994944 | bytes 4718592 | tf_op jit(solution)/shard_map/edge_sums/pallas_call | solution.py:214
  7.2 1.5 fusion.21
  8.8 7.2 %all-to-all-start = ((bf16[16,48,768]{2,1,0:T(8,128)(2,1)}), bf16[16,48,768]{2,1,0:T(8,128)(2,1)S(1)}, u32[]{:S(2)}, u32[]{:S(2)}) async-start(bf16[16,48,768]{2,1,0:T(8,128)(2,1)} %bitcast.22), calls=%async_computation | async-start | bytes 2359296 | tf_op jit(solution)/shard_map/all_to_all | solution.py:573
  17.8 2.0 %collective-permute-start.1 = (bf16[1,2,16,1536]{3,2,1,0:T(8,128)(2,1)S(1)}, bf16[1,2,16,1536]{3,2,1,0:T(8,128)(2,1)S(1)}, u32[]{:S(2)}, u32[]{:S(2)}) collective-permute-start(bf16[1,2,16,1536]{3,2,1,0:T(8,128)(2,1)S(1)} %add_convert_fusion.3), channel_id=1, source_target_pairs={{0,4},{2,6},{4,0},{6,2},{8,12},{10,14},{12,8},{14,10},{16,20},{18,... | collective-permute-start | bytes 294920 | tf_op jit(solution)/shard_map/ppermute | solution.py:513
  19.8 2.9 %prepare_x.1 = (bf16[1536,128]{1,0:T(8,128)(2,1)}, bf16[384,1536]{1,0:T(8,128)(2,1)}) custom-call(f32[1,1536]{1,0:T(1,128)} %broadcast_in_dim.66.step_ref, bf16[2,2,16,1536]{3,2,1,0:T(8,128)(2,1)} %copy-done.4), custom_call_target="tpu_custom_call" | custom-call | flops 47185920 | bytes 1572864 | tf_op jit(solution)/shard_map/prepare_x/pallas_call | solution.py:93
  22.7 5.5 %filter_x.2 = (bf16[1,768,1536]{2,1,0:T(8,128)(2,1)}, f32[1,2]{1,0:T(1,128)}) custom-call(bf16[2,768,1536]{2,1,0:T(8,128)(2,1)} %bitcast.66, bf16[1536,128]{1,0:T(8,128)(2,1)} %get-tuple-element.14.refs_0_.spread_ref, bf16[384,1536]{1,0:T(8,128)(2,1)} %get-tuple-element.15.refs_1_.block_ref, bf16[2,2,16,1536]{3,2,1,0:T(8,128)(2,1)} %copy-done.4), custom_call_target="tpu_custom_call" | custom-call | flops 1207959552 | bytes 4718592 | tf_op jit(solution)/shard_map/filter_x/pallas_call | solution.py:282
  28.2 0.7 bitcast_add_fusion.3
  29.0 1.5 collective-permute-start.2
  30.5 5.6 %filter_x.3 = (bf16[1,768,1536]{2,1,0:T(8,128)(2,1)}, f32[1,2]{1,0:T(1,128)}) custom-call(bf16[2,768,1536]{2,1,0:T(8,128)(2,1)} %bitcast.67, bf16[1536,128]{1,0:T(8,128)(2,1)} %get-tuple-element.14.refs_0_.spread_ref, bf16[384,1536]{1,0:T(8,128)(2,1)} %get-tuple-element.15.refs_1_.block_ref, bf16[1,2,16,1536]{3,2,1,0:T(8,128)(2,1)} %copy-done.11), custom_call_target="tpu_custom_call" | custom-call | flops 1207959552 | bytes 4718592 | tf_op jit(solution)/shard_map/filter_x/pallas_call | solution.py:282
  36.1 0.7 bitcast_add_fusion.1
  36.8 1.5 collective-permute-done.2.after_ref
  38.4 4.4 %collective-permute-start.3 = (bf16[1,16,1536]{2,1,0:T(8,128)(2,1)S(1)}, bf16[1,16,1536]{2,1,0:T(8,128)(2,1)S(1)}, u32[]{:S(2)}, u32[]{:S(2)}) collective-permute-start(bf16[1,16,1536]{2,1,0:T(8,128)(2,1)S(1)} %fusion.16), channel_id=1, source_target_pairs={{0,16},{2,18},{4,20},{6,22},{8,24},{10,26},{12,28},{14,30},{16,0},... | collective-permute-start | bytes 147464 | tf_op jit(solution)/shard_map/ppermute | solution.py:513
  42.9 4.2 %prepare_y.1 = (bf16[768,768]{1,0:T(8,128)(2,1)}, bf16[768,32]{1,0:T(8,128)(2,1)}, f32[1,2]{1,0:T(1,128)}) custom-call(s32[1]{0:T(128)} %bitcast.1.tile_ref, f32[1,768]{1,0:T(1,128)} %broadcast_in_dim.59.step_ref.step_y_ref, f32[1,16]{1,0:T(1,128)} %bitcast.90, bf16[1,2,16,1536]{3,2,1,0:T(8,128)(2,1)} %copy-done.9), custom_call_target="tpu_custom_call" | custom-call | flops 11796480 | bytes 1179648 | tf_op jit(solution)/shard_map/prepare_y/pallas_call | solution.py:159
  47.1 0.7 bitcast_add_fusion.2
  48.4 3.8 %all-to-all-start.1 = ((bf16[16,48,768]{2,1,0:T(8,128)(2,1)}), bf16[16,48,768]{2,1,0:T(8,128)(2,1)S(1)}, u32[]{:S(2)}, u32[]{:S(2)}) async-start(bf16[16,48,768]{2,1,0:T(8,128)(2,1)} %bitcast.72), calls=%async_computation.1 | async-start | bytes 2359296 | tf_op jit(solution)/shard_map/all_to_all | solution.py:573
  52.9 0.9 collective-permute-done.4
  53.8 0.8 add_convert_fusion.1
  54.6 5.6 %partial_increment.4.refs_2_ = bf16[768,512]{1,0:T(8,128)(2,1)} custom-call(s32[1]{0:T(128)} %bitcast.25.first_ref, bf16[768,768]{1,0:T(8,128)(2,1)} %get-tuple-element.17.mix_ref.refs_2_, bf16[768,32]{1,0:T(8,128)(2,1)} %get-tuple-element.18.mix_halo_ref, bf16[2,768,1536]{2,1,0:T(8,128)(2,1)} %bitcast.57, bf16[2,32,1536]{2,1,0:T(8,128)(2,1)} %bitcast.77, ...), custom_call_target="tpu_custom_call" | custom-call | flops 1258291200 | bytes 4325376 | tf_op jit(solution)/shard_map/partial_increment/pallas_call | solution.py:339
  60.2 1.5 collective-permute-start.5
  61.8 4.2 %partial_increment.5.after_ref = bf16[768,256]{1,0:T(8,128)(2,1)} custom-call(s32[1]{0:T(128)} %bitcast.24.first_ref, bf16[768,768]{1,0:T(8,128)(2,1)} %get-tuple-element.17.mix_ref.refs_2_, bf16[768,32]{1,0:T(8,128)(2,1)} %get-tuple-element.18.mix_halo_ref, bf16[2,768,1536]{2,1,0:T(8,128)(2,1)} %bitcast.58, bf16[2,32,1536]{2,1,0:T(8,128)(2,1)} %bitcast.79, ...), custom_call_target="tpu_custom_call" | custom-call | flops 629145600 | bytes 2752512 | tf_op jit(solution)/shard_map/partial_increment/pallas_call | solution.py:339
  66.5 4.0 %weighted_edge_sums.2.refs_2_ = bf16[2,32,768]{2,1,0:T(8,128)(2,1)} custom-call(bf16[32,768]{1,0:T(8,128)(2,1)} %get-tuple-element.23.edge_ref, bf16[2,768,1536]{2,1,0:T(8,128)(2,1)} %bitcast.59, bf16[768,768]{1,0:T(8,128)(2,1)} %bitcast.68, bf16[768,256]{1,0:T(8,128)(2,1)} %partial_increment.5.after_ref), custom_call_target="tpu_custom_call" | custom-call | flops 75497472 | bytes 4718592 | tf_op jit(solution)/shard_map/weighted_edge_sums/pallas_call | solution.py:247
  70.6 5.6 %partial_increment.6.after_ref.own_ref = bf16[768,512]{1,0:T(8,128)(2,1)} custom-call(s32[1]{0:T(128)} %bitcast.first_ref, bf16[768,768]{1,0:T(8,128)(2,1)} %get-tuple-element.17.mix_ref.refs_2_, bf16[768,32]{1,0:T(8,128)(2,1)} %get-tuple-element.18.mix_halo_ref, bf16[2,768,1536]{2,1,0:T(8,128)(2,1)} %bitcast.60, bf16[2,32,1536]{2,1,0:T(8,128)(2,1)} %bitcast.80, ...), custom_call_target="tpu_custom_call" | custom-call | flops 1258291200 | bytes 4325376 | tf_op jit(solution)/shard_map/partial_increment/pallas_call | solution.py:339
  76.2 1.2 all-to-all-done.1
  77.3 1.1 copy-done.1
  78.4 4.0 %weighted_edge_sums.3.after_ref = bf16[2,32,768]{2,1,0:T(8,128)(2,1)} custom-call(bf16[32,768]{1,0:T(8,128)(2,1)} %get-tuple-element.23.edge_ref, bf16[2,768,1536]{2,1,0:T(8,128)(2,1)} %bitcast.61, bf16[768,768]{1,0:T(8,128)(2,1)} %bitcast.70, bf16[768,512]{1,0:T(8,128)(2,1)} %partial_increment.6.after_ref.own_ref), custom_call_target="tpu_custom_call" | custom-call | flops 75497472 | bytes 4718592 | tf_op jit(solution)/shard_map/weighted_edge_sums/pallas_call | solution.py:247
  82.4 0.9 copy-done.14
  83.3 2.2 %join.2.refs_2_ = bf16[768,512]{1,0:T(8,128)(2,1)} custom-call(bf16[768,512]{1,0:T(8,128)(2,1)} %partial_increment.6.after_ref.own_ref, bf16[768,512]{1,0:T(8,128)(2,1)} %copy-done.14, bf16[2,32,768]{2,1,0:T(8,128)(2,1)} %weighted_edge_sums.3.after_ref), custom_call_target="tpu_custom_call" | custom-call | flops 393216 | bytes 2359296 | tf_op jit(solution)/shard_map/join/pallas_call | solution.py:375
  85.5 7.5 %all-to-all-start.2 = ((bf16[16,48,512]{2,1,0:T(8,128)(2,1)}), bf16[16,48,512]{2,1,0:T(8,128)(2,1)S(1)}, u32[]{:S(2)}, u32[]{:S(2)}) async-start(bf16[16,48,512]{2,1,0:T(8,128)(2,1)} %bitcast.76), calls=%async_computation.2 | async-start | bytes 1572864 | tf_op jit(solution)/shard_map/all_to_all | solution.py:576
  93.5 4.2 %partial_increment.7.after_ref.own_ref = bf16[768,256]{1,0:T(8,128)(2,1)} custom-call(s32[1]{0:T(128)} %bitcast.30.first_ref, bf16[768,768]{1,0:T(8,128)(2,1)} %get-tuple-element.17.mix_ref.refs_2_, bf16[768,32]{1,0:T(8,128)(2,1)} %get-tuple-element.18.mix_halo_ref, bf16[2,768,1536]{2,1,0:T(8,128)(2,1)} %bitcast.62, bf16[2,32,1536]{2,1,0:T(8,128)(2,1)} %bitcast.81, ...), custom_call_target="tpu_custom_call" | custom-call | flops 629145600 | bytes 2752512 | tf_op jit(solution)/shard_map/partial_increment/pallas_call | solution.py:339
  97.7 6.3 %adjoint_inside.2.after_ref.left_ref = bf16[2,768,768]{2,1,0:T(8,128)(2,1)} custom-call(bf16[768,768]{1,0:T(8,128)(2,1)} %get-tuple-element.17.mix_ref.refs_2_, bf16[2,768,1536]{2,1,0:T(8,128)(2,1)} %bitcast.63, bf16[768,768]{1,0:T(8,128)(2,1)} %bitcast.69, bf16[768,256]{1,0:T(8,128)(2,1)} %partial_increment.7.after_ref.own_ref), custom_call_target="tpu_custom_call" | custom-call | flops 1811939328 | bytes 5898240 | tf_op jit(solution)/shard_map/adjoint_inside/pallas_call | solution.py:424
  104.0 2.0 %join.3.after_ref = bf16[768,256]{1,0:T(8,128)(2,1)} custom-call(bf16[768,256]{1,0:T(8,128)(2,1)} %partial_increment.7.after_ref.own_ref, bf16[768,256]{1,0:T(8,128)(2,1)} %collective-permute-done.6.other_ref, bf16[2,768,768]{2,1,0:T(8,128)(2,1)} %adjoint_inside.2.after_ref.left_ref), custom_call_target="tpu_custom_call" | custom-call | flops 196608 | bytes 1179648 | tf_op jit(solution)/shard_map/join/pallas_call | solution.py:375
  106.1 1.7 %collective-permute-start.10 = (bf16[1,2,16,1536]{3,2,1,0:T(8,128)(2,1)S(1)}, bf16[1,2,16,1536]{3,2,1,0:T(8,128)(2,1)S(1)}, u32[]{:S(2)}, u32[]{:S(2)}) collective-permute-start(bf16[1,2,16,1536]{3,2,1,0:T(8,128)(2,1)S(1)} %add_convert_fusion.2), channel_id=1, source_target_pairs={{0,4},{2,6},{4,0},{6,2},{8,12},{10,14},{12,8},{14,10},{16,20},{18,... | collective-permute-start | bytes 294920 | tf_op jit(solution)/shard_map/ppermute | solution.py:513
  107.8 6.3 %adjoint_inside.3.refs_2_.right_ref = bf16[2,768,768]{2,1,0:T(8,128)(2,1)} custom-call(bf16[768,768]{1,0:T(8,128)(2,1)} %get-tuple-element.17.mix_ref.refs_2_, bf16[2,768,1536]{2,1,0:T(8,128)(2,1)} %bitcast.64, bf16[768,768]{1,0:T(8,128)(2,1)} %bitcast.71, bf16[768,256]{1,0:T(8,128)(2,1)} %join.3.after_ref), custom_call_target="tpu_custom_call" | custom-call | flops 1811939328 | bytes 5898240 | tf_op jit(solution)/shard_map/adjoint_inside/pallas_call | solution.py:424
  114.3 1.5 collective-permute-start.11
  115.8 0.9 copy-done.2
  117.2 0.6 bitcast_add_fusion
  117.9 1.2 collective-permute-done.11
  119.2 2.4 %collective-permute-start.12 = (bf16[1,16,1536]{2,1,0:T(8,128)(2,1)S(1)}, bf16[1,16,1536]{2,1,0:T(8,128)(2,1)S(1)}, u32[]{:S(2)}, u32[]{:S(2)}) collective-permute-start(bf16[1,16,1536]{2,1,0:T(8,128)(2,1)S(1)} %fusion.15), channel_id=1, source_target_pairs={{0,16},{2,18},{4,20},{6,22},{8,24},{10,26},{12,28},{14,30},{16,0},... | collective-permute-start | bytes 147464 | tf_op jit(solution)/shard_map/ppermute | solution.py:513
  121.7 3.6 %all-to-all-start.3 = ((bf16[16,48,256]{2,1,0:T(8,128)(2,1)}), bf16[16,48,256]{2,1,0:T(8,128)(2,1)S(1)}, u32[]{:S(2)}, u32[]{:S(2)}) async-start(bf16[16,48,256]{2,1,0:T(8,128)(2,1)} %bitcast.31), calls=%async_computation.3 | async-start | bytes 786432 | tf_op jit(solution)/shard_map/all_to_all | solution.py:576
  125.2 1.6 %collective-permute-start.7 = (bf16[1,768,512]{2,1,0:T(8,128)(2,1)}, bf16[1,768,512]{2,1,0:T(8,128)(2,1)S(1)}, u32[]{:S(2)}, u32[]{:S(2)}) collective-permute-start(bf16[1,768,512]{2,1,0:T(8,128)(2,1)} %bitcast.74), channel_id=1, source_target_pairs={{0,1},{1,0},{2,3},{3,2},{4,5},{5,4},{6,7},{7,6},{8,9},{9,8},{10,11... | collective-permute-start | bytes 2359304 | tf_op jit(solution)/shard_map/ppermute | solution.py:632
  126.8 1.0 fusion.9
  127.9 9.5 %all-to-all-done.3 = bf16[16,48,256]{2,1,0:T(8,128)(2,1)S(1)} async-done(((bf16[16,48,256]{2,1,0:T(8,128)(2,1)}), bf16[16,48,256]{2,1,0:T(8,128)(2,1)S(1)}, u32[]{:S(2)}, u32[]{:S(2)}) %all-to-all-start.3) | async-done | bytes 393248 | tf_op jit(solution)/shard_map/all_to_all | solution.py:576
  137.4 1.5 collective-permute-start.8
  138.9 0.9 add_convert_fusion
  139.7 9.9 %adjoint_outside.1 = bf16[2,768,1536]{2,1,0:T(8,128)(2,1)} custom-call(bf16[2,768,768]{2,1,0:T(8,128)(2,1)} %adjoint_inside.2.after_ref.left_ref, bf16[2,768,768]{2,1,0:T(8,128)(2,1)} %adjoint_inside.3.refs_2_.right_ref, bf16[768,32]{1,0:T(8,128)(2,1)} %get-tuple-element.18.mix_halo_ref, bf16[2,32,1536]{2,1,0:T(8,128)(2,1)} %bitcast.85, ...), custom_call_target="tpu_custom_call" | custom-call | flops 2415919104 | bytes 9437184 | tf_op jit(solution)/shard_map/adjoint_outside/pallas_call | solution.py:459
  149.7 3.9 %collective-permute-done.8 = bf16[1,768,256]{2,1,0:T(8,128)(2,1)S(1)} collective-permute-done((bf16[1,768,256]{2,1,0:T(8,128)(2,1)S(1)}, bf16[1,768,256]{2,1,0:T(8,128)(2,1)S(1)}, u32[]{:S(2)}, u32[]{:S(2)}) %collective-permute-start.8) | collective-permute-done | bytes 393248 | tf_op jit(solution)/shard_map/ppermute | solution.py:632
  153.6 1.7 %maximum_select_fusion = bf16[1,768,1536]{2,1,0:T(8,128)(2,1)} fusion(bf16[1,768,256]{2,1,0:T(8,128)(2,1)S(1)} %collective-permute-done.8, bf16[1,768,512]{2,1,0:T(8,128)(2,1)S(1)} %collective-permute-done.7, bf16[1,768,256]{2,1,0:T(8,128)(2,1)S(1)} %bitcast.84, bf16[1,768,512]{2,1,0:T(8,128)(2,1)S(1)} %bitcast.75, pred[]{:T(512)S(6)} %eq.14), kind=kLoop, calls=%fused_computation | loop fusion | flops 20054016 | bytes 4718593 | tf_op jit(solution)/shard_map/jit(_where)/select_n | solution.py:565
  (88 shorter events, 5.7 us)
Async XLA Ops:
  1.9 5.3 %copy-start.6 = (bf16[1,768,1536]{2,1,0:T(8,128)(2,1)S(1)}, bf16[1,768,1536]{2,1,0:T(8,128)(2,1)}, u32[]{:S(2)}) copy-start(bf16[1,768,1536]{2,1,0:T(8,128)(2,1)} %param.11) | copy-start | bytes 7077892
  6.7 11.0 %collective-permute-start = (bf16[2,2,16,1536]{3,2,1,0:T(8,128)(2,1)}, bf16[2,2,16,1536]{3,2,1,0:T(8,128)(2,1)S(1)}, u32[]{:S(2)}, u32[]{:S(2)}) collective-permute-start(bf16[2,2,16,1536]{3,2,1,0:T(8,128)(2,1)} %bitcast.88), channel_id=1, source_target_pairs={{0,2},{2,0},{4,6},{6,4},{8,10},{10,8},{12,14},{14,12},{16,18},{18,... | collective-permute-start | bytes 589832 | tf_op jit(solution)/shard_map/ppermute | solution.py:513
  8.7 7.3 %copy-start.20 = (s32[4]{0:T(128)S(1)}, s32[4]{0:T(128)}, u32[]{:S(2)}) copy-start(s32[4]{0:T(128)} %constant.47.clone) | copy-start | bytes 52
  8.7 7.3 %copy-start.21 = (pred[4]{0:T(512)(128)(4,1)S(1)}, pred[4]{0:T(512)(128)(4,1)}, u32[]{:S(2)}) copy-start(pred[4]{0:T(512)(128)(4,1)} %constant.48.clone) | copy-start | bytes 16
  8.7 7.3 %copy-start.22 = (s32[4]{0:T(128)S(1)}, s32[4]{0:T(128)}, u32[]{:S(2)}) copy-start(s32[4]{0:T(128)} %constant.50) | copy-start | bytes 52
  8.7 7.5 %copy-start.23 = (s32[4]{0:T(128)S(1)}, s32[4]{0:T(128)}, u32[]{:S(2)}) copy-start(s32[4]{0:T(128)} %constant.51) | copy-start | bytes 52
  8.7 7.7 %copy-start.18 = (f32[768]{0:T(1024)S(1)}, f32[768]{0:T(1024)}, u32[]{:S(2)}) copy-start(f32[768]{0:T(1024)} %param.13) | copy-start | bytes 9220
  8.7 8.0 %copy-start.19 = (f32[1536]{0:T(1024)S(1)}, f32[1536]{0:T(1024)}, u32[]{:S(2)}) copy-start(f32[1536]{0:T(1024)} %param.12) | copy-start | bytes 18436
  8.7 9.0 %copy-start.17 = (bf16[2,32,1536]{2,1,0:T(8,128)(2,1)S(1)}, bf16[2,32,1536]{2,1,0:T(8,128)(2,1)}, u32[]{:S(2)}) copy-start(bf16[2,32,1536]{2,1,0:T(8,128)(2,1)} %get-tuple-element.13) | copy-start | bytes 589828
  8.8 39.6 %all-to-all-start = ((bf16[16,48,768]{2,1,0:T(8,128)(2,1)}), bf16[16,48,768]{2,1,0:T(8,128)(2,1)S(1)}, u32[]{:S(2)}, u32[]{:S(2)}) async-start(bf16[16,48,768]{2,1,0:T(8,128)(2,1)} %bitcast.22), calls=%async_computation | async-start | bytes 2359296 | tf_op jit(solution)/shard_map/all_to_all | solution.py:573
  17.7 2.1 %copy-start.4 = (bf16[2,2,16,1536]{3,2,1,0:T(8,128)(2,1)}, bf16[2,2,16,1536]{3,2,1,0:T(8,128)(2,1)S(1)}, u32[]{:S(2)}) copy-start(bf16[2,2,16,1536]{3,2,1,0:T(8,128)(2,1)S(1)} %collective-permute-done.after_ref.refs_2_) | copy-start | bytes 589828
  17.8 11.0 %collective-permute-start.1 = (bf16[1,2,16,1536]{3,2,1,0:T(8,128)(2,1)S(1)}, bf16[1,2,16,1536]{3,2,1,0:T(8,128)(2,1)S(1)}, u32[]{:S(2)}, u32[]{:S(2)}) collective-permute-start(bf16[1,2,16,1536]{3,2,1,0:T(8,128)(2,1)S(1)} %add_convert_fusion.3), channel_id=1, source_target_pairs={{0,4},{2,6},{4,0},{6,2},{8,12},{10,14},{12,8},{14,10},{16,20},{18,... | collective-permute-start | bytes 294920 | tf_op jit(solution)/shard_map/ppermute | solution.py:513
  28.9 1.6 %copy-start.11 = (bf16[1,2,16,1536]{3,2,1,0:T(8,128)(2,1)}, bf16[1,2,16,1536]{3,2,1,0:T(8,128)(2,1)S(1)}, u32[]{:S(2)}) copy-start(bf16[1,2,16,1536]{3,2,1,0:T(8,128)(2,1)S(1)} %collective-permute-done.1.refs_2_) | copy-start | bytes 294916
  29.0 9.3 %collective-permute-start.2 = (bf16[1,2,16,1536]{3,2,1,0:T(8,128)(2,1)S(1)}, bf16[1,2,16,1536]{3,2,1,0:T(8,128)(2,1)S(1)}, u32[]{:S(2)}, u32[]{:S(2)}) collective-permute-start(bf16[1,2,16,1536]{3,2,1,0:T(8,128)(2,1)S(1)} %fusion.1), channel_id=1, source_target_pairs={{0,8},{2,10},{4,12},{6,14},{8,0},{10,2},{12,4},{14,6},{16,24},{18,... | collective-permute-start | bytes 294920 | tf_op jit(solution)/shard_map/ppermute | solution.py:513
  38.3 4.6 %copy-start.9 = (bf16[1,2,16,1536]{3,2,1,0:T(8,128)(2,1)}, bf16[1,2,16,1536]{3,2,1,0:T(8,128)(2,1)S(1)}, u32[]{:S(2)}) copy-start(bf16[1,2,16,1536]{3,2,1,0:T(8,128)(2,1)S(1)} %collective-permute-done.2.after_ref) | copy-start | bytes 294916
  38.4 9.4 %collective-permute-start.3 = (bf16[1,16,1536]{2,1,0:T(8,128)(2,1)S(1)}, bf16[1,16,1536]{2,1,0:T(8,128)(2,1)S(1)}, u32[]{:S(2)}, u32[]{:S(2)}) collective-permute-start(bf16[1,16,1536]{2,1,0:T(8,128)(2,1)S(1)} %fusion.16), channel_id=1, source_target_pairs={{0,16},{2,18},{4,20},{6,22},{8,24},{10,26},{12,28},{14,30},{16,0},... | collective-permute-start | bytes 147464 | tf_op jit(solution)/shard_map/ppermute | solution.py:513
  47.8 0.6 copy-start.15
  48.4 3.9 %copy-start.10 = (bf16[1,2,16,1536]{3,2,1,0:T(8,128)(2,1)S(1)}, bf16[1,2,16,1536]{3,2,1,0:T(8,128)(2,1)}, u32[]{:S(2)}) copy-start(bf16[1,2,16,1536]{3,2,1,0:T(8,128)(2,1)} %copy-done.9) | copy-start | bytes 294916
  48.4 3.9 %copy-start.12 = (bf16[1,2,16,1536]{3,2,1,0:T(8,128)(2,1)S(1)}, bf16[1,2,16,1536]{3,2,1,0:T(8,128)(2,1)}, u32[]{:S(2)}) copy-start(bf16[1,2,16,1536]{3,2,1,0:T(8,128)(2,1)} %copy-done.11) | copy-start | bytes 294916
  48.4 5.4 %copy-start.5 = (bf16[2,2,16,1536]{3,2,1,0:T(8,128)(2,1)S(1)}, bf16[2,2,16,1536]{3,2,1,0:T(8,128)(2,1)}, u32[]{:S(2)}) copy-start(bf16[2,2,16,1536]{3,2,1,0:T(8,128)(2,1)} %copy-done.4) | copy-start | bytes 589828
  48.4 3.9 %copy-start.16 = (bf16[1,16,1536]{2,1,0:T(8,128)(2,1)S(1)}, bf16[1,16,1536]{2,1,0:T(8,128)(2,1)}, u32[]{:S(2)}) copy-start(bf16[1,16,1536]{2,1,0:T(8,128)(2,1)} %copy-done.15) | copy-start | bytes 147460
  48.4 11.8 %copy-start = (bf16[16,48,768]{2,1,0:T(8,128)(2,1)}, bf16[16,48,768]{2,1,0:T(8,128)(2,1)S(1)}, u32[]{:S(2)}) copy-start(bf16[16,48,768]{2,1,0:T(8,128)(2,1)S(1)} %all-to-all-done) | copy-start | bytes 3538948
  48.4 28.9 %all-to-all-start.1 = ((bf16[16,48,768]{2,1,0:T(8,128)(2,1)}), bf16[16,48,768]{2,1,0:T(8,128)(2,1)S(1)}, u32[]{:S(2)}, u32[]{:S(2)}) async-start(bf16[16,48,768]{2,1,0:T(8,128)(2,1)} %bitcast.72), calls=%async_computation.1 | async-start | bytes 2359296 | tf_op jit(solution)/shard_map/all_to_all | solution.py:573
  52.4 1.4 collective-permute-start.4
  60.2 22.2 %collective-permute-start.5 = (bf16[768,512]{1,0:T(8,128)(2,1)}, bf16[768,512]{1,0:T(8,128)(2,1)S(1)}, u32[]{:S(2)}, u32[]{:S(2)}) collective-permute-start(bf16[768,512]{1,0:T(8,128)(2,1)} %partial_increment.4.refs_2_), channel_id=1, source_target_pairs={{0,1},{1,0},{2,3},{3,2},{4,5},{5,4},{6,7},{7,6},{8,9},{9,8},{10,11... | collective-permute-start | bytes 2359304 | tf_op jit(solution)/shard_map/ppermute | solution.py:621
  66.0 38.0 %collective-permute-start.6 = (bf16[768,256]{1,0:T(8,128)(2,1)}, bf16[768,256]{1,0:T(8,128)(2,1)}, u32[]{:S(2)}, u32[]{:S(2)}) collective-permute-start(bf16[768,256]{1,0:T(8,128)(2,1)} %partial_increment.5.after_ref), channel_id=1, source_target_pairs={{0,1},{1,0},{2,3},{3,2},{4,5},{5,4},{6,7},{7,6},{8,9},{9,8},{10,11... | collective-permute-start | bytes 1179656 | tf_op jit(solution)/shard_map/ppermute | solution.py:621
  77.3 1.1 copy-start.1
  82.4 10.6 %copy-start.7 = (bf16[2,32,768]{2,1,0:T(8,128)(2,1)S(1)}, bf16[2,32,768]{2,1,0:T(8,128)(2,1)}, u32[]{:S(2)}) copy-start(bf16[2,32,768]{2,1,0:T(8,128)(2,1)} %weighted_edge_sums.2.refs_2_) | copy-start | bytes 294916
  82.4 10.6 %copy-start.13 = (bf16[2,32,768]{2,1,0:T(8,128)(2,1)S(1)}, bf16[2,32,768]{2,1,0:T(8,128)(2,1)}, u32[]{:S(2)}) copy-start(bf16[2,32,768]{2,1,0:T(8,128)(2,1)} %weighted_edge_sums.3.after_ref) | copy-start | bytes 294916
  82.4 0.9 copy-start.14
  85.5 30.3 %all-to-all-start.2 = ((bf16[16,48,512]{2,1,0:T(8,128)(2,1)}), bf16[16,48,512]{2,1,0:T(8,128)(2,1)S(1)}, u32[]{:S(2)}, u32[]{:S(2)}) async-start(bf16[16,48,512]{2,1,0:T(8,128)(2,1)} %bitcast.76), calls=%async_computation.2 | async-start | bytes 1572864 | tf_op jit(solution)/shard_map/all_to_all | solution.py:576
  93.0 12.9 %collective-permute-start.9 = (bf16[2,2,16,1536]{3,2,1,0:T(8,128)(2,1)S(1)}, bf16[2,2,16,1536]{3,2,1,0:T(8,128)(2,1)S(1)}, u32[]{:S(2)}, u32[]{:S(2)}) collective-permute-start(bf16[2,2,16,1536]{3,2,1,0:T(8,128)(2,1)S(1)} %bitcast.86), channel_id=1, source_target_pairs={{0,2},{2,0},{4,6},{6,4},{8,10},{10,8},{12,14},{14,12},{16,18},{18,... | collective-permute-start | bytes 589832 | tf_op jit(solution)/shard_map/ppermute | solution.py:513
  106.1 8.1 %collective-permute-start.10 = (bf16[1,2,16,1536]{3,2,1,0:T(8,128)(2,1)S(1)}, bf16[1,2,16,1536]{3,2,1,0:T(8,128)(2,1)S(1)}, u32[]{:S(2)}, u32[]{:S(2)}) collective-permute-start(bf16[1,2,16,1536]{3,2,1,0:T(8,128)(2,1)S(1)} %add_convert_fusion.2), channel_id=1, source_target_pairs={{0,4},{2,6},{4,0},{6,2},{8,12},{10,14},{12,8},{14,10},{16,20},{18,... | collective-permute-start | bytes 294920 | tf_op jit(solution)/shard_map/ppermute | solution.py:513
  114.2 1.7 %copy-start.8 = (bf16[1,2,16,1536]{3,2,1,0:T(8,128)(2,1)}, bf16[1,2,16,1536]{3,2,1,0:T(8,128)(2,1)S(1)}, u32[]{:S(2)}) copy-start(bf16[1,2,16,1536]{3,2,1,0:T(8,128)(2,1)S(1)} %collective-permute-done.10.refs_0_) | copy-start | bytes 294916
  114.3 4.8 %collective-permute-start.11 = (bf16[1,2,16,1536]{3,2,1,0:T(8,128)(2,1)S(1)}, bf16[1,2,16,1536]{3,2,1,0:T(8,128)(2,1)S(1)}, u32[]{:S(2)}, u32[]{:S(2)}) collective-permute-start(bf16[1,2,16,1536]{3,2,1,0:T(8,128)(2,1)S(1)} %fusion.11), channel_id=1, source_target_pairs={{0,8},{2,10},{4,12},{6,14},{8,0},{10,2},{12,4},{14,6},{16,24},{18,... | collective-permute-start | bytes 294920 | tf_op jit(solution)/shard_map/ppermute | solution.py:513
  115.8 0.9 copy-start.2
  119.2 7.6 %collective-permute-start.12 = (bf16[1,16,1536]{2,1,0:T(8,128)(2,1)S(1)}, bf16[1,16,1536]{2,1,0:T(8,128)(2,1)S(1)}, u32[]{:S(2)}, u32[]{:S(2)}) collective-permute-start(bf16[1,16,1536]{2,1,0:T(8,128)(2,1)S(1)} %fusion.15), channel_id=1, source_target_pairs={{0,16},{2,18},{4,20},{6,22},{8,24},{10,26},{12,28},{14,30},{16,0},... | collective-permute-start | bytes 147464 | tf_op jit(solution)/shard_map/ppermute | solution.py:513
  121.7 15.7 %all-to-all-start.3 = ((bf16[16,48,256]{2,1,0:T(8,128)(2,1)}), bf16[16,48,256]{2,1,0:T(8,128)(2,1)S(1)}, u32[]{:S(2)}, u32[]{:S(2)}) async-start(bf16[16,48,256]{2,1,0:T(8,128)(2,1)} %bitcast.31), calls=%async_computation.3 | async-start | bytes 786432 | tf_op jit(solution)/shard_map/all_to_all | solution.py:576
  125.2 28.4 %collective-permute-start.7 = (bf16[1,768,512]{2,1,0:T(8,128)(2,1)}, bf16[1,768,512]{2,1,0:T(8,128)(2,1)S(1)}, u32[]{:S(2)}, u32[]{:S(2)}) collective-permute-start(bf16[1,768,512]{2,1,0:T(8,128)(2,1)} %bitcast.74), channel_id=1, source_target_pairs={{0,1},{1,0},{2,3},{3,2},{4,5},{5,4},{6,7},{7,6},{8,9},{9,8},{10,11... | collective-permute-start | bytes 2359304 | tf_op jit(solution)/shard_map/ppermute | solution.py:632
  127.8 11.1 %collective-permute-start.13 = (bf16[1,2,16,1536]{3,2,1,0:T(8,128)(2,1)S(1)}, bf16[1,2,16,1536]{3,2,1,0:T(8,128)(2,1)S(1)}, u32[]{:S(2)}, u32[]{:S(2)}) collective-permute-start(bf16[1,2,16,1536]{3,2,1,0:T(8,128)(2,1)S(1)} %fusion.9), channel_id=1, source_target_pairs={{0,2},{2,0},{4,6},{6,4},{8,10},{10,8},{12,14},{14,12},{16,18},{18,... | collective-permute-start | bytes 294920 | tf_op jit(solution)/shard_map/ppermute | solution.py:513
  137.4 16.2 %collective-permute-start.8 = (bf16[1,768,256]{2,1,0:T(8,128)(2,1)S(1)}, bf16[1,768,256]{2,1,0:T(8,128)(2,1)S(1)}, u32[]{:S(2)}, u32[]{:S(2)}) collective-permute-start(bf16[1,768,256]{2,1,0:T(8,128)(2,1)S(1)} %bitcast.83), channel_id=1, source_target_pairs={{0,1},{1,0},{2,3},{3,2},{4,5},{5,4},{6,7},{7,6},{8,9},{9,8},{10,11... | collective-permute-start | bytes 1179656 | tf_op jit(solution)/shard_map/ppermute | solution.py:632
  139.7 13.9 %copy-start.3 = (bf16[16,48,512]{2,1,0:T(8,128)(2,1)S(1)}, bf16[16,48,512]{2,1,0:T(8,128)(2,1)}, u32[]{:S(2)}) copy-start(bf16[16,48,512]{2,1,0:T(8,128)(2,1)} %copy-done.2) | copy-start | bytes 2359300

commit v3 on v2

--- a/solution.py
+++ b/solution.py
@@ -242,7 +242,7 @@
 def weighted_edge_sums(which, edge, memb, grad, after):
     count, rows, columns = memb.shape
     half = columns // 2
-    block = pick_block(half, 384, 256, 128)
+    block = pick_block(half, 768, 256, 128)
     steps = half // block
     return pl.pallas_call(
         weigh_kernel,
@@ -419,7 +419,7 @@
 def adjoint_inside(which, mix, memb, grad, after):
     count, rows, columns = memb.shape
     half = columns // 2
-    block = pick_block(half, 384, 256, 128)
+    block = pick_block(half, 768, 256, 128)
     steps = half // block
     return pl.pallas_call(
         adjoint_inside_kernel,

time: 156 us -> 153 us (0.981)
  Pallas kernels: 78 us -> 73.6 us
    pallas_call x2, Pallas kernels: 12.6 us -> 10.4 us  [adjoint_inside(): pl.pallas_call(adjoint_inside_kernel, grid=(steps, count), in_specs=[pl.B...]
    pallas_call x2, Pallas kernels: 8.06 us -> 5.9 us  [weighted_edge_sums(): pl.pallas_call(weigh_kernel, grid=(steps, count), in_specs=[pl.BlockSpec(...]
  transfers between devices with their start and end apart: 18 -> 18, of which waited for: 6 -> 7; matrix products, arithmetic and copies ran while one was open for 6% -> 6% of each run, Pallas kernels for 47% -> 45%
where the time goes in v3:
time: 153 us; the launch traced here: 152 us
  Pallas kernels  73.6 us (48%)
  starting transfers between devices  41.9 us (27%)
  waiting for transfers between devices  19.6 us (13%)
  other arithmetic  8.38 us (5%)
  local copies, waits for them, and re-layouts  7.52 us (5%)
    pallas_call x4, Pallas kernels, partial_increment(): pl.pallas_call(functools.partial(increment_kernel, block), grid_spec=pltp...  19.6 us
    ppermute x10, starting transfers between devices, pair(): return lax.ppermute(x, 'tile', [(s, s ^ hop) for s in range(tiles)])  14.8 us
    pallas_call x2, Pallas kernels, filter_x(): pl.pallas_call(functools.partial(filter_x_kernel, block, len(weights)), g...  11.1 us
    all_to_all x2, starting transfers between devices, to_rows(): lax.all_to_all(part, 'tile', 0, 0, tiled=True).reshape(levels * rows, -1)  11 us
    all_to_all x2, starting transfers between devices, to_levels(): lax.all_to_all(part.reshape(levels, rows, -1), 'tile', 0, 0, tiled=True)  11 us
    pallas_call x2, Pallas kernels, adjoint_inside(): pl.pallas_call(adjoint_inside_kernel, grid=(steps, count), in_specs=[pl.B...  10.4 us
    pallas_call x1, Pallas kernels, adjoint_outside(): pl.pallas_call(functools.partial(adjoint_kernel, block), grid=(count, row...  9.95 us
    all_to_all x2, waiting for transfers between devices, to_levels(): lax.all_to_all(part.reshape(levels, rows, -1), 'tile', 0, 0, tiled=True)  9.49 us
  transfers between devices with their start and end apart: 18, of which 7 were waited for; matrix products, arithmetic and copies ran while one was open for 6% of the time, Pallas kernels for 45%

profile of v3, /device:TPU:0, one launch (start us, length us, event | category | flops | bytes accessed | tf_op | source)
XLA Modules:
  0.0 152.0 jit_solution(9351357810329886847)
XLA Ops:
  0.6 1.3 broadcast_in_dim.59.step_ref.step_y_ref
  1.9 4.8 %edge_sums.1 = (bf16[32,768]{1,0:T(8,128)(2,1)}, bf16[2,32,1536]{2,1,0:T(8,128)(2,1)}) custom-call(s32[1]{0:T(128)} %bitcast.1.tile_ref, f32[1,768]{1,0:T(1,128)} %broadcast_in_dim.59.step_ref.step_y_ref, bf16[2,768,1536]{2,1,0:T(8,128)(2,1)} %bitcast.65), custom_call_target="tpu_custom_call" | custom-call | flops 150994944 | bytes 4718592 | tf_op jit(solution)/shard_map/edge_sums/pallas_call | solution.py:214
  7.2 1.5 %fusion.21 = (bf16[1,768,768]{2,1,0:T(8,128)(2,1)}, bf16[1,768,768]{2,1,0:T(8,128)(2,1)}) fusion(bf16[1,768,1536]{2,1,0:T(8,128)(2,1)S(1)} %copy-done.6), kind=kLoop, calls=%fused_computation.75 | loop fusion | bytes 4718592 | tf_op jit(solution)/shard_map/slice | solution.py:607
  8.8 7.2 %all-to-all-start = ((bf16[16,48,768]{2,1,0:T(8,128)(2,1)}), bf16[16,48,768]{2,1,0:T(8,128)(2,1)S(1)}, u32[]{:S(2)}, u32[]{:S(2)}) async-start(bf16[16,48,768]{2,1,0:T(8,128)(2,1)} %bitcast.22), calls=%async_computation | async-start | bytes 2359296 | tf_op jit(solution)/shard_map/all_to_all | solution.py:573
  17.8 2.0 %collective-permute-start.1 = (bf16[1,2,16,1536]{3,2,1,0:T(8,128)(2,1)S(1)}, bf16[1,2,16,1536]{3,2,1,0:T(8,128)(2,1)S(1)}, u32[]{:S(2)}, u32[]{:S(2)}) collective-permute-start(bf16[1,2,16,1536]{3,2,1,0:T(8,128)(2,1)S(1)} %add_convert_fusion.3), channel_id=1, source_target_pairs={{0,4},{2,6},{4,0},{6,2},{8,12},{10,14},{12,8},{14,10},{16,20},{18,... | collective-permute-start | bytes 294920 | tf_op jit(solution)/shard_map/ppermute | solution.py:513
  19.8 2.9 %prepare_x.1 = (bf16[1536,128]{1,0:T(8,128)(2,1)}, bf16[384,1536]{1,0:T(8,128)(2,1)}) custom-call(f32[1,1536]{1,0:T(1,128)} %broadcast_in_dim.66.step_ref, bf16[2,2,16,1536]{3,2,1,0:T(8,128)(2,1)} %copy-done.4), custom_call_target="tpu_custom_call" | custom-call | flops 47185920 | bytes 1572864 | tf_op jit(solution)/shard_map/prepare_x/pallas_call | solution.py:93
  22.7 5.5 %filter_x.2 = (bf16[1,768,1536]{2,1,0:T(8,128)(2,1)}, f32[1,2]{1,0:T(1,128)}) custom-call(bf16[2,768,1536]{2,1,0:T(8,128)(2,1)} %bitcast.66, bf16[1536,128]{1,0:T(8,128)(2,1)} %get-tuple-element.14.refs_0_.spread_ref, bf16[384,1536]{1,0:T(8,128)(2,1)} %get-tuple-element.15.refs_1_.block_ref, bf16[2,2,16,1536]{3,2,1,0:T(8,128)(2,1)} %copy-done.4), custom_call_target="tpu_custom_call" | custom-call | flops 1207959552 | bytes 4718592 | tf_op jit(solution)/shard_map/filter_x/pallas_call | solution.py:282
  28.2 0.7 bitcast_add_fusion.3
  29.0 1.5 %collective-permute-start.2 = (bf16[1,2,16,1536]{3,2,1,0:T(8,128)(2,1)S(1)}, bf16[1,2,16,1536]{3,2,1,0:T(8,128)(2,1)S(1)}, u32[]{:S(2)}, u32[]{:S(2)}) collective-permute-start(bf16[1,2,16,1536]{3,2,1,0:T(8,128)(2,1)S(1)} %fusion.1), channel_id=1, source_target_pairs={{0,8},{2,10},{4,12},{6,14},{8,0},{10,2},{12,4},{14,6},{16,24},{18,... | collective-permute-start | bytes 294920 | tf_op jit(solution)/shard_map/ppermute | solution.py:513
  30.5 5.6 %filter_x.3 = (bf16[1,768,1536]{2,1,0:T(8,128)(2,1)}, f32[1,2]{1,0:T(1,128)}) custom-call(bf16[2,768,1536]{2,1,0:T(8,128)(2,1)} %bitcast.67, bf16[1536,128]{1,0:T(8,128)(2,1)} %get-tuple-element.14.refs_0_.spread_ref, bf16[384,1536]{1,0:T(8,128)(2,1)} %get-tuple-element.15.refs_1_.block_ref, bf16[1,2,16,1536]{3,2,1,0:T(8,128)(2,1)} %copy-done.11), custom_call_target="tpu_custom_call" | custom-call | flops 1207959552 | bytes 4718592 | tf_op jit(solution)/shard_map/filter_x/pallas_call | solution.py:282
  36.1 0.7 bitcast_add_fusion.1
  36.8 1.5 collective-permute-done.2.after_ref
  38.4 4.4 %collective-permute-start.3 = (bf16[1,16,1536]{2,1,0:T(8,128)(2,1)S(1)}, bf16[1,16,1536]{2,1,0:T(8,128)(2,1)S(1)}, u32[]{:S(2)}, u32[]{:S(2)}) collective-permute-start(bf16[1,16,1536]{2,1,0:T(8,128)(2,1)S(1)} %fusion.16), channel_id=1, source_target_pairs={{0,16},{2,18},{4,20},{6,22},{8,24},{10,26},{12,28},{14,30},{16,0},... | collective-permute-start | bytes 147464 | tf_op jit(solution)/shard_map/ppermute | solution.py:513
  42.9 4.2 %prepare_y.1 = (bf16[768,768]{1,0:T(8,128)(2,1)}, bf16[768,32]{1,0:T(8,128)(2,1)}, f32[1,2]{1,0:T(1,128)}) custom-call(s32[1]{0:T(128)} %bitcast.1.tile_ref, f32[1,768]{1,0:T(1,128)} %broadcast_in_dim.59.step_ref.step_y_ref, f32[1,16]{1,0:T(1,128)} %bitcast.90, bf16[1,2,16,1536]{3,2,1,0:T(8,128)(2,1)} %copy-done.9), custom_call_target="tpu_custom_call" | custom-call | flops 11796480 | bytes 1179648 | tf_op jit(solution)/shard_map/prepare_y/pallas_call | solution.py:159
  47.1 0.7 bitcast_add_fusion.2
  48.4 3.8 %all-to-all-start.1 = ((bf16[16,48,768]{2,1,0:T(8,128)(2,1)}), bf16[16,48,768]{2,1,0:T(8,128)(2,1)S(1)}, u32[]{:S(2)}, u32[]{:S(2)}) async-start(bf16[16,48,768]{2,1,0:T(8,128)(2,1)} %bitcast.72), calls=%async_computation.1 | async-start | bytes 2359296 | tf_op jit(solution)/shard_map/all_to_all | solution.py:573
  52.9 0.9 collective-permute-done.4
  53.8 0.8 add_convert_fusion.1
  54.6 5.6 %partial_increment.4.refs_2_ = bf16[768,512]{1,0:T(8,128)(2,1)} custom-call(s32[1]{0:T(128)} %bitcast.25.first_ref, bf16[768,768]{1,0:T(8,128)(2,1)} %get-tuple-element.17.mix_ref.refs_2_, bf16[768,32]{1,0:T(8,128)(2,1)} %get-tuple-element.18.mix_halo_ref, bf16[2,768,1536]{2,1,0:T(8,128)(2,1)} %bitcast.57, bf16[2,32,1536]{2,1,0:T(8,128)(2,1)} %bitcast.77, ...), custom_call_target="tpu_custom_call" | custom-call | flops 1258291200 | bytes 4325376 | tf_op jit(solution)/shard_map/partial_increment/pallas_call | solution.py:339
  60.2 1.5 %collective-permute-start.5 = (bf16[768,512]{1,0:T(8,128)(2,1)}, bf16[768,512]{1,0:T(8,128)(2,1)S(1)}, u32[]{:S(2)}, u32[]{:S(2)}) collective-permute-start(bf16[768,512]{1,0:T(8,128)(2,1)} %partial_increment.4.refs_2_), channel_id=1, source_target_pairs={{0,1},{1,0},{2,3},{3,2},{4,5},{5,4},{6,7},{7,6},{8,9},{9,8},{10,11... | collective-permute-start | bytes 2359304 | tf_op jit(solution)/shard_map/ppermute | solution.py:621
  61.8 4.2 %partial_increment.5.after_ref = bf16[768,256]{1,0:T(8,128)(2,1)} custom-call(s32[1]{0:T(128)} %bitcast.24.first_ref, bf16[768,768]{1,0:T(8,128)(2,1)} %get-tuple-element.17.mix_ref.refs_2_, bf16[768,32]{1,0:T(8,128)(2,1)} %get-tuple-element.18.mix_halo_ref, bf16[2,768,1536]{2,1,0:T(8,128)(2,1)} %bitcast.58, bf16[2,32,1536]{2,1,0:T(8,128)(2,1)} %bitcast.79, ...), custom_call_target="tpu_custom_call" | custom-call | flops 629145600 | bytes 2752512 | tf_op jit(solution)/shard_map/partial_increment/pallas_call | solution.py:339
  66.5 2.9 %weighted_edge_sums.2.refs_2_ = bf16[2,32,768]{2,1,0:T(8,128)(2,1)} custom-call(bf16[32,768]{1,0:T(8,128)(2,1)} %get-tuple-element.23.edge_ref, bf16[2,768,1536]{2,1,0:T(8,128)(2,1)} %bitcast.59, bf16[768,768]{1,0:T(8,128)(2,1)} %bitcast.68, bf16[768,256]{1,0:T(8,128)(2,1)} %partial_increment.5.after_ref), custom_call_target="tpu_custom_call" | custom-call | flops 75497472 | bytes 4718592 | tf_op jit(solution)/shard_map/weighted_edge_sums/pallas_call | solution.py:247
  69.5 5.6 %partial_increment.6.after_ref.own_ref = bf16[768,512]{1,0:T(8,128)(2,1)} custom-call(s32[1]{0:T(128)} %bitcast.first_ref, bf16[768,768]{1,0:T(8,128)(2,1)} %get-tuple-element.17.mix_ref.refs_2_, bf16[768,32]{1,0:T(8,128)(2,1)} %get-tuple-element.18.mix_halo_ref, bf16[2,768,1536]{2,1,0:T(8,128)(2,1)} %bitcast.60, bf16[2,32,1536]{2,1,0:T(8,128)(2,1)} %bitcast.80, ...), custom_call_target="tpu_custom_call" | custom-call | flops 1258291200 | bytes 4325376 | tf_op jit(solution)/shard_map/partial_increment/pallas_call | solution.py:339
  75.1 2.2 %all-to-all-done.1 = bf16[16,48,768]{2,1,0:T(8,128)(2,1)S(1)} async-done(((bf16[16,48,768]{2,1,0:T(8,128)(2,1)}), bf16[16,48,768]{2,1,0:T(8,128)(2,1)S(1)}, u32[]{:S(2)}, u32[]{:S(2)}) %all-to-all-start.1) | async-done | bytes 1179680 | tf_op jit(solution)/shard_map/all_to_all | solution.py:573
  77.3 1.1 copy-done.1
  78.4 3.0 %weighted_edge_sums.3.after_ref = bf16[2,32,768]{2,1,0:T(8,128)(2,1)} custom-call(bf16[32,768]{1,0:T(8,128)(2,1)} %get-tuple-element.23.edge_ref, bf16[2,768,1536]{2,1,0:T(8,128)(2,1)} %bitcast.61, bf16[768,768]{1,0:T(8,128)(2,1)} %bitcast.70, bf16[768,512]{1,0:T(8,128)(2,1)} %partial_increment.6.after_ref.own_ref), custom_call_target="tpu_custom_call" | custom-call | flops 75497472 | bytes 4718592 | tf_op jit(solution)/shard_map/weighted_edge_sums/pallas_call | solution.py:247
  81.4 0.9 copy-done.14
  82.2 2.2 %join.2.refs_2_ = bf16[768,512]{1,0:T(8,128)(2,1)} custom-call(bf16[768,512]{1,0:T(8,128)(2,1)} %partial_increment.6.after_ref.own_ref, bf16[768,512]{1,0:T(8,128)(2,1)} %copy-done.14, bf16[2,32,768]{2,1,0:T(8,128)(2,1)} %weighted_edge_sums.3.after_ref), custom_call_target="tpu_custom_call" | custom-call | flops 393216 | bytes 2359296 | tf_op jit(solution)/shard_map/join/pallas_call | solution.py:375
  84.4 7.5 %all-to-all-start.2 = ((bf16[16,48,512]{2,1,0:T(8,128)(2,1)}), bf16[16,48,512]{2,1,0:T(8,128)(2,1)S(1)}, u32[]{:S(2)}, u32[]{:S(2)}) async-start(bf16[16,48,512]{2,1,0:T(8,128)(2,1)} %bitcast.76), calls=%async_computation.2 | async-start | bytes 1572864 | tf_op jit(solution)/shard_map/all_to_all | solution.py:576
  92.4 4.2 %partial_increment.7.after_ref.own_ref = bf16[768,256]{1,0:T(8,128)(2,1)} custom-call(s32[1]{0:T(128)} %bitcast.30.first_ref, bf16[768,768]{1,0:T(8,128)(2,1)} %get-tuple-element.17.mix_ref.refs_2_, bf16[768,32]{1,0:T(8,128)(2,1)} %get-tuple-element.18.mix_halo_ref, bf16[2,768,1536]{2,1,0:T(8,128)(2,1)} %bitcast.62, bf16[2,32,1536]{2,1,0:T(8,128)(2,1)} %bitcast.81, ...), custom_call_target="tpu_custom_call" | custom-call | flops 629145600 | bytes 2752512 | tf_op jit(solution)/shard_map/partial_increment/pallas_call | solution.py:339
  96.6 5.2 %adjoint_inside.2.after_ref.left_ref = bf16[2,768,768]{2,1,0:T(8,128)(2,1)} custom-call(bf16[768,768]{1,0:T(8,128)(2,1)} %get-tuple-element.17.mix_ref.refs_2_, bf16[2,768,1536]{2,1,0:T(8,128)(2,1)} %bitcast.63, bf16[768,768]{1,0:T(8,128)(2,1)} %bitcast.69, bf16[768,256]{1,0:T(8,128)(2,1)} %partial_increment.7.after_ref.own_ref), custom_call_target="tpu_custom_call" | custom-call | flops 1811939328 | bytes 5898240 | tf_op jit(solution)/shard_map/adjoint_inside/pallas_call | solution.py:424
  101.8 2.0 %join.3.after_ref = bf16[768,256]{1,0:T(8,128)(2,1)} custom-call(bf16[768,256]{1,0:T(8,128)(2,1)} %partial_increment.7.after_ref.own_ref, bf16[768,256]{1,0:T(8,128)(2,1)} %collective-permute-done.6.other_ref, bf16[2,768,768]{2,1,0:T(8,128)(2,1)} %adjoint_inside.2.after_ref.left_ref), custom_call_target="tpu_custom_call" | custom-call | flops 196608 | bytes 1179648 | tf_op jit(solution)/shard_map/join/pallas_call | solution.py:375
  103.9 1.7 %collective-permute-start.10 = (bf16[1,2,16,1536]{3,2,1,0:T(8,128)(2,1)S(1)}, bf16[1,2,16,1536]{3,2,1,0:T(8,128)(2,1)S(1)}, u32[]{:S(2)}, u32[]{:S(2)}) collective-permute-start(bf16[1,2,16,1536]{3,2,1,0:T(8,128)(2,1)S(1)} %add_convert_fusion.2), channel_id=1, source_target_pairs={{0,4},{2,6},{4,0},{6,2},{8,12},{10,14},{12,8},{14,10},{16,20},{18,... | collective-permute-start | bytes 294920 | tf_op jit(solution)/shard_map/ppermute | solution.py:513
  105.6 5.2 %adjoint_inside.3.refs_2_.right_ref = bf16[2,768,768]{2,1,0:T(8,128)(2,1)} custom-call(bf16[768,768]{1,0:T(8,128)(2,1)} %get-tuple-element.17.mix_ref.refs_2_, bf16[2,768,1536]{2,1,0:T(8,128)(2,1)} %bitcast.64, bf16[768,768]{1,0:T(8,128)(2,1)} %bitcast.71, bf16[768,256]{1,0:T(8,128)(2,1)} %join.3.after_ref), custom_call_target="tpu_custom_call" | custom-call | flops 1811939328 | bytes 5898240 | tf_op jit(solution)/shard_map/adjoint_inside/pallas_call | solution.py:424
  111.1 1.4 collective-permute-start.11
  112.5 0.9 copy-done.2
  113.9 0.6 bitcast_add_fusion
  114.5 1.3 collective-permute-done.11
  115.9 2.4 %collective-permute-start.12 = (bf16[1,16,1536]{2,1,0:T(8,128)(2,1)S(1)}, bf16[1,16,1536]{2,1,0:T(8,128)(2,1)S(1)}, u32[]{:S(2)}, u32[]{:S(2)}) collective-permute-start(bf16[1,16,1536]{2,1,0:T(8,128)(2,1)S(1)} %fusion.15), channel_id=1, source_target_pairs={{0,16},{2,18},{4,20},{6,22},{8,24},{10,26},{12,28},{14,30},{16,0},... | collective-permute-start | bytes 147464 | tf_op jit(solution)/shard_map/ppermute | solution.py:513
  118.3 3.6 %all-to-all-start.3 = ((bf16[16,48,256]{2,1,0:T(8,128)(2,1)}), bf16[16,48,256]{2,1,0:T(8,128)(2,1)S(1)}, u32[]{:S(2)}, u32[]{:S(2)}) async-start(bf16[16,48,256]{2,1,0:T(8,128)(2,1)} %bitcast.31), calls=%async_computation.3 | async-start | bytes 786432 | tf_op jit(solution)/shard_map/all_to_all | solution.py:576
  121.9 1.5 %collective-permute-start.7 = (bf16[1,768,512]{2,1,0:T(8,128)(2,1)}, bf16[1,768,512]{2,1,0:T(8,128)(2,1)S(1)}, u32[]{:S(2)}, u32[]{:S(2)}) collective-permute-start(bf16[1,768,512]{2,1,0:T(8,128)(2,1)} %bitcast.74), channel_id=1, source_target_pairs={{0,1},{1,0},{2,3},{3,2},{4,5},{5,4},{6,7},{7,6},{8,9},{9,8},{10,11... | collective-permute-start | bytes 2359304 | tf_op jit(solution)/shard_map/ppermute | solution.py:632
  123.5 1.0 fusion.9
  124.6 9.5 %all-to-all-done.3 = bf16[16,48,256]{2,1,0:T(8,128)(2,1)S(1)} async-done(((bf16[16,48,256]{2,1,0:T(8,128)(2,1)}), bf16[16,48,256]{2,1,0:T(8,128)(2,1)S(1)}, u32[]{:S(2)}, u32[]{:S(2)}) %all-to-all-start.3) | async-done | bytes 393248 | tf_op jit(solution)/shard_map/all_to_all | solution.py:576
  134.1 1.5 collective-permute-start.8
  135.5 0.9 add_convert_fusion
  136.4 9.9 %adjoint_outside.1 = bf16[2,768,1536]{2,1,0:T(8,128)(2,1)} custom-call(bf16[2,768,768]{2,1,0:T(8,128)(2,1)} %adjoint_inside.2.after_ref.left_ref, bf16[2,768,768]{2,1,0:T(8,128)(2,1)} %adjoint_inside.3.refs_2_.right_ref, bf16[768,32]{1,0:T(8,128)(2,1)} %get-tuple-element.18.mix_halo_ref, bf16[2,32,1536]{2,1,0:T(8,128)(2,1)} %bitcast.85, ...), custom_call_target="tpu_custom_call" | custom-call | flops 2415919104 | bytes 9437184 | tf_op jit(solution)/shard_map/adjoint_outside/pallas_call | solution.py:459
  146.3 3.9 %collective-permute-done.8 = bf16[1,768,256]{2,1,0:T(8,128)(2,1)S(1)} collective-permute-done((bf16[1,768,256]{2,1,0:T(8,128)(2,1)S(1)}, bf16[1,768,256]{2,1,0:T(8,128)(2,1)S(1)}, u32[]{:S(2)}, u32[]{:S(2)}) %collective-permute-start.8) | collective-permute-done | bytes 393248 | tf_op jit(solution)/shard_map/ppermute | solution.py:632
  150.3 1.7 %maximum_select_fusion = bf16[1,768,1536]{2,1,0:T(8,128)(2,1)} fusion(bf16[1,768,256]{2,1,0:T(8,128)(2,1)S(1)} %collective-permute-done.8, bf16[1,768,512]{2,1,0:T(8,128)(2,1)S(1)} %collective-permute-done.7, bf16[1,768,256]{2,1,0:T(8,128)(2,1)S(1)} %bitcast.84, bf16[1,768,512]{2,1,0:T(8,128)(2,1)S(1)} %bitcast.75, pred[]{:T(512)S(6)} %eq.14), kind=kLoop, calls=%fused_computation | loop fusion | flops 20054016 | bytes 4718593 | tf_op jit(solution)/shard_map/jit(_where)/select_n | solution.py:565
  (88 shorter events, 5.9 us)
Async XLA Ops:
  1.9 5.3 %copy-start.6 = (bf16[1,768,1536]{2,1,0:T(8,128)(2,1)S(1)}, bf16[1,768,1536]{2,1,0:T(8,128)(2,1)}, u32[]{:S(2)}) copy-start(bf16[1,768,1536]{2,1,0:T(8,128)(2,1)} %param.11) | copy-start | bytes 7077892
  6.7 11.0 %collective-permute-start = (bf16[2,2,16,1536]{3,2,1,0:T(8,128)(2,1)}, bf16[2,2,16,1536]{3,2,1,0:T(8,128)(2,1)S(1)}, u32[]{:S(2)}, u32[]{:S(2)}) collective-permute-start(bf16[2,2,16,1536]{3,2,1,0:T(8,128)(2,1)} %bitcast.88), channel_id=1, source_target_pairs={{0,2},{2,0},{4,6},{6,4},{8,10},{10,8},{12,14},{14,12},{16,18},{18,... | collective-permute-start | bytes 589832 | tf_op jit(solution)/shard_map/ppermute | solution.py:513
  8.7 7.3 %copy-start.20 = (s32[4]{0:T(128)S(1)}, s32[4]{0:T(128)}, u32[]{:S(2)}) copy-start(s32[4]{0:T(128)} %constant.47.clone) | copy-start | bytes 52
  8.7 7.3 %copy-start.21 = (pred[4]{0:T(512)(128)(4,1)S(1)}, pred[4]{0:T(512)(128)(4,1)}, u32[]{:S(2)}) copy-start(pred[4]{0:T(512)(128)(4,1)} %constant.48.clone) | copy-start | bytes 16
  8.7 7.3 %copy-start.22 = (s32[4]{0:T(128)S(1)}, s32[4]{0:T(128)}, u32[]{:S(2)}) copy-start(s32[4]{0:T(128)} %constant.50) | copy-start | bytes 52
  8.7 7.5 %copy-start.23 = (s32[4]{0:T(128)S(1)}, s32[4]{0:T(128)}, u32[]{:S(2)}) copy-start(s32[4]{0:T(128)} %constant.51) | copy-start | bytes 52
  8.7 7.7 %copy-start.18 = (f32[768]{0:T(1024)S(1)}, f32[768]{0:T(1024)}, u32[]{:S(2)}) copy-start(f32[768]{0:T(1024)} %param.13) | copy-start | bytes 9220
  8.7 8.0 %copy-start.19 = (f32[1536]{0:T(1024)S(1)}, f32[1536]{0:T(1024)}, u32[]{:S(2)}) copy-start(f32[1536]{0:T(1024)} %param.12) | copy-start | bytes 18436
  8.7 9.0 %copy-start.17 = (bf16[2,32,1536]{2,1,0:T(8,128)(2,1)S(1)}, bf16[2,32,1536]{2,1,0:T(8,128)(2,1)}, u32[]{:S(2)}) copy-start(bf16[2,32,1536]{2,1,0:T(8,128)(2,1)} %get-tuple-element.13) | copy-start | bytes 589828
  8.8 39.6 %all-to-all-start = ((bf16[16,48,768]{2,1,0:T(8,128)(2,1)}), bf16[16,48,768]{2,1,0:T(8,128)(2,1)S(1)}, u32[]{:S(2)}, u32[]{:S(2)}) async-start(bf16[16,48,768]{2,1,0:T(8,128)(2,1)} %bitcast.22), calls=%async_computation | async-start | bytes 2359296 | tf_op jit(solution)/shard_map/all_to_all | solution.py:573
  17.7 2.1 %copy-start.4 = (bf16[2,2,16,1536]{3,2,1,0:T(8,128)(2,1)}, bf16[2,2,16,1536]{3,2,1,0:T(8,128)(2,1)S(1)}, u32[]{:S(2)}) copy-start(bf16[2,2,16,1536]{3,2,1,0:T(8,128)(2,1)S(1)} %collective-permute-done.after_ref.refs_2_) | copy-start | bytes 589828
  17.8 11.0 %collective-permute-start.1 = (bf16[1,2,16,1536]{3,2,1,0:T(8,128)(2,1)S(1)}, bf16[1,2,16,1536]{3,2,1,0:T(8,128)(2,1)S(1)}, u32[]{:S(2)}, u32[]{:S(2)}) collective-permute-start(bf16[1,2,16,1536]{3,2,1,0:T(8,128)(2,1)S(1)} %add_convert_fusion.3), channel_id=1, source_target_pairs={{0,4},{2,6},{4,0},{6,2},{8,12},{10,14},{12,8},{14,10},{16,20},{18,... | collective-permute-start | bytes 294920 | tf_op jit(solution)/shard_map/ppermute | solution.py:513
  28.9 1.6 %copy-start.11 = (bf16[1,2,16,1536]{3,2,1,0:T(8,128)(2,1)}, bf16[1,2,16,1536]{3,2,1,0:T(8,128)(2,1)S(1)}, u32[]{:S(2)}) copy-start(bf16[1,2,16,1536]{3,2,1,0:T(8,128)(2,1)S(1)} %collective-permute-done.1.refs_2_) | copy-start | bytes 294916
  29.0 9.3 %collective-permute-start.2 = (bf16[1,2,16,1536]{3,2,1,0:T(8,128)(2,1)S(1)}, bf16[1,2,16,1536]{3,2,1,0:T(8,128)(2,1)S(1)}, u32[]{:S(2)}, u32[]{:S(2)}) collective-permute-start(bf16[1,2,16,1536]{3,2,1,0:T(8,128)(2,1)S(1)} %fusion.1), channel_id=1, source_target_pairs={{0,8},{2,10},{4,12},{6,14},{8,0},{10,2},{12,4},{14,6},{16,24},{18,... | collective-permute-start | bytes 294920 | tf_op jit(solution)/shard_map/ppermute | solution.py:513
  38.3 4.6 %copy-start.9 = (bf16[1,2,16,1536]{3,2,1,0:T(8,128)(2,1)}, bf16[1,2,16,1536]{3,2,1,0:T(8,128)(2,1)S(1)}, u32[]{:S(2)}) copy-start(bf16[1,2,16,1536]{3,2,1,0:T(8,128)(2,1)S(1)} %collective-permute-done.2.after_ref) | copy-start | bytes 294916
  38.4 9.4 %collective-permute-start.3 = (bf16[1,16,1536]{2,1,0:T(8,128)(2,1)S(1)}, bf16[1,16,1536]{2,1,0:T(8,128)(2,1)S(1)}, u32[]{:S(2)}, u32[]{:S(2)}) collective-permute-start(bf16[1,16,1536]{2,1,0:T(8,128)(2,1)S(1)} %fusion.16), channel_id=1, source_target_pairs={{0,16},{2,18},{4,20},{6,22},{8,24},{10,26},{12,28},{14,30},{16,0},... | collective-permute-start | bytes 147464 | tf_op jit(solution)/shard_map/ppermute | solution.py:513
  47.8 0.6 copy-start.15
  48.4 3.9 %copy-start.10 = (bf16[1,2,16,1536]{3,2,1,0:T(8,128)(2,1)S(1)}, bf16[1,2,16,1536]{3,2,1,0:T(8,128)(2,1)}, u32[]{:S(2)}) copy-start(bf16[1,2,16,1536]{3,2,1,0:T(8,128)(2,1)} %copy-done.9) | copy-start | bytes 294916
  48.4 3.9 %copy-start.12 = (bf16[1,2,16,1536]{3,2,1,0:T(8,128)(2,1)S(1)}, bf16[1,2,16,1536]{3,2,1,0:T(8,128)(2,1)}, u32[]{:S(2)}) copy-start(bf16[1,2,16,1536]{3,2,1,0:T(8,128)(2,1)} %copy-done.11) | copy-start | bytes 294916
  48.4 5.4 %copy-start.5 = (bf16[2,2,16,1536]{3,2,1,0:T(8,128)(2,1)S(1)}, bf16[2,2,16,1536]{3,2,1,0:T(8,128)(2,1)}, u32[]{:S(2)}) copy-start(bf16[2,2,16,1536]{3,2,1,0:T(8,128)(2,1)} %copy-done.4) | copy-start | bytes 589828
  48.4 3.9 %copy-start.16 = (bf16[1,16,1536]{2,1,0:T(8,128)(2,1)S(1)}, bf16[1,16,1536]{2,1,0:T(8,128)(2,1)}, u32[]{:S(2)}) copy-start(bf16[1,16,1536]{2,1,0:T(8,128)(2,1)} %copy-done.15) | copy-start | bytes 147460
  48.4 11.8 %copy-start = (bf16[16,48,768]{2,1,0:T(8,128)(2,1)}, bf16[16,48,768]{2,1,0:T(8,128)(2,1)S(1)}, u32[]{:S(2)}) copy-start(bf16[16,48,768]{2,1,0:T(8,128)(2,1)S(1)} %all-to-all-done) | copy-start | bytes 3538948
  48.4 28.9 %all-to-all-start.1 = ((bf16[16,48,768]{2,1,0:T(8,128)(2,1)}), bf16[16,48,768]{2,1,0:T(8,128)(2,1)S(1)}, u32[]{:S(2)}, u32[]{:S(2)}) async-start(bf16[16,48,768]{2,1,0:T(8,128)(2,1)} %bitcast.72), calls=%async_computation.1 | async-start | bytes 2359296 | tf_op jit(solution)/shard_map/all_to_all | solution.py:573
  52.4 1.4 collective-permute-start.4
  60.2 21.2 %collective-permute-start.5 = (bf16[768,512]{1,0:T(8,128)(2,1)}, bf16[768,512]{1,0:T(8,128)(2,1)S(1)}, u32[]{:S(2)}, u32[]{:S(2)}) collective-permute-start(bf16[768,512]{1,0:T(8,128)(2,1)} %partial_increment.4.refs_2_), channel_id=1, source_target_pairs={{0,1},{1,0},{2,3},{3,2},{4,5},{5,4},{6,7},{7,6},{8,9},{9,8},{10,11... | collective-permute-start | bytes 2359304 | tf_op jit(solution)/shard_map/ppermute | solution.py:621
  66.0 35.8 %collective-permute-start.6 = (bf16[768,256]{1,0:T(8,128)(2,1)}, bf16[768,256]{1,0:T(8,128)(2,1)}, u32[]{:S(2)}, u32[]{:S(2)}) collective-permute-start(bf16[768,256]{1,0:T(8,128)(2,1)} %partial_increment.5.after_ref), channel_id=1, source_target_pairs={{0,1},{1,0},{2,3},{3,2},{4,5},{5,4},{6,7},{7,6},{8,9},{9,8},{10,11... | collective-permute-start | bytes 1179656 | tf_op jit(solution)/shard_map/ppermute | solution.py:621
  77.3 1.1 copy-start.1
  81.3 10.6 %copy-start.7 = (bf16[2,32,768]{2,1,0:T(8,128)(2,1)S(1)}, bf16[2,32,768]{2,1,0:T(8,128)(2,1)}, u32[]{:S(2)}) copy-start(bf16[2,32,768]{2,1,0:T(8,128)(2,1)} %weighted_edge_sums.2.refs_2_) | copy-start | bytes 294916
  81.4 10.6 %copy-start.13 = (bf16[2,32,768]{2,1,0:T(8,128)(2,1)S(1)}, bf16[2,32,768]{2,1,0:T(8,128)(2,1)}, u32[]{:S(2)}) copy-start(bf16[2,32,768]{2,1,0:T(8,128)(2,1)} %weighted_edge_sums.3.after_ref) | copy-start | bytes 294916
  81.4 0.9 copy-start.14
  84.4 28.0 %all-to-all-start.2 = ((bf16[16,48,512]{2,1,0:T(8,128)(2,1)}), bf16[16,48,512]{2,1,0:T(8,128)(2,1)S(1)}, u32[]{:S(2)}, u32[]{:S(2)}) async-start(bf16[16,48,512]{2,1,0:T(8,128)(2,1)} %bitcast.76), calls=%async_computation.2 | async-start | bytes 1572864 | tf_op jit(solution)/shard_map/all_to_all | solution.py:576
  92.0 11.8 %collective-permute-start.9 = (bf16[2,2,16,1536]{3,2,1,0:T(8,128)(2,1)S(1)}, bf16[2,2,16,1536]{3,2,1,0:T(8,128)(2,1)S(1)}, u32[]{:S(2)}, u32[]{:S(2)}) collective-permute-start(bf16[2,2,16,1536]{3,2,1,0:T(8,128)(2,1)S(1)} %bitcast.86), channel_id=1, source_target_pairs={{0,2},{2,0},{4,6},{6,4},{8,10},{10,8},{12,14},{14,12},{16,18},{18,... | collective-permute-start | bytes 589832 | tf_op jit(solution)/shard_map/ppermute | solution.py:513
  103.9 7.1 %collective-permute-start.10 = (bf16[1,2,16,1536]{3,2,1,0:T(8,128)(2,1)S(1)}, bf16[1,2,16,1536]{3,2,1,0:T(8,128)(2,1)S(1)}, u32[]{:S(2)}, u32[]{:S(2)}) collective-permute-start(bf16[1,2,16,1536]{3,2,1,0:T(8,128)(2,1)S(1)} %add_convert_fusion.2), channel_id=1, source_target_pairs={{0,4},{2,6},{4,0},{6,2},{8,12},{10,14},{12,8},{14,10},{16,20},{18,... | collective-permute-start | bytes 294920 | tf_op jit(solution)/shard_map/ppermute | solution.py:513
  111.0 1.5 copy-start.8
  111.1 4.7 %collective-permute-start.11 = (bf16[1,2,16,1536]{3,2,1,0:T(8,128)(2,1)S(1)}, bf16[1,2,16,1536]{3,2,1,0:T(8,128)(2,1)S(1)}, u32[]{:S(2)}, u32[]{:S(2)}) collective-permute-start(bf16[1,2,16,1536]{3,2,1,0:T(8,128)(2,1)S(1)} %fusion.11), channel_id=1, source_target_pairs={{0,8},{2,10},{4,12},{6,14},{8,0},{10,2},{12,4},{14,6},{16,24},{18,... | collective-permute-start | bytes 294920 | tf_op jit(solution)/shard_map/ppermute | solution.py:513
  112.5 0.9 copy-start.2
  115.9 7.5 %collective-permute-start.12 = (bf16[1,16,1536]{2,1,0:T(8,128)(2,1)S(1)}, bf16[1,16,1536]{2,1,0:T(8,128)(2,1)S(1)}, u32[]{:S(2)}, u32[]{:S(2)}) collective-permute-start(bf16[1,16,1536]{2,1,0:T(8,128)(2,1)S(1)} %fusion.15), channel_id=1, source_target_pairs={{0,16},{2,18},{4,20},{6,22},{8,24},{10,26},{12,28},{14,30},{16,0},... | collective-permute-start | bytes 147464 | tf_op jit(solution)/shard_map/ppermute | solution.py:513
  118.3 15.7 %all-to-all-start.3 = ((bf16[16,48,256]{2,1,0:T(8,128)(2,1)}), bf16[16,48,256]{2,1,0:T(8,128)(2,1)S(1)}, u32[]{:S(2)}, u32[]{:S(2)}) async-start(bf16[16,48,256]{2,1,0:T(8,128)(2,1)} %bitcast.31), calls=%async_computation.3 | async-start | bytes 786432 | tf_op jit(solution)/shard_map/all_to_all | solution.py:576
  121.9 28.4 %collective-permute-start.7 = (bf16[1,768,512]{2,1,0:T(8,128)(2,1)}, bf16[1,768,512]{2,1,0:T(8,128)(2,1)S(1)}, u32[]{:S(2)}, u32[]{:S(2)}) collective-permute-start(bf16[1,768,512]{2,1,0:T(8,128)(2,1)} %bitcast.74), channel_id=1, source_target_pairs={{0,1},{1,0},{2,3},{3,2},{4,5},{5,4},{6,7},{7,6},{8,9},{9,8},{10,11... | collective-permute-start | bytes 2359304 | tf_op jit(solution)/shard_map/ppermute | solution.py:632
  124.5 11.1 %collective-permute-start.13 = (bf16[1,2,16,1536]{3,2,1,0:T(8,128)(2,1)S(1)}, bf16[1,2,16,1536]{3,2,1,0:T(8,128)(2,1)S(1)}, u32[]{:S(2)}, u32[]{:S(2)}) collective-permute-start(bf16[1,2,16,1536]{3,2,1,0:T(8,128)(2,1)S(1)} %fusion.9), channel_id=1, source_target_pairs={{0,2},{2,0},{4,6},{6,4},{8,10},{10,8},{12,14},{14,12},{16,18},{18,... | collective-permute-start | bytes 294920 | tf_op jit(solution)/shard_map/ppermute | solution.py:513
  134.1 16.2 %collective-permute-start.8 = (bf16[1,768,256]{2,1,0:T(8,128)(2,1)S(1)}, bf16[1,768,256]{2,1,0:T(8,128)(2,1)S(1)}, u32[]{:S(2)}, u32[]{:S(2)}) collective-permute-start(bf16[1,768,256]{2,1,0:T(8,128)(2,1)S(1)} %bitcast.83), channel_id=1, source_target_pairs={{0,1},{1,0},{2,3},{3,2},{4,5},{5,4},{6,7},{7,6},{8,9},{9,8},{10,11... | collective-permute-start | bytes 1179656 | tf_op jit(solution)/shard_map/ppermute | solution.py:632
  136.4 13.9 %copy-start.3 = (bf16[16,48,512]{2,1,0:T(8,128)(2,1)S(1)}, bf16[16,48,512]{2,1,0:T(8,128)(2,1)}, u32[]{:S(2)}) copy-start(bf16[16,48,512]{2,1,0:T(8,128)(2,1)} %copy-done.2) | copy-start | bytes 2359300
